TPU v7x, 32 devices: a whole 2x2x4 slice. The times are simulated.
32 devices in a mesh: parts: 2 (over x), node: 2 (over core), local: 8 (over z, y).
Axes of the slice: x: 2, y: 2, z: 4, core: 2. Of those that a mesh axis runs over, the one named last changes fastest.
Arguments:
- tokens: bfloat16 [4096, 3584], P(('parts', 'node', 'local')), parts along dimension 0, may hold values from -6 to 6
- expert_ids: int32 [4096, 4], P(('parts', 'node', 'local')), parts along dimension 0, may hold values from 0 to 7, all different within a row; in each aligned block of 128 rows (0 to 127, 128 to 255, ...) at most 80 rows name the same one
- combine_weights: bfloat16 [4096, 4], P(('parts', 'node', 'local')), parts along dimension 0, may hold values from 0.19921875 to 1
- gate_weight: bfloat16 [16, 3584, 512], P(('node', 'local')), may hold values from -0.09375 to 0.09375
- up_weight: bfloat16 [16, 3584, 512], P(('node', 'local')), may hold values from -0.09375 to 0.09375
- down_weight: bfloat16 [16, 512, 3584], P(('node', 'local')), may hold values from -0.1875 to 0.1875
Outputs:
- moe_out: bfloat16 [4096, 3584], P(('parts', 'node', 'local')), parts along dimension 0
There are 2 independent parts, one for each index of `parts`. A program takes and returns all parts, laid end to end along the dimension named above; an argument that names none is the same for every part. Nothing has to cross between parts.
Inputs may be any that keep to these rules, and one draw needn't show every extreme that they name: `expert_ids`: each row names 4 different experts. Among the 128 rows of one device, no expert is named by more than 80 rows, and this bound is reached.
All inputs are finite; a program needn't handle non-finite values.
Results may differ from a plain program's by a relative error of at most 0.0072.
Values may be sent and summed in bfloat16 or wider, within the bound.
No kernel may reach another device: no remote copies, remote signals or barrier semaphores. Data moves between devices by JAX's collectives and lax.ppermute only.
A program may use at most 128 MiB of HBM per device.

v0:
```python
import jax
import jax.numpy as jnp
from jax import lax
from jax.sharding import PartitionSpec as P


def slot_tables(routes, first_expert, expert_count, capacity, expert_total):
    options = jnp.arange(expert_total, dtype=jnp.int32)
    matches = routes[:, :, None] == options[None, None, :]
    counts = jnp.sum(matches.astype(jnp.int32), axis=1)
    before = jnp.cumsum(counts, axis=0) - counts
    rank_in = jnp.sum(jnp.where(matches, before[:, None, :], 0), axis=2)
    local_index = routes - first_expert
    inside = (local_index >= 0) & (local_index < expert_count)
    return (local_index * capacity + rank_in, inside)


def dispatch_matrix(slot_index, inside, total_slots):
    positions = jnp.arange(total_slots, dtype=jnp.int32)
    matches = (slot_index[None, :, :] == positions[:, None, None]) & inside[None, :, :]
    return jnp.sum(matches.astype(jnp.float32), axis=2).astype(jnp.bfloat16)


def weight_matrix(slot_index, inside, weights, total_slots):
    positions = jnp.arange(total_slots, dtype=jnp.int32)
    matches = (slot_index[:, :, None] == positions[None, None, :]) & inside[:, :, None]
    spread = jnp.where(matches, weights.astype(jnp.float32)[:, :, None], 0.0)
    return jnp.sum(spread, axis=1).astype(jnp.bfloat16)


def apply_expert(rows, gate_local, up_local, down_local):
    gate_value = jnp.dot(rows, gate_local, preferred_element_type=jnp.float32)
    up_value = jnp.dot(rows, up_local, preferred_element_type=jnp.float32)
    hidden = (jax.nn.silu(gate_value) * up_value).astype(jnp.bfloat16)
    return jnp.dot(hidden, down_local, preferred_element_type=jnp.float32).astype(jnp.bfloat16)


def on_device(tokens, expert_ids, combine_weights, gate_weight, up_weight, down_weight):
    node_count = lax.axis_size("node")
    local_count = lax.axis_size("local")
    per_node = local_count // 2
    expert_total = node_count * per_node
    token_count = tokens.shape[0]
    model_width = tokens.shape[1]
    top_count = expert_ids.shape[1]
    capacity = token_count * top_count * 5 // (4 * expert_total)
    gate_local = gate_weight[0]
    up_local = up_weight[0]
    down_local = down_weight[0]
    rows_all, weights_all = (
        lax.all_gather(tokens, "node", axis=0, tiled=True),
        lax.all_gather(combine_weights, "node", axis=0, tiled=True),
    )
    routes_all = lax.all_gather(expert_ids, "node", axis=0, tiled=True)
    first_expert = lax.axis_index("node") * per_node
    total_slots = per_node * capacity
    routes_blocks = routes_all.reshape(node_count, token_count, top_count)
    slot_index, inside = jax.vmap(
        lambda routes: slot_tables(routes, first_expert, per_node, capacity, expert_total)
    )(routes_blocks)
    placing = jax.vmap(lambda slots, marks: dispatch_matrix(slots, marks, total_slots))(
        slot_index, inside
    )
    row_blocks = rows_all.reshape(node_count, token_count, model_width)
    packed = jnp.einsum(
        "bst,btd->bsd", placing, row_blocks, preferred_element_type=jnp.float32
    ).astype(jnp.bfloat16)
    packed = packed.reshape(node_count, per_node, capacity, model_width).transpose(1, 0, 2, 3)
    outgoing = jnp.broadcast_to(packed[:, None], (per_node, 2, node_count, capacity, model_width))
    outgoing = outgoing.reshape(local_count, node_count * capacity, model_width)
    rows = lax.all_to_all(outgoing, "local", split_axis=0, concat_axis=0, tiled=True)
    in_shape = rows.shape
    flat_rows = rows.reshape(-1, model_width)
    returned = lax.all_to_all(
        apply_expert(flat_rows, gate_local, up_local, down_local).reshape(in_shape),
        "local",
        split_axis=0,
        concat_axis=0,
        tiled=True,
    )
    returned = returned.reshape(per_node, 2, node_count, capacity, model_width).astype(jnp.float32)
    results = (returned[:, 0] + returned[:, 1]).astype(jnp.bfloat16)
    by_block = results.transpose(1, 0, 2, 3).reshape(node_count, total_slots, model_width)
    weight_blocks = weights_all.reshape(node_count, token_count, top_count)
    mixing = jax.vmap(
        lambda slots, marks, weights: weight_matrix(slots, marks, weights, total_slots)
    )(slot_index, inside, weight_blocks)
    contrib = jnp.einsum(
        "bts,bsd->btd", mixing, by_block, preferred_element_type=jnp.float32
    ).astype(jnp.bfloat16)
    contrib = lax.optimization_barrier(contrib)
    summed_out = lax.psum_scatter(
        contrib.astype(jnp.float32).astype(jnp.bfloat16), "node", scatter_dimension=0, tiled=True
    ).astype(jnp.float32)
    return summed_out[0].astype(jnp.bfloat16)


def solution(mesh):
    in_specs = (
        P(("parts", "node", "local"), None),
        P(("parts", "node", "local"), None),
        P(("parts", "node", "local"), None),
        P(("node", "local"), None, None),
        P(("node", "local"), None, None),
        P(("node", "local"), None, None),
    )
    out_specs = P(("parts", "node", "local"), None)
    return jax.shard_map(
        on_device, mesh=mesh, in_specs=in_specs, out_specs=out_specs, check_vma=False
    )
```

profile of v0, /device:TPU:0, one launch (start us, length us, event | category | flops | bytes accessed | tf_op | source)
XLA Modules:
  0.0 512.3 jit_solution(13762043688094892559)
XLA Ops:
  6.5 0.7 all-gather.2.cloned.1.call-update
  7.3 2.1 all_gather.9
  9.3 0.1 copy.16
  9.5 0.2 reduce_window_sum.11
  9.7 0.1 copy.18
  9.8 0.3 convert_reduce_fusion
  10.1 11.8 %all-gather.2.cloned.1.call-done = bf16[256,3584]{1,0:T(8,128)(2,1)} async-done(((bf16[128,3584]{1,0:T(8,128)(2,1)}), bf16[256,3584]{1,0:T(8,128)(2,1)}) %all-gather.2.cloned.1.call-update) | async-done | bytes 1835024 | tf_op jit(solution)/shard_map/all_gather | solution.py:51
  21.8 2.8 convolution_convert_fusion.1
  24.7 2.5 copy.20
  27.1 6.7 %broadcast_in_dim.43 = bf16[4,2,2,80,3584]{4,3,2,1,0:T(8,128)(2,1)} broadcast(bf16[4,2,80,3584]{3,2,1,0:T(8,128)(2,1)} %copy.20), dimensions={0,2,3,4} | broadcast | bytes 13762560 | tf_op jit(solution)/shard_map/broadcast_in_dim | solution.py:69
  33.9 206.4 %all_to_all.10 = bf16[8,160,3584]{2,1,0:T(8,128)(2,1)S(1)} all-to-all(bf16[8,160,3584]{2,1,0:T(8,128)(2,1)} %bitcast.42), channel_id=1, replica_groups=mesh['parts'=2,'node'=2,'local'=8] {'local'}, dimensions={0} | all-to-all | bytes 18350080 | tf_op jit(solution)/shard_map/all_to_all | solution.py:71
  240.2 3.5 copy-done
  243.7 4.9 fusion.4
  248.7 16.6 %convolution_convert_fusion = bf16[1280,3584]{1,0:T(8,128)(2,1)} fusion(bf16[1,512,3584]{2,1,0:T(8,128)(2,1)} %param.11, bf16[1280,3584]{1,0:T(8,128)(2,1)} %bitcast.47, bf16[1,3584,512]{2,1,0:T(8,128)(2,1)} %param.10, f32[1280,512]{1,0:T(8,128)S(1)} %fusion.4), kind=kOutput, calls=%fused_computation | convolution fusion | flops 9403760640 | bytes 28311552 | tf_op jit(solution)/shard_map/dot_general | solution.py:35
  265.2 5.1 %all-to-all-start.1 = ((bf16[8,160,3584]{2,1,0:T(8,128)(2,1)}), bf16[8,160,3584]{2,1,0:T(8,128)(2,1)}, u32[]{:S(2)}, u32[]{:S(2)}) async-start(bf16[8,160,3584]{2,1,0:T(8,128)(2,1)} %bitcast.45), calls=%async_computation.1 | async-start | bytes 18350080 | tf_op jit(solution)/shard_map/all_to_all | solution.py:74
  270.4 0.0 reduce-scatter.2.cloned.1.call-start
  270.5 2.0 all_gather.10
  272.4 0.3 select_reduce_fusion
  272.8 197.2 %all-to-all-done.1 = bf16[8,160,3584]{2,1,0:T(8,128)(2,1)} async-done(((bf16[8,160,3584]{2,1,0:T(8,128)(2,1)}), bf16[8,160,3584]{2,1,0:T(8,128)(2,1)}, u32[]{:S(2)}, u32[]{:S(2)}) %all-to-all-start.1) | async-done | bytes 9175072 | tf_op jit(solution)/shard_map/all_to_all | solution.py:74
  469.9 12.6 %fusion.25 = (f32[4,1,2,80,3584]{4,3,2,1,0:T(8,128)}, f32[4,1,2,80,3584]{4,3,2,1,0:T(8,128)}) fusion(bf16[4,2,2,80,3584]{4,3,2,1,0:T(8,128)(2,1)} %bitcast.12), kind=kLoop, calls=%fused_computation.33 | loop fusion | bytes 36700160 | tf_op jit(solution)/shard_map/slice | solution.py:82
  482.5 9.6 %fusion = bf16[4,1,2,80,3584]{4,3,0,2,1:T(8,128)(2,1)} fusion(f32[4,1,2,80,3584]{4,3,2,1,0:T(8,128)} %get-tuple-element.6, f32[4,1,2,80,3584]{4,3,2,1,0:T(8,128)} %get-tuple-element.5), kind=kLoop, calls=%fused_computation.2 | loop fusion | flops 4587520 | bytes 22937600 | tf_op jit(solution)/shard_map/convert_element_type | solution.py:82
  492.1 4.7 convolution_convert_fusion.2
  496.9 0.0 reduce-scatter.2.cloned.1.call-update
  496.9 8.5 %reduce-scatter.2.cloned.1.call-done = bf16[1,128,3584]{2,1,0:T(8,128)(2,1)} async-done(((bf16[2,128,3584]{2,1,0:T(8,128)(2,1)}), bf16[1,128,3584]{2,1,0:T(8,128)(2,1)}) %reduce-scatter.2.cloned.1.call-update) | async-done | bytes 917520 | tf_op jit(solution)/shard_map/reduce_scatter | solution.py:92
  (12 shorter events, 0.1 us)
Async XLA Ops:
  6.5 15.3 %all-gather.2.cloned.1.call-start = ((), (), s32[]{:S(2)}) async-start(), calls=%async_computation.3 | async-start | bytes 2752512 | tf_op jit(solution)/shard_map/all_gather | solution.py:51
  33.9 209.9 %copy-start.2 = (bf16[1,3584,512]{2,1,0:T(8,128)(2,1)S(1)}, bf16[1,3584,512]{2,1,0:T(8,128)(2,1)}, u32[]{:S(2)}) copy-start(bf16[1,3584,512]{2,1,0:T(8,128)(2,1)} %param.9) | copy-start | bytes 11010052
  240.2 3.5 copy-start
  265.2 5.2 %copy-start.1 = (bf16[128,4]{0,1:T(4,128)(2,1)S(1)}, bf16[128,4]{0,1:T(4,128)(2,1)}, u32[]{:S(2)}) copy-start(bf16[128,4]{0,1:T(4,128)(2,1)} %param.8) | copy-start | bytes 3076
  265.2 204.7 %all-to-all-start.1 = ((bf16[8,160,3584]{2,1,0:T(8,128)(2,1)}), bf16[8,160,3584]{2,1,0:T(8,128)(2,1)}, u32[]{:S(2)}, u32[]{:S(2)}) async-start(bf16[8,160,3584]{2,1,0:T(8,128)(2,1)} %bitcast.45), calls=%async_computation.1 | async-start | bytes 18350080 | tf_op jit(solution)/shard_map/all_to_all | solution.py:74
  270.4 235.0 %reduce-scatter.2.cloned.1.call-start = ((), (), s32[]{:S(2)}) async-start(), calls=%async_computation.4 | async-start | bytes 2752512 | tf_op jit(solution)/shard_map/reduce_scatter | solution.py:92
Sparse Core Ops, SparseCore 0:
  8.9 12.8 all-gather.1
  497.0 8.3 reduce-scatter.1
where the time goes:
time: 513 us; the launch traced here: 512 us
  waiting for transfers between devices  218 us (42%)
  blocking collectives  210 us (41%)
  matrix products  29 us (6%)
  local copies, waits for them, and re-layouts  25.5 us (5%)
  between operations  13.5 us (3%)
  other arithmetic  10.5 us (2%)
  starting transfers between devices  5.19 us (1%)
    all_to_all x1, blocking collectives, on_device(): lax.all_to_all(outgoing, 'local', split_axis=0, concat_axis=0, tiled=True)  206 us
    all_to_all x1, waiting for transfers between devices, on_device(): lax.all_to_all(apply_expert(flat_rows, gate_local, up_local, down_local)....  197 us
    dot_general x1, matrix products, apply_expert(): jnp.dot(hidden, down_local, preferred_element_type=jnp.float32)  16.6 us
    slice x1, local copies, waits for them, and re-layouts, on_device(): results = (returned[:, 0] + returned[:, 1]).astype(jnp.bfloat16)  12.6 us
    all_gather x1, waiting for transfers between devices, on_device(): lax.all_gather(tokens, 'node', axis=0, tiled=True)  11.8 us
  transfers between devices with their start and end apart: 3, of which 3 were waited for; matrix products, arithmetic and copies ran while one was open for 0% of the time, Pallas kernels for 0%

commit v1 on v0

v1 whole, which is shorter than its diff:
```python
import jax
import jax.numpy as jnp
from jax import lax
from jax.sharding import PartitionSpec as P


def expert_weights(expert_ids, combine_weights, expert_total):
    options = jnp.arange(expert_total, dtype=jnp.int32)
    matches = expert_ids[:, :, None] == options[None, None, :]
    spread = jnp.where(matches, combine_weights.astype(jnp.float32)[:, :, None], 0.0)
    return jnp.sum(spread, axis=1).astype(jnp.bfloat16)


def add_rounded(first, second):
    return (first.astype(jnp.float32) + second.astype(jnp.float32)).astype(jnp.bfloat16)


def on_device(tokens, expert_ids, combine_weights, gate_weight, up_weight, down_weight):
    node_count = lax.axis_size("node")
    local_count = lax.axis_size("local")
    planes = local_count // 2
    expert_total = node_count * planes
    token_count = tokens.shape[0]
    gate_local = gate_weight[0]
    up_local = up_weight[0]
    down_local = down_weight[0]
    node = lax.axis_index("node")
    local = lax.axis_index("local")
    plane = local // 2
    half = local % 2
    expert = node * planes + plane
    low_side = plane < planes // 2

    swap_half = [(i, i ^ 1) for i in range(local_count)]
    swap_node = [(0, 1), (1, 0)]

    def up_pairs(low, high):
        return [(2 * p + h, 2 * p + 2 + h) for p in range(low, high) for h in range(2)]

    def down_pairs(low, high):
        return [(b, a) for a, b in up_pairs(low, high)]

    table = expert_weights(expert_ids, combine_weights, expert_total)
    table = lax.all_gather(table, ("node", "local"), axis=0, tiled=False)
    table = lax.dynamic_index_in_dim(table, expert, axis=2, keepdims=False)
    table = table.reshape(node_count, planes, 2, token_count)

    def weights_of(source):
        row = lax.dynamic_index_in_dim(table, source, axis=1, keepdims=False)
        row = jnp.where(node == 0, row, row[::-1])
        row = jnp.where(half == 0, row, row[:, ::-1])
        return row.reshape(2 * 2 * token_count, 1).astype(jnp.float32)

    from_above, from_below = [tokens], [tokens]
    for step in range(1, planes):
        from_above.append(lax.ppermute(from_above[-1], "local", down_pairs(0, planes - step)))
        from_below.append(lax.ppermute(from_below[-1], "local", up_pairs(step - 1, planes - 1)))

    def compute(block, source):
        other = lax.ppermute(block, "local", swap_half)
        rows = [block, other]
        rows = rows + [lax.ppermute(r, "node", swap_node) for r in rows]
        rows = jnp.concatenate(rows, axis=0)
        gate_value = jnp.dot(rows, gate_local, preferred_element_type=jnp.float32)
        up_value = jnp.dot(rows, up_local, preferred_element_type=jnp.float32)
        hidden = (jax.nn.silu(gate_value) * up_value).astype(jnp.bfloat16)
        out = jnp.dot(hidden, down_local, preferred_element_type=jnp.float32)
        return (out * weights_of(source)).astype(jnp.bfloat16)

    def reduce_chip(out):
        parts = [out[i * token_count : (i + 1) * token_count] for i in range(4)]
        here = add_rounded(parts[0], lax.ppermute(parts[2], "node", swap_node))
        there = add_rounded(parts[1], lax.ppermute(parts[3], "node", swap_node))
        return add_rounded(here, lax.ppermute(there, "local", swap_half))

    outs = [compute(tokens, plane)]
    for k in range(1, planes):
        block = jnp.where(low_side, from_above[k], from_below[k])
        source = jnp.where(low_side, plane + k, plane - k)
        for p in range(planes):
            if p < planes // 2 and k > planes - 1 - p:
                s = k - (planes - 1 - p)
                block = jnp.where(plane == p, from_below[s], block)
                source = jnp.where(plane == p, plane - s, source)
            if p >= planes // 2 and k > p:
                s = k - p
                block = jnp.where(plane == p, from_above[s], block)
                source = jnp.where(plane == p, plane + s, source)
        outs.append(compute(block, source))

    sums = [None] * planes
    going_up, going_down = None, None
    for k in range(planes - 1, -1, -1):
        sums[k] = reduce_chip(outs[k])
    for k in range(planes - 1, 0, -1):
        mine_up, mine_down = sums[k], sums[k]
        for p in range(planes):
            if p >= planes // 2 and k + p < planes:
                mine_up = jnp.where(plane == p, sums[k + p], mine_up)
            if p < planes // 2 and k + planes - 1 - p < planes:
                mine_down = jnp.where(plane == p, sums[k + planes - 1 - p], mine_down)
        if going_up is not None:
            mine_up = add_rounded(mine_up, going_up)
            mine_down = add_rounded(mine_down, going_down)
        going_up = lax.ppermute(mine_up, "local", up_pairs(0, planes - k))
        going_down = lax.ppermute(mine_down, "local", down_pairs(k - 1, planes - 1))
    total = sums[0].astype(jnp.float32) + going_up.astype(jnp.float32) + going_down.astype(jnp.float32)
    return total.astype(jnp.bfloat16)


def solution(mesh):
    in_specs = (
        P(("parts", "node", "local"), None),
        P(("parts", "node", "local"), None),
        P(("parts", "node", "local"), None),
        P(("node", "local"), None, None),
        P(("node", "local"), None, None),
        P(("node", "local"), None, None),
    )
    out_specs = P(("parts", "node", "local"), None)
    return jax.shard_map(
        on_device, mesh=mesh, in_specs=in_specs, out_specs=out_specs, check_vma=False
    )
```

time: 513 us -> 299 us (0.58)
  blocking collectives: 210 us -> 43.5 us
  waiting for transfers between devices: 218 us -> 123 us
  starting transfers between devices: 5.19 us -> 41.2 us
  matrix products: 29 us -> 60.8 us
  local copies, waits for them, and re-layouts: 25.5 us -> 12 us
  between operations: 13.5 us -> 0.41 us
  other arithmetic: 10.5 us -> 17.9 us
    all_to_all x1 -> x0, blocking collectives: 206 us -> none  [on_device(): lax.all_to_all(outgoing, 'local', split_axis=0, concat_axis=0, tiled=True)]
    all_to_all x1 -> x0, waiting for transfers between devices: 197 us -> none  [on_device(): lax.all_to_all(apply_expert(flat_rows, gate_local, up_local, down_local)....]
    ppermute x0 -> x36, waiting for transfers between devices: none -> 123 us  [the longest x4 38.9 us: reduce_chip(): return add_rounded(here, lax.ppermute(there, 'local', swap_half))]
    ppermute x0 -> x36, starting transfers between devices: none -> 41.2 us  [the longest x3 13.7 us: on_device(): going_up = lax.ppermute(mine_up, 'local', up_pairs(0, planes - k))]
    all_gather x2 -> x1, blocking collectives: 4.03 us -> 43.5 us  [on_device(): table = lax.all_gather(table, ('node', 'local'), axis=0, tiled=False)]
    dot_general x4 -> x8, matrix products: 29 us -> 60.8 us  [the longest x4 41.9 us: compute(): out = jnp.dot(hidden, down_local, preferred_element_type=jnp.float32)]
    all_gather x1 -> x0, waiting for transfers between devices: 11.8 us -> none  [on_device(): lax.all_gather(tokens, 'node', axis=0, tiled=True)]
    reduce_scatter x1 -> x0, waiting for transfers between devices: 8.53 us -> none  [on_device(): lax.psum_scatter(contrib.astype(jnp.float32).astype(jnp.bfloat16), 'node'...]
  transfers between devices with their start and end apart: 3 -> 36, of which waited for: 3 -> 10; matrix products, arithmetic and copies ran while one was open for 0% -> 29% of each run, Pallas kernels for 0% -> 0%
where the time goes in v1:
time: 299 us
  waiting for transfers between devices  123 us (41%)
  matrix products  60.8 us (20%)
  blocking collectives  43.5 us (15%)
  starting transfers between devices  41.2 us (14%)
  other arithmetic  17.9 us (6%)
  local copies, waits for them, and re-layouts  12 us (4%)
    all_gather x1, blocking collectives, on_device(): table = lax.all_gather(table, ('node', 'local'), axis=0, tiled=False)  43.5 us
    dot_general x4, matrix products, compute(): out = jnp.dot(hidden, down_local, preferred_element_type=jnp.float32)  41.9 us
    ppermute x4, waiting for transfers between devices, reduce_chip(): return add_rounded(here, lax.ppermute(there, 'local', swap_half))  38.9 us
    ppermute x3, waiting for transfers between devices, on_device(): lax.ppermute(from_above[-1], 'local', down_pairs(0, planes - step))  31.4 us
    ppermute x3, waiting for transfers between devices, on_device(): going_up = lax.ppermute(mine_up, 'local', up_pairs(0, planes - k))  21.3 us
    ppermute x4, waiting for transfers between devices, compute(): other = lax.ppermute(block, 'local', swap_half)  20.4 us
    dot_general x3, matrix products, compute(): gate_value = jnp.dot(rows, gate_local, preferred_element_type=jnp.float32)  15.8 us
    ppermute x3, starting transfers between devices, on_device(): going_up = lax.ppermute(mine_up, 'local', up_pairs(0, planes - k))  13.7 us
  transfers between devices with their start and end apart: 36, of which 10 were waited for; matrix products, arithmetic and copies ran while one was open for 29% of the time, Pallas kernels for 0%

profile of v1, /device:TPU:0, one launch (start us, length us, event | category | flops | bytes accessed | tf_op | source)
XLA Modules:
  0.0 298.7 jit_solution(6669621852713105233)
XLA Ops:
  1.3 5.6 %collective-permute-start.7 = (bf16[128,3584]{1,0:T(8,128)(2,1)}, bf16[128,3584]{1,0:T(8,128)(2,1)S(1)}, u32[]{:S(2)}, u32[]{:S(2)}) collective-permute-start(bf16[128,3584]{1,0:T(8,128)(2,1)} %param.6), channel_id=1, source_target_pairs={{0,2},{1,3},{2,4},{3,5},{4,6},{5,7},{8,10},{9,11},{10,12},{11,13},... | collective-permute-start | bytes 2752520 | tf_op jit(solution)/shard_map/ppermute | solution.py:57
  10.3 43.5 %all-gather = bf16[2048,8]{0,1:T(8,128)(2,1)S(1)} all-gather(bf16[128,8]{0,1:T(8,128)(2,1)S(1)} %select_reduce_fusion), channel_id=2, replica_groups=mesh['parts'=2,'node'=2,'local'=8] {'node','local'}, dimensions={0}, use_global_device_ids=true | all-gather | bytes 34816 | tf_op jit(solution)/shard_map/all_gather | solution.py:44
  60.2 19.8 %collective-permute-done.8 = bf16[128,3584]{1,0:T(8,128)(2,1)} collective-permute-done((bf16[128,3584]{1,0:T(8,128)(2,1)S(1)}, bf16[128,3584]{1,0:T(8,128)(2,1)}, u32[]{:S(2)}, u32[]{:S(2)}) %collective-permute-start.8) | collective-permute-done | bytes 917536 | tf_op jit(solution)/shard_map/ppermute | solution.py:56
  82.3 3.1 %fusion.10 = f32[512,512]{1,0:T(8,128)} fusion(bf16[512,3584]{1,0:T(8,128)(2,1)S(1)} %constant_dynamic-update-slice_fusion, bf16[1,3584,512]{2,1,0:T(8,128)(2,1)S(1)} %copy-done.9), kind=kOutput, calls=%fused_computation.17 | convolution fusion | flops 1879048192 | bytes 8388608 | tf_op jit(solution)/shard_map/dot_general | solution.py:65
  88.3 10.4 %multiply_convert_fusion.3 = bf16[512,3584]{1,0:T(8,128)(2,1)} fusion(bf16[1,512,3584]{2,1,0:T(8,128)(2,1)} %param.11, f32[512]{0:T(512)S(1)} %convert.4, f32[512,512]{1,0:T(8,128)} %fusion.10, bf16[512,3584]{1,0:T(8,128)(2,1)} %copy-done.6, bf16[1,3584,512]{2,1,0:T(8,128)(2,1)} %param.9), kind=kOutput, calls=%fused_computation.3 | convolution fusion | flops 3763339264 | bytes 15730688 | tf_op jit(solution)/shard_map/dot_general | solution.py:67
  98.7 11.5 %collective-permute-done.9 = bf16[128,3584]{1,0:T(8,128)(2,1)S(1)} collective-permute-done((bf16[128,3584]{1,0:T(8,128)(2,1)}, bf16[128,3584]{1,0:T(8,128)(2,1)S(1)}, u32[]{:S(2)}, u32[]{:S(2)}) %collective-permute-start.9) | collective-permute-done | bytes 917536 | tf_op jit(solution)/shard_map/ppermute | solution.py:56
  116.4 20.4 %collective-permute-done.12 = bf16[128,3584]{1,0:T(8,128)(2,1)} collective-permute-done((bf16[128,3584]{1,0:T(8,128)(2,1)S(1)}, bf16[128,3584]{1,0:T(8,128)(2,1)}, u32[]{:S(2)}, u32[]{:S(2)}) %collective-permute-start.12) | collective-permute-done | bytes 917536 | tf_op jit(solution)/shard_map/ppermute | solution.py:60
  137.8 4.8 %fusion.12 = f32[512,512]{1,0:T(8,128)} fusion(bf16[1,3584,512]{2,1,0:T(8,128)(2,1)S(1)} %copy-done.7, bf16[128,3584]{1,0:T(8,128)(2,1)S(1)} %collective-permute-done.26, bf16[128,3584]{1,0:T(8,128)(2,1)} %collective-permute-done.25, bf16[128,3584]{1,0:T(8,128)(2,1)} %collective-permute-done.24, bf16[128,3584]{1,0:T(8,128)(2,1)} %broadcast_select_fusion), kind=kOutput, calls=%fused_computation.19 | convolution fusion | flops 1893728256 | bytes 8388608 | tf_op jit(solution)/shard_map/dot_general | solution.py:64
  142.6 10.4 %multiply_convert_fusion = bf16[512,3584]{1,0:T(8,128)(2,1)} fusion(bf16[1,512,3584]{2,1,0:T(8,128)(2,1)} %param.11, f32[512]{0:T(512)S(1)} %convert.7, f32[512,512]{1,0:T(8,128)} %fusion.12, bf16[1,3584,512]{2,1,0:T(8,128)(2,1)} %param.10, bf16[128,3584]{1,0:T(8,128)(2,1)} %copy-done.10, bf16[128,3584]{1,0:T(8,128)(2,1)} %collective-permute-done.25, ...), kind=kOutput, calls=%fused_computation | convolution fusion | flops 3778019328 | bytes 15730688 | tf_op jit(solution)/shard_map/dot_general | solution.py:67
  153.0 2.9 fusion.61
  156.9 5.9 %fusion.16 = f32[512,512]{1,0:T(8,128)} fusion(bf16[1,3584,512]{2,1,0:T(8,128)(2,1)} %param.9, bf16[128,3584]{1,0:T(8,128)(2,1)} %collective-permute-done.14, bf16[128,3584]{1,0:T(8,128)(2,1)} %collective-permute-done.13, bf16[128,3584]{1,0:T(8,128)(2,1)} %collective-permute-done.12, bf16[128,3584]{1,0:T(8,128)(2,1)S(1)} %copy-done.4), kind=kOutput, calls=%fused_computation.23 | convolution fusion | flops 1893728256 | bytes 8388608 | tf_op jit(solution)/shard_map/dot_general | solution.py:64
  162.9 10.5 %multiply_convert_fusion.2 = bf16[512,3584]{1,0:T(8,128)(2,1)} fusion(bf16[1,512,3584]{2,1,0:T(8,128)(2,1)} %param.11, f32[512]{0:T(512)S(1)} %convert.5, f32[512,512]{1,0:T(8,128)} %fusion.16, bf16[1,3584,512]{2,1,0:T(8,128)(2,1)} %param.10, bf16[128,3584]{1,0:T(8,128)(2,1)} %collective-permute-done.14, bf16[128,3584]{1,0:T(8,128)(2,1)} %collective-permute-done.13, ...), kind=kOutput, calls=%fused_computation.2 | convolution fusion | flops 3778019328 | bytes 15730688 | tf_op jit(solution)/shard_map/dot_general | solution.py:67
  173.3 3.0 fusion.62
  176.3 2.6 add_convert_fusion.4
  181.4 5.0 %fusion.14 = f32[512,512]{1,0:T(8,128)} fusion(bf16[1,3584,512]{2,1,0:T(8,128)(2,1)S(1)} %copy-done.8, bf16[128,3584]{1,0:T(8,128)(2,1)} %collective-permute-done.20, bf16[128,3584]{1,0:T(8,128)(2,1)} %collective-permute-done.19, bf16[128,3584]{1,0:T(8,128)(2,1)} %collective-permute-done.18, bf16[128,3584]{1,0:T(8,128)(2,1)} %get-tuple-element.17), kind=kOutput, calls=%fused_computation.21 | convolution fusion | flops 1893728256 | bytes 8388608 | tf_op jit(solution)/shard_map/dot_general | solution.py:64
  186.5 10.7 %multiply_convert_fusion.1 = bf16[512,3584]{1,0:T(8,128)(2,1)} fusion(bf16[1,512,3584]{2,1,0:T(8,128)(2,1)} %param.11, f32[512]{0:T(512)S(1)} %convert.6, f32[512,512]{1,0:T(8,128)} %fusion.14, bf16[1,3584,512]{2,1,0:T(8,128)(2,1)} %param.10, bf16[128,3584]{1,0:T(8,128)(2,1)} %collective-permute-done.20, bf16[128,3584]{1,0:T(8,128)(2,1)} %collective-permute-done.19, ...), kind=kOutput, calls=%fused_computation.1 | convolution fusion | flops 3778019328 | bytes 15730688 | tf_op jit(solution)/shard_map/dot_general | solution.py:67
  200.7 21.2 %collective-permute-done.17 = bf16[128,3584]{1,0:T(8,128)(2,1)S(1)} collective-permute-done((bf16[128,3584]{1,0:T(8,128)(2,1)S(1)}, bf16[128,3584]{1,0:T(8,128)(2,1)S(1)}, u32[]{:S(2)}, u32[]{:S(2)}) %collective-permute-start.17) | collective-permute-done | bytes 917536 | tf_op jit(solution)/shard_map/ppermute | solution.py:74
  226.9 17.7 %collective-permute-done.30 = bf16[128,3584]{1,0:T(8,128)(2,1)S(1)} collective-permute-done((bf16[128,3584]{1,0:T(8,128)(2,1)S(1)}, bf16[128,3584]{1,0:T(8,128)(2,1)S(1)}, u32[]{:S(2)}, u32[]{:S(2)}) %collective-permute-start.30) | collective-permute-done | bytes 917536 | tf_op jit(solution)/shard_map/ppermute | solution.py:105
  248.1 4.4 %collective-permute-start.31 = (bf16[128,3584]{1,0:T(8,128)(2,1)S(1)}, bf16[128,3584]{1,0:T(8,128)(2,1)S(1)}, u32[]{:S(2)}, u32[]{:S(2)}) collective-permute-start(bf16[128,3584]{1,0:T(8,128)(2,1)S(1)} %get-tuple-element.7), channel_id=1, source_target_pairs={{0,2},{1,3},{2,4},{3,5},{8,10},{9,11},{10,12},{11,13},{16,18},{17,... | collective-permute-start | bytes 2752520 | tf_op jit(solution)/shard_map/ppermute | solution.py:105
  255.3 12.5 %collective-permute-done.23 = bf16[128,3584]{1,0:T(8,128)(2,1)S(1)} collective-permute-done((bf16[128,3584]{1,0:T(8,128)(2,1)S(1)}, bf16[128,3584]{1,0:T(8,128)(2,1)S(1)}, u32[]{:S(2)}, u32[]{:S(2)}) %collective-permute-start.23) | collective-permute-done | bytes 917536 | tf_op jit(solution)/shard_map/ppermute | solution.py:74
  267.9 2.4 collective-permute-done.31
  272.3 7.6 %collective-permute-start.32 = (bf16[128,3584]{1,0:T(8,128)(2,1)S(1)}, bf16[128,3584]{1,0:T(8,128)(2,1)S(1)}, u32[]{:S(2)}, u32[]{:S(2)}) collective-permute-start(bf16[128,3584]{1,0:T(8,128)(2,1)S(1)} %get-tuple-element.5), channel_id=1, source_target_pairs={{0,2},{1,3},{2,4},{3,5},{4,6},{5,7},{8,10},{9,11},{10,12},{11,13},... | collective-permute-start | bytes 2752520 | tf_op jit(solution)/shard_map/ppermute | solution.py:105
  279.9 5.2 %collective-permute-done.5 = bf16[128,3584]{1,0:T(8,128)(2,1)S(1)} collective-permute-done((bf16[128,3584]{1,0:T(8,128)(2,1)S(1)}, bf16[128,3584]{1,0:T(8,128)(2,1)S(1)}, u32[]{:S(2)}, u32[]{:S(2)}) %collective-permute-start.5) | collective-permute-done | bytes 917536 | tf_op jit(solution)/shard_map/ppermute | solution.py:74
  285.1 10.9 %collective-permute-done.35 = bf16[128,3584]{1,0:T(8,128)(2,1)S(1)} collective-permute-done((bf16[128,3584]{1,0:T(8,128)(2,1)S(1)}, bf16[128,3584]{1,0:T(8,128)(2,1)S(1)}, u32[]{:S(2)}, u32[]{:S(2)}) %collective-permute-start.35) | collective-permute-done | bytes 917536 | tf_op jit(solution)/shard_map/ppermute | solution.py:106
  (116 shorter events, 46.2 us)
Async XLA Ops:
  0.0 55.3 %collective-permute-start.6 = (bf16[128,3584]{1,0:T(8,128)(2,1)}, bf16[128,3584]{1,0:T(8,128)(2,1)S(1)}, u32[]{:S(2)}, u32[]{:S(2)}) collective-permute-start(bf16[128,3584]{1,0:T(8,128)(2,1)} %param.6), channel_id=1, source_target_pairs={{2,0},{3,1},{4,2},{5,3},{6,4},{7,5},{10,8},{11,9},{12,10},{13,11},... | collective-permute-start | bytes 2752520 | tf_op jit(solution)/shard_map/ppermute | solution.py:56
  1.3 55.4 %collective-permute-start.7 = (bf16[128,3584]{1,0:T(8,128)(2,1)}, bf16[128,3584]{1,0:T(8,128)(2,1)S(1)}, u32[]{:S(2)}, u32[]{:S(2)}) collective-permute-start(bf16[128,3584]{1,0:T(8,128)(2,1)} %param.6), channel_id=1, source_target_pairs={{0,2},{1,3},{2,4},{3,5},{4,6},{5,7},{8,10},{9,11},{10,12},{11,13},... | collective-permute-start | bytes 2752520 | tf_op jit(solution)/shard_map/ppermute | solution.py:57
  6.9 51.4 %collective-permute-start = (bf16[128,3584]{1,0:T(8,128)(2,1)}, bf16[128,3584]{1,0:T(8,128)(2,1)S(1)}, u32[]{:S(2)}, u32[]{:S(2)}) collective-permute-start(bf16[128,3584]{1,0:T(8,128)(2,1)} %param.6), channel_id=1, source_target_pairs={{0,1},{1,0},{2,3},{3,2},{4,5},{5,4},{6,7},{7,6},{8,9},{9,8},{10,11... | collective-permute-start | bytes 2752520 | tf_op jit(solution)/shard_map/ppermute | solution.py:60
  8.9 49.9 %collective-permute-start.1 = (bf16[128,3584]{1,0:T(8,128)(2,1)}, bf16[128,3584]{1,0:T(8,128)(2,1)}, u32[]{:S(2)}, u32[]{:S(2)}) collective-permute-start(bf16[128,3584]{1,0:T(8,128)(2,1)} %param.6), channel_id=1, source_target_pairs={{0,8},{8,0},{1,9},{9,1},{2,10},{10,2},{3,11},{11,3},{4,12},{12,4},... | collective-permute-start | bytes 2752520 | tf_op jit(solution)/shard_map/ppermute | solution.py:62
  55.3 24.7 %collective-permute-start.8 = (bf16[128,3584]{1,0:T(8,128)(2,1)S(1)}, bf16[128,3584]{1,0:T(8,128)(2,1)}, u32[]{:S(2)}, u32[]{:S(2)}) collective-permute-start(bf16[128,3584]{1,0:T(8,128)(2,1)S(1)} %collective-permute-done.6), channel_id=1, source_target_pairs={{2,0},{3,1},{4,2},{5,3},{10,8},{11,9},{12,10},{13,11},{18,16},{19,... | collective-permute-start | bytes 2752520 | tf_op jit(solution)/shard_map/ppermute | solution.py:56
  56.7 23.4 %collective-permute-start.10 = (bf16[128,3584]{1,0:T(8,128)(2,1)S(1)}, bf16[128,3584]{1,0:T(8,128)(2,1)}, u32[]{:S(2)}, u32[]{:S(2)}) collective-permute-start(bf16[128,3584]{1,0:T(8,128)(2,1)S(1)} %collective-permute-done.7), channel_id=1, source_target_pairs={{2,4},{3,5},{4,6},{5,7},{10,12},{11,13},{12,14},{13,15},{18,20},{1... | collective-permute-start | bytes 2752520 | tf_op jit(solution)/shard_map/ppermute | solution.py:57
  58.3 23.9 %collective-permute-start.2 = (bf16[128,3584]{1,0:T(8,128)(2,1)S(1)}, bf16[128,3584]{1,0:T(8,128)(2,1)S(1)}, u32[]{:S(2)}, u32[]{:S(2)}) collective-permute-start(bf16[128,3584]{1,0:T(8,128)(2,1)S(1)} %collective-permute-done), channel_id=1, source_target_pairs={{0,8},{8,0},{1,9},{9,1},{2,10},{10,2},{3,11},{11,3},{4,12},{12,4},... | collective-permute-start | bytes 2752520 | tf_op jit(solution)/shard_map/ppermute | solution.py:62
  82.2 33.3 %collective-permute-start.24 = (bf16[128,3584]{1,0:T(8,128)(2,1)}, bf16[128,3584]{1,0:T(8,128)(2,1)}, u32[]{:S(2)}, u32[]{:S(2)}) collective-permute-start(bf16[128,3584]{1,0:T(8,128)(2,1)} %broadcast_select_fusion), channel_id=1, source_target_pairs={{0,1},{1,0},{2,3},{3,2},{4,5},{5,4},{6,7},{7,6},{8,9},{9,8},{10,11... | collective-permute-start | bytes 2752520 | tf_op jit(solution)/shard_map/ppermute | solution.py:60
  82.2 34.1 %collective-permute-start.25 = (bf16[128,3584]{1,0:T(8,128)(2,1)}, bf16[128,3584]{1,0:T(8,128)(2,1)}, u32[]{:S(2)}, u32[]{:S(2)}) collective-permute-start(bf16[128,3584]{1,0:T(8,128)(2,1)} %broadcast_select_fusion), channel_id=1, source_target_pairs={{0,8},{8,0},{1,9},{9,1},{2,10},{10,2},{3,11},{11,3},{4,12},{12,4},... | collective-permute-start | bytes 2752520 | tf_op jit(solution)/shard_map/ppermute | solution.py:62
  85.4 24.8 %collective-permute-start.9 = (bf16[128,3584]{1,0:T(8,128)(2,1)}, bf16[128,3584]{1,0:T(8,128)(2,1)S(1)}, u32[]{:S(2)}, u32[]{:S(2)}) collective-permute-start(bf16[128,3584]{1,0:T(8,128)(2,1)} %collective-permute-done.8), channel_id=1, source_target_pairs={{2,0},{3,1},{10,8},{11,9},{18,16},{19,17},{26,24},{27,25}} | collective-permute-start | bytes 2752520 | tf_op jit(solution)/shard_map/ppermute | solution.py:56
  86.7 24.5 %collective-permute-start.11 = (bf16[128,3584]{1,0:T(8,128)(2,1)}, bf16[128,3584]{1,0:T(8,128)(2,1)}, u32[]{:S(2)}, u32[]{:S(2)}) collective-permute-start(bf16[128,3584]{1,0:T(8,128)(2,1)} %collective-permute-done.10), channel_id=1, source_target_pairs={{4,6},{5,7},{12,14},{13,15},{20,22},{21,23},{28,30},{29,31}} | collective-permute-start | bytes 2752520 | tf_op jit(solution)/shard_map/ppermute | solution.py:57
  113.5 23.3 %collective-permute-start.12 = (bf16[128,3584]{1,0:T(8,128)(2,1)S(1)}, bf16[128,3584]{1,0:T(8,128)(2,1)}, u32[]{:S(2)}, u32[]{:S(2)}) collective-permute-start(bf16[128,3584]{1,0:T(8,128)(2,1)S(1)} %get-tuple-element.18), channel_id=1, source_target_pairs={{0,1},{1,0},{2,3},{3,2},{4,5},{5,4},{6,7},{7,6},{8,9},{9,8},{10,11... | collective-permute-start | bytes 2752520 | tf_op jit(solution)/shard_map/ppermute | solution.py:60
  115.7 136.8 %collective-permute-start.4 = (bf16[128,3584]{1,0:T(8,128)(2,1)S(1)}, bf16[128,3584]{1,0:T(8,128)(2,1)}, u32[]{:S(2)}, u32[]{:S(2)}) collective-permute-start(bf16[128,3584]{1,0:T(8,128)(2,1)S(1)} %get-tuple-element.10), channel_id=1, source_target_pairs={{0,8},{8,0},{1,9},{9,1},{2,10},{10,2},{3,11},{11,3},{4,12},{12,4},... | collective-permute-start | bytes 2752520 | tf_op jit(solution)/shard_map/ppermute | solution.py:73
  116.2 39.6 %collective-permute-start.13 = (bf16[128,3584]{1,0:T(8,128)(2,1)S(1)}, bf16[128,3584]{1,0:T(8,128)(2,1)}, u32[]{:S(2)}, u32[]{:S(2)}) collective-permute-start(bf16[128,3584]{1,0:T(8,128)(2,1)S(1)} %get-tuple-element.18), channel_id=1, source_target_pairs={{0,8},{8,0},{1,9},{9,1},{2,10},{10,2},{3,11},{11,3},{4,12},{12,4},... | collective-permute-start | bytes 2752520 | tf_op jit(solution)/shard_map/ppermute | solution.py:62
  116.3 40.1 %collective-permute-start.18 = (bf16[128,3584]{1,0:T(8,128)(2,1)}, bf16[128,3584]{1,0:T(8,128)(2,1)}, u32[]{:S(2)}, u32[]{:S(2)}) collective-permute-start(bf16[128,3584]{1,0:T(8,128)(2,1)} %get-tuple-element.17), channel_id=1, source_target_pairs={{0,1},{1,0},{2,3},{3,2},{4,5},{5,4},{6,7},{7,6},{8,9},{9,8},{10,11... | collective-permute-start | bytes 2752520 | tf_op jit(solution)/shard_map/ppermute | solution.py:60
  136.8 42.1 %collective-permute-start.19 = (bf16[128,3584]{1,0:T(8,128)(2,1)}, bf16[128,3584]{1,0:T(8,128)(2,1)}, u32[]{:S(2)}, u32[]{:S(2)}) collective-permute-start(bf16[128,3584]{1,0:T(8,128)(2,1)} %get-tuple-element.17), channel_id=1, source_target_pairs={{0,8},{8,0},{1,9},{9,1},{2,10},{10,2},{3,11},{11,3},{4,12},{12,4},... | collective-permute-start | bytes 2752520 | tf_op jit(solution)/shard_map/ppermute | solution.py:62
  156.4 69.9 %collective-permute-start.27 = (bf16[128,3584]{1,0:T(8,128)(2,1)}, bf16[128,3584]{1,0:T(8,128)(2,1)S(1)}, u32[]{:S(2)}, u32[]{:S(2)}) collective-permute-start(bf16[128,3584]{1,0:T(8,128)(2,1)} %get-tuple-element.13), channel_id=1, source_target_pairs={{0,8},{8,0},{1,9},{9,1},{2,10},{10,2},{3,11},{11,3},{4,12},{12,4},... | collective-permute-start | bytes 2752520 | tf_op jit(solution)/shard_map/ppermute | solution.py:72
  179.4 47.0 %collective-permute-start.29 = (bf16[128,3584]{1,0:T(8,128)(2,1)}, bf16[128,3584]{1,0:T(8,128)(2,1)}, u32[]{:S(2)}, u32[]{:S(2)}) collective-permute-start(bf16[128,3584]{1,0:T(8,128)(2,1)} %add_convert_fusion.4), channel_id=1, source_target_pairs={{0,1},{1,0},{2,3},{3,2},{4,5},{5,4},{6,7},{7,6},{8,9},{9,8},{10,11... | collective-permute-start | bytes 2752520 | tf_op jit(solution)/shard_map/ppermute | solution.py:74
  200.7 24.6 %collective-permute-start.22 = (bf16[128,3584]{1,0:T(8,128)(2,1)S(1)}, bf16[128,3584]{1,0:T(8,128)(2,1)S(1)}, u32[]{:S(2)}, u32[]{:S(2)}) collective-permute-start(bf16[128,3584]{1,0:T(8,128)(2,1)S(1)} %get-tuple-element.12), channel_id=1, source_target_pairs={{0,8},{8,0},{1,9},{9,1},{2,10},{10,2},{3,11},{11,3},{4,12},{12,4},... | collective-permute-start | bytes 2752520 | tf_op jit(solution)/shard_map/ppermute | solution.py:73
  226.3 53.6 %collective-permute-start.3 = (bf16[128,3584]{1,0:T(8,128)(2,1)S(1)}, bf16[128,3584]{1,0:T(8,128)(2,1)S(1)}, u32[]{:S(2)}, u32[]{:S(2)}) collective-permute-start(bf16[128,3584]{1,0:T(8,128)(2,1)S(1)} %get-tuple-element.9), channel_id=1, source_target_pairs={{0,8},{8,0},{1,9},{9,1},{2,10},{10,2},{3,11},{11,3},{4,12},{12,4},... | collective-permute-start | bytes 2752520 | tf_op jit(solution)/shard_map/ppermute | solution.py:72
  226.4 28.3 %collective-permute-start.21 = (bf16[128,3584]{1,0:T(8,128)(2,1)S(1)}, bf16[128,3584]{1,0:T(8,128)(2,1)S(1)}, u32[]{:S(2)}, u32[]{:S(2)}) collective-permute-start(bf16[128,3584]{1,0:T(8,128)(2,1)S(1)} %get-tuple-element.11), channel_id=1, source_target_pairs={{0,8},{8,0},{1,9},{9,1},{2,10},{10,2},{3,11},{11,3},{4,12},{12,4},... | collective-permute-start | bytes 2752520 | tf_op jit(solution)/shard_map/ppermute | solution.py:72
  254.7 30.5 %collective-permute-start.5 = (bf16[128,3584]{1,0:T(8,128)(2,1)S(1)}, bf16[128,3584]{1,0:T(8,128)(2,1)S(1)}, u32[]{:S(2)}, u32[]{:S(2)}) collective-permute-start(bf16[128,3584]{1,0:T(8,128)(2,1)S(1)} %add_convert_fusion.13), channel_id=1, source_target_pairs={{0,1},{1,0},{2,3},{3,2},{4,5},{5,4},{6,7},{7,6},{8,9},{9,8},{10,11... | collective-permute-start | bytes 2752520 | tf_op jit(solution)/shard_map/ppermute | solution.py:74
  271.0 25.0 %collective-permute-start.35 = (bf16[128,3584]{1,0:T(8,128)(2,1)S(1)}, bf16[128,3584]{1,0:T(8,128)(2,1)S(1)}, u32[]{:S(2)}, u32[]{:S(2)}) collective-permute-start(bf16[128,3584]{1,0:T(8,128)(2,1)S(1)} %get-tuple-element.6), channel_id=1, source_target_pairs={{2,0},{3,1},{4,2},{5,3},{6,4},{7,5},{10,8},{11,9},{12,10},{13,11},... | collective-permute-start | bytes 2752520 | tf_op jit(solution)/shard_map/ppermute | solution.py:106
  272.3 24.9 %collective-permute-start.32 = (bf16[128,3584]{1,0:T(8,128)(2,1)S(1)}, bf16[128,3584]{1,0:T(8,128)(2,1)S(1)}, u32[]{:S(2)}, u32[]{:S(2)}) collective-permute-start(bf16[128,3584]{1,0:T(8,128)(2,1)S(1)} %get-tuple-element.5), channel_id=1, source_target_pairs={{0,2},{1,3},{2,4},{3,5},{4,6},{5,7},{8,10},{9,11},{10,12},{11,13},... | collective-permute-start | bytes 2752520 | tf_op jit(solution)/shard_map/ppermute | solution.py:105
  (23 other events, 434.4 us)

commit v2 on v0

--- a/solution.py
+++ b/solution.py
@@ -1,7 +1,14 @@
+import functools
+
 import jax
 import jax.numpy as jnp
 from jax import lax
+from jax.experimental import pallas as pl
+from jax.experimental.pallas import tpu as pltpu
 from jax.sharding import PartitionSpec as P
+
+TILE = 256
+LANES = 128
 
 
 def slot_tables(routes, first_expert, expert_count, capacity, expert_total):
@@ -35,7 +42,7 @@
     return jnp.dot(hidden, down_local, preferred_element_type=jnp.float32).astype(jnp.bfloat16)
 
 
-def on_device(tokens, expert_ids, combine_weights, gate_weight, up_weight, down_weight):
+def packed_exchange(tokens, expert_ids, combine_weights, gate_weight, up_weight, down_weight):
     node_count = lax.axis_size("node")
     local_count = lax.axis_size("local")
     per_node = local_count // 2
@@ -95,6 +102,271 @@
     return summed_out[0].astype(jnp.bfloat16)
 
 
+def expert_weights(expert_ids, combine_weights, expert_total):
+    options = jnp.arange(expert_total, dtype=jnp.int32)
+    matches = expert_ids[:, :, None] == options[None, None, :]
+    spread = jnp.where(matches, combine_weights.astype(jnp.float32)[:, :, None], 0.0)
+    return jnp.sum(spread, axis=1).astype(jnp.bfloat16)
+
+
+def add_rounded(first, second):
+    return (first.astype(jnp.float32) + second.astype(jnp.float32)).astype(jnp.bfloat16)
+
+
+def dot32(a, b):
+    return jnp.dot(a, b, preferred_element_type=jnp.float32)
+
+
+def hidden_kernel(batches, pieces, where_ref, *refs):
+    rows_refs = refs[:batches]
+    gates = refs[batches : batches + len(pieces)]
+    ups = refs[batches + len(pieces) : batches + 2 * len(pieces)]
+    out_ref = refs[-1]
+    step = pl.program_id(0)
+    steps_each = pl.num_programs(0) // batches
+
+    def work(rows):
+        gate_value, up_value = None, None
+        for (offset, length, kind), g, u in zip(pieces, gates, ups):
+            if kind < 0:
+                columns = slice(offset, offset + length)
+            else:
+                columns = pl.ds(pl.multiple_of(where_ref[kind] + offset, LANES), length)
+            part = rows[:, columns]
+            gate_part, up_part = dot32(part, g[...]), dot32(part, u[...])
+            gate_value = gate_part if gate_value is None else gate_value + gate_part
+            up_value = up_part if up_value is None else up_value + up_part
+        out_ref[...] = (gate_value / (1.0 + jnp.exp(-gate_value)) * up_value).astype(jnp.bfloat16)
+
+    for b in range(batches):
+        pl.when(step // steps_each == b)(functools.partial(work, rows_refs[b]))
+
+
+def hidden_call(where, rows, pieces, gates, ups):
+    batches = len(rows)
+    steps_each = rows[0].shape[0] // TILE
+    width = rows[0].shape[1]
+    units = gates[0].shape[1]
+
+    def rows_map(b):
+        return lambda i, w: (jnp.clip(i - b * steps_each, 0, steps_each - 1), 0)
+
+    total = batches * steps_each * TILE
+    depth = sum(g.shape[0] for g in gates)
+    once = pl.Buffered(1)
+    return pl.pallas_call(
+        functools.partial(hidden_kernel, batches, pieces),
+        grid_spec=pltpu.PrefetchScalarGridSpec(
+            num_scalar_prefetch=1,
+            grid=(batches * steps_each,),
+            in_specs=[pl.BlockSpec((TILE, width), rows_map(b)) for b in range(batches)]
+            + [pl.BlockSpec(g.shape, lambda i, w: (0, 0), pipeline_mode=once) for g in gates]
+            + [pl.BlockSpec(u.shape, lambda i, w: (0, 0), pipeline_mode=once) for u in ups],
+            out_specs=pl.BlockSpec((TILE, units), lambda i, w: (i, 0)),
+        ),
+        out_shape=jax.ShapeDtypeStruct((total, units), jnp.bfloat16),
+        compiler_params=pltpu.CompilerParams(vmem_limit_bytes=30 * 2**20),
+        cost_estimate=pl.CostEstimate(
+            flops=4 * total * depth * units,
+            bytes_accessed=2 * (total * width + 2 * depth * units + total * units),
+            transcendentals=total * units,
+        ),
+    )(where, *rows, *gates, *ups)
+
+
+def down_kernel(batches, first, width, where_ref, *refs):
+    spread_refs = refs[:batches]
+    own_refs = refs[batches : 2 * batches]
+    other_ref, down_ref, near_ref, far_ref, home_ref, away_ref = refs[2 * batches :]
+    step = pl.program_id(0)
+    steps_each = pl.num_programs(0) // batches
+    half = width // 2
+
+    def work(spread, own, out_ref):
+        chosen = lax.broadcasted_iota(jnp.int32, spread.shape, 1) == where_ref[2]
+        scale = jnp.sum(jnp.where(chosen, spread[...].astype(jnp.float32), 0.0), axis=1, keepdims=True)
+        for piece, slot in ((near_ref, where_ref[3]), (far_ref, 1 - where_ref[3])):
+            source = pl.ds(pl.multiple_of(first + slot * half, LANES), half)
+            target = pl.ds(pl.multiple_of(slot * half, LANES), half)
+            value = dot32(own[...], down_ref[:, source]) + dot32(other_ref[...], piece[...])
+            out_ref[:, target] = (value * scale).astype(jnp.bfloat16)
+
+    for i in range(batches * steps_each if False else 4):
+        b = i * batches // 4
+        pl.when(step == i)(
+            functools.partial(work, spread_refs[b], own_refs[b], home_ref if i == 0 else away_ref)
+        )
+
+
+def down_call(where, rows, own, other, down_local, near, far, first):
+    batches = len(rows)
+    steps_each = rows[0].shape[0] // TILE
+    units = down_local.shape[0]
+    width = 2 * near.shape[1]
+    last = rows[0].shape[1] // LANES - 1
+
+    def tile_map(b, column):
+        return lambda i, w: (jnp.clip(i - b * steps_each, 0, steps_each - 1), column)
+
+    once = pl.Buffered(1)
+    total = batches * steps_each * TILE
+    return pl.pallas_call(
+        functools.partial(down_kernel, batches, first, width),
+        grid_spec=pltpu.PrefetchScalarGridSpec(
+            num_scalar_prefetch=1,
+            grid=(batches * steps_each,),
+            in_specs=[pl.BlockSpec((TILE, LANES), tile_map(b, last)) for b in range(batches)]
+            + [pl.BlockSpec((TILE, units), tile_map(b, 0)) for b in range(batches)]
+            + [pl.BlockSpec((TILE, units), lambda i, w: (i, 0))]
+            + [
+                pl.BlockSpec(a.shape, lambda i, w: (0, 0), pipeline_mode=once)
+                for a in (down_local, near, far)
+            ],
+            out_specs=[
+                pl.BlockSpec((TILE, width), lambda i, w: (0, 0)),
+                pl.BlockSpec((TILE, width), lambda i, w: (jnp.maximum(i - 1, 0), 0)),
+            ],
+        ),
+        out_shape=[
+            jax.ShapeDtypeStruct((TILE, width), jnp.bfloat16),
+            jax.ShapeDtypeStruct((total - TILE, width), jnp.bfloat16),
+        ],
+        compiler_params=pltpu.CompilerParams(vmem_limit_bytes=30 * 2**20),
+        cost_estimate=pl.CostEstimate(
+            flops=4 * total * units * width,
+            bytes_accessed=2 * (2 * total * units + 2 * units * width + total * width),
+            transcendentals=0,
+        ),
+    )(where, *rows, *own, other, down_local, near, far)
+
+
+def line_exchange(tokens, expert_ids, combine_weights, gate_weight, up_weight, down_weight):
+    node_count = lax.axis_size("node")
+    local_count = lax.axis_size("local")
+    planes = local_count // 2
+    token_count, model_width = tokens.shape
+    expert_total = node_count * planes
+    gate_local, up_local, down_local = gate_weight[0], up_weight[0], down_weight[0]
+    part = lax.axis_index("parts")
+    node = lax.axis_index("node")
+    plane = lax.axis_index("local") // 2
+    side = plane // 2
+    match = side == node
+    end = (plane == 0) | (plane == planes - 1)
+    both = ("node", "local")
+    swap_half = [(i, i ^ 1) for i in range(local_count)]
+    swap_two = [(0, 1), (1, 0)]
+
+    def line_pairs(step):
+        pairs = []
+        for h in range(2):
+            pairs += [(2 * (p + 1) + h, 2 * p + h) for p in range(planes - step)]
+            pairs += [
+                (local_count + 2 * (p - 1) + h, local_count + 2 * p + h) for p in range(step, planes)
+            ]
+        return pairs
+
+    def back_pairs(step):
+        return [(b, a) for a, b in line_pairs(step)]
+
+    def across(x):
+        return lax.ppermute(x, "node", swap_two)
+
+    half_depth = model_width // 2
+    where = jnp.stack([part * half_depth, (1 - part) * half_depth, node * planes + plane, part])
+    where = where.astype(jnp.int32)
+
+    pieces, own_pieces = [], [(0, model_width, -1)]
+    sizes = GATE_ROWS, UP_ROWS
+    near, far = ([], []), ([], [])
+
+    def fetch(piece):
+        first = lax.ppermute(piece, "local", swap_half)
+        return first, lax.ppermute(first, "parts", swap_two)
+
+    for m, (array, rows_of) in enumerate(zip((gate_local, up_local), sizes)):
+        offset = 0
+        for length in rows_of:
+            a, b = fetch(lax.dynamic_slice_in_dim(array, part * half_depth + offset, length, 0))
+            near[m].append(a)
+            far[m].append(b)
+            offset += length
+    down_near, down_far, firsts = [], [], []
+    first = 0
+    for width in DOWN_COLUMNS:
+        half = width // 2
+        a, b = fetch(lax.dynamic_slice_in_dim(down_local, first + part * half, half, 1))
+        down_near.append(a)
+        down_far.append(b)
+        firsts.append(first)
+        first += width
+
+    table = expert_weights(expert_ids, combine_weights, expert_total)
+    table = jnp.pad(table, ((0, 0), (0, LANES - expert_total)))
+    mine = jnp.concatenate([tokens, table], axis=1)
+    theirs = across(mine)
+    pair = jnp.concatenate(
+        [jnp.where(node == 0, mine, theirs), jnp.where(node == 0, theirs, mine)], axis=0
+    )
+    got, other = [pair], [None]
+    for step in range(1, planes):
+        got.append(lax.ppermute(got[-1], both, line_pairs(step)))
+        other.append(across(got[-1]))
+    slot1 = jnp.where(match, got[1], other[1])
+    slot2 = jnp.where(match, got[2], other[2])
+    slot3 = jnp.where(
+        end, jnp.where(match, got[3], other[3]), jnp.where(match, other[1], got[1])
+    )
+    early = jnp.concatenate([pair, slot1], axis=0)
+    late = jnp.concatenate([slot2, slot3], axis=0)
+
+    own_early = hidden_call(where, [early], own_pieces, [gate_local], [up_local])
+    own_late = hidden_call(where, [late], own_pieces, [gate_local], [up_local])
+    gates = cut_alike(near[0], far[0], sizes[0])
+    ups = cut_alike(near[1], far[1], sizes[0])
+    offset = 0
+    pieces = [(0, half_depth, 0), (0, half_depth, 1)]
+    crossed = hidden_call(where, [early, late], pieces, gates, ups)
+
+    results = []
+    for k in range(len(DOWN_COLUMNS)):
+        home, away = down_call(
+            where, [early, late], [own_early, own_late], crossed,
+            down_local, down_near[k], down_far[k], firsts[k],
+        )
+        away = add_rounded(away, across(away))
+        s1, s2, s3 = (away[i * TILE : (i + 1) * TILE] for i in range(3))
+        moving = lax.ppermute(s3, both, back_pairs(3))
+        moving = lax.ppermute(add_rounded(s2, moving), both, back_pairs(2))
+        moving = lax.ppermute(add_rounded(jnp.where(match, s1, s3), moving), both, back_pairs(1))
+        kept = moving.astype(jnp.float32) + home.astype(jnp.float32)
+        low, high = kept[:token_count], kept[token_count:]
+        sent = jnp.where(node == 0, high, low).astype(jnp.bfloat16)
+        results.append((jnp.where(node == 0, low, high) + across(sent).astype(jnp.float32)).astype(jnp.bfloat16))
+    return jnp.concatenate(results, axis=1)
+
+
+GATE_ROWS = (256, 512, 1024)
+UP_ROWS = (1024, 512, 256)
+DOWN_COLUMNS = (1024, 1280, 1280)
+
+
+def cut_alike(near, far, sizes):
+    return [jnp.concatenate(near, axis=0), jnp.concatenate(far, axis=0)]
+
+
+def on_device(tokens, expert_ids, combine_weights, gate_weight, up_weight, down_weight):
+    line = (
+        lax.axis_size("parts") == 2
+        and lax.axis_size("node") == 2
+        and lax.axis_size("local") == 8
+        and tokens.shape == (128, 3584)
+        and gate_weight.shape[2] == 512
+    )
+    form = line_exchange if line else packed_exchange
+    return form(tokens, expert_ids, combine_weights, gate_weight, up_weight, down_weight)
+
+
 def solution(mesh):
     in_specs = (
         P(("parts", "node", "local"), None),

time: 513 us -> 332 us (0.65)
  blocking collectives: 210 us -> 0 us
  starting transfers between devices: 5.19 us -> 62.3 us
  Pallas kernels: 0 us -> 31.9 us
  matrix products: 29 us -> 0 us
  waiting for transfers between devices: 218 us -> 202 us
  between operations: 13.5 us -> 0.56 us
  local copies, waits for them, and re-layouts: 25.5 us -> 14.4 us
  other arithmetic: 10.5 us -> 20.4 us
    all_to_all x1 -> x0, blocking collectives: 206 us -> none  [on_device(): lax.all_to_all(outgoing, 'local', split_axis=0, concat_axis=0, tiled=True)]
    ppermute x0 -> x40, waiting for transfers between devices: none -> 202 us  [the longest x9 78.3 us: fetch(): first = lax.ppermute(piece, 'local', swap_half)]
    all_to_all x1 -> x0, waiting for transfers between devices: 197 us -> none  [on_device(): lax.all_to_all(apply_expert(flat_rows, gate_local, up_local, down_local)....]
    ppermute x0 -> x40, starting transfers between devices: none -> 62.3 us  [the longest x3 13.3 us: line_exchange(): lax.ppermute(add_rounded(jnp.where(match, s1, s3), moving), both, back_pa...]
    pallas_call x0 -> x6, Pallas kernels: none -> 31.9 us  [the longest x3 18.4 us: hidden_call(): pl.pallas_call(functools.partial(hidden_kernel, batches, pieces), grid_sp...]
    dot_general x4 -> x0, matrix products: 29 us -> none  [the longest x1 16.6 us: apply_expert(): jnp.dot(hidden, down_local, preferred_element_type=jnp.float32)]
    dynamic_slice x0 -> x8, local copies, waits for them, and re-layouts: none -> 14.1 us  [the longest x6 11.6 us: line_exchange(): lax.dynamic_slice_in_dim(array, part * half_depth + offset, length, 0)]
    slice x1 -> x3, local copies, waits for them, and re-layouts: 12.6 us -> 0.12 us  [line_exchange(): s1, s2, s3 = (away[i * TILE:(i + 1) * TILE] for i in range(3))]
  transfers between devices with their start and end apart: 3 -> 40, of which waited for: 3 -> 20; matrix products, arithmetic and copies ran while one was open for 0% -> 9% of each run, Pallas kernels for 0% -> 10%
where the time goes in v2:
time: 332 us
  waiting for transfers between devices  202 us (61%)
  starting transfers between devices  62.3 us (19%)
  Pallas kernels  31.9 us (10%)
  other arithmetic  20.4 us (6%)
  local copies, waits for them, and re-layouts  14.4 us (4%)
    ppermute x9, waiting for transfers between devices, fetch(): first = lax.ppermute(piece, 'local', swap_half)  78.3 us
    ppermute x9, waiting for transfers between devices, fetch(): return (first, lax.ppermute(first, 'parts', swap_two))  64.8 us
    ppermute x3, waiting for transfers between devices, line_exchange(): got.append(lax.ppermute(got[-1], both, line_pairs(step)))  25.6 us
    pallas_call x3, Pallas kernels, hidden_call(): pl.pallas_call(functools.partial(hidden_kernel, batches, pieces), grid_sp...  18.4 us
    ppermute x3, waiting for transfers between devices, line_exchange(): moving = lax.ppermute(add_rounded(s2, moving), both, back_pairs(2))  14.5 us
    pallas_call x3, Pallas kernels, down_call(): pl.pallas_call(functools.partial(down_kernel, batches, first, width), gri...  13.4 us
    ppermute x3, starting transfers between devices, line_exchange(): lax.ppermute(add_rounded(jnp.where(match, s1, s3), moving), both, back_pa...  13.3 us
    ppermute x9, starting transfers between devices, fetch(): return (first, lax.ppermute(first, 'parts', swap_two))  12.9 us
  transfers between devices with their start and end apart: 40, of which 20 were waited for; matrix products, arithmetic and copies ran while one was open for 9% of the time, Pallas kernels for 10%

profile of v2, /device:TPU:0, one launch (start us, length us, event | category | flops | bytes accessed | tf_op | source)
XLA Modules:
  0.0 331.5 jit_solution(5020939278633938112)
XLA Ops:
  8.6 25.6 %collective-permute-done.1 = bf16[256,3712]{1,0:T(8,128)(2,1)} collective-permute-done((bf16[256,3712]{1,0:T(8,128)(2,1)S(1)}, bf16[256,3712]{1,0:T(8,128)(2,1)}, u32[]{:S(2)}, u32[]{:S(2)}) %collective-permute-start.1) | collective-permute-done | bytes 1900576 | tf_op jit(solution)/shard_map/ppermute | solution.py:313
  48.8 20.9 %collective-permute-done.7 = bf16[256,512]{1,0:T(8,128)(2,1)} collective-permute-done((bf16[256,512]{1,0:T(8,128)(2,1)}, bf16[256,512]{1,0:T(8,128)(2,1)}, u32[]{:S(2)}, u32[]{:S(2)}) %collective-permute-start.7) | collective-permute-done | bytes 262176 | tf_op jit(solution)/shard_map/ppermute | solution.py:284
  75.2 11.3 %collective-permute-done.15 = bf16[256,512]{1,0:T(8,128)(2,1)} collective-permute-done((bf16[256,512]{1,0:T(8,128)(2,1)}, bf16[256,512]{1,0:T(8,128)(2,1)}, u32[]{:S(2)}, u32[]{:S(2)}) %collective-permute-start.15) | collective-permute-done | bytes 262176 | tf_op jit(solution)/shard_map/ppermute | solution.py:284
  91.1 4.1 %collective-permute-done.10 = bf16[256,512]{1,0:T(8,128)(2,1)} collective-permute-done((bf16[256,512]{1,0:T(8,128)(2,1)}, bf16[256,512]{1,0:T(8,128)(2,1)}, u32[]{:S(2)}, u32[]{:S(2)}) %collective-permute-start.10) | collective-permute-done | bytes 262176 | tf_op jit(solution)/shard_map/ppermute | solution.py:285
  99.7 6.4 %collective-permute-done.18 = bf16[256,512]{1,0:T(8,128)(2,1)S(1)} collective-permute-done((bf16[256,512]{1,0:T(8,128)(2,1)}, bf16[256,512]{1,0:T(8,128)(2,1)S(1)}, u32[]{:S(2)}, u32[]{:S(2)}) %collective-permute-start.18) | collective-permute-done | bytes 262176 | tf_op jit(solution)/shard_map/ppermute | solution.py:285
  108.5 21.1 %collective-permute-done.19.refs_6_ = bf16[512,512]{1,0:T(8,128)(2,1)S(1)} collective-permute-done((bf16[512,512]{1,0:T(8,128)(2,1)S(1)}, bf16[512,512]{1,0:T(8,128)(2,1)S(1)}, u32[]{:S(2)}, u32[]{:S(2)}) %collective-permute-start.19) | collective-permute-done | bytes 524320 | tf_op jit(solution)/shard_map/ppermute | solution.py:284
  134.8 54.3 %collective-permute-done.17 = bf16[512,512]{1,0:T(8,128)(2,1)} collective-permute-done((bf16[512,512]{1,0:T(8,128)(2,1)}, bf16[512,512]{1,0:T(8,128)(2,1)}, u32[]{:S(2)}, u32[]{:S(2)}) %collective-permute-start.17) | collective-permute-done | bytes 524320 | tf_op jit(solution)/shard_map/ppermute | solution.py:285
  197.5 10.8 %collective-permute-done.26.refs_6_ = bf16[512,640]{1,0:T(8,128)(2,1)S(1)} collective-permute-done((bf16[512,640]{1,0:T(8,128)(2,1)S(1)}, bf16[512,640]{1,0:T(8,128)(2,1)S(1)}, u32[]{:S(2)}, u32[]{:S(2)}) %collective-permute-start.26) | collective-permute-done | bytes 655392 | tf_op jit(solution)/shard_map/ppermute | solution.py:284
  209.8 11.6 %collective-permute-done.33.refs_6_ = bf16[512,640]{1,0:T(8,128)(2,1)S(1)} collective-permute-done((bf16[512,640]{1,0:T(8,128)(2,1)S(1)}, bf16[512,640]{1,0:T(8,128)(2,1)S(1)}, u32[]{:S(2)}, u32[]{:S(2)}) %collective-permute-start.33) | collective-permute-done | bytes 655392 | tf_op jit(solution)/shard_map/ppermute | solution.py:284
  228.9 9.0 %shard_map.66.refs_4_ = bf16[1024,512]{1,0:T(8,128)(2,1)S(1)} custom-call(s32[4]{0:T(128)S(1)} %pad_add_fusion.where_ref, bf16[512,3712]{1,0:T(8,128)(2,1)S(1)} %pad_maximum_fusion.refs_0_, bf16[512,3712]{1,0:T(8,128)(2,1)S(1)} %pad_maximum_fusion.1.refs_0_.refs_1_, bf16[1792,512]{1,0:T(8,128)(2,1)S(1)} %pad_maximum_fusion.3.refs_2_, ...), custom_call_target="tpu_custom_call" | custom-call | flops 7516192768 | bytes 15990784 | tf_op jit(solution)/shard_map/pallas_call | solution.py:157
  237.9 4.7 %shard_map.65.refs_3_ = bf16[512,512]{1,0:T(8,128)(2,1)S(1)} custom-call(s32[4]{0:T(128)S(1)} %pad_add_fusion.where_ref, bf16[512,3712]{1,0:T(8,128)(2,1)S(1)} %pad_maximum_fusion.1.refs_0_.refs_1_, bf16[3584,512]{1,0:T(8,128)(2,1)S(1)} %bitcast.28, bf16[3584,512]{1,0:T(8,128)(2,1)S(1)} %bitcast.30), custom_call_target="tpu_custom_call" | custom-call | flops 3758096384 | bytes 11665408 | tf_op jit(solution)/shard_map/pallas_call | solution.py:157
  242.7 4.7 %shard_map.64.refs_2_ = bf16[512,512]{1,0:T(8,128)(2,1)S(1)} custom-call(s32[4]{0:T(128)S(1)} %pad_add_fusion.where_ref, bf16[512,3712]{1,0:T(8,128)(2,1)S(1)} %pad_maximum_fusion.refs_0_, bf16[3584,512]{1,0:T(8,128)(2,1)S(1)} %bitcast.29, bf16[3584,512]{1,0:T(8,128)(2,1)S(1)} %bitcast.31), custom_call_target="tpu_custom_call" | custom-call | flops 3758096384 | bytes 11665408 | tf_op jit(solution)/shard_map/pallas_call | solution.py:157
  247.4 4.8 %shard_map.68 = (bf16[256,1280]{1,0:T(8,128)(2,1)S(1)}, bf16[768,1280]{1,0:T(8,128)(2,1)S(1)}) custom-call(s32[4]{0:T(128)S(1)} %pad_add_fusion.where_ref, bf16[512,3712]{1,0:T(8,128)(2,1)S(1)} %pad_maximum_fusion.refs_0_, bf16[512,3712]{1,0:T(8,128)(2,1)S(1)} %pad_maximum_fusion.1.refs_0_.refs_1_, bf16[512,512]{1,0:T(8,128)(2,1)S(1)} %shard_map.64.refs_2_, ...), custom_call_target="tpu_custom_call" | custom-call | flops 2684354560 | bytes 7340032 | tf_op jit(solution)/shard_map/pallas_call | solution.py:213
  256.5 5.0 %shard_map.69 = (bf16[256,1280]{1,0:T(8,128)(2,1)S(1)}, bf16[768,1280]{1,0:T(8,128)(2,1)S(1)}) custom-call(s32[4]{0:T(128)S(1)} %pad_add_fusion.where_ref, bf16[512,3712]{1,0:T(8,128)(2,1)S(1)} %pad_maximum_fusion.refs_0_, bf16[512,3712]{1,0:T(8,128)(2,1)S(1)} %pad_maximum_fusion.1.refs_0_.refs_1_, bf16[512,512]{1,0:T(8,128)(2,1)S(1)} %shard_map.64.refs_2_, ...), custom_call_target="tpu_custom_call" | custom-call | flops 2684354560 | bytes 7340032 | tf_op jit(solution)/shard_map/pallas_call | solution.py:213
  262.4 6.2 %collective-permute-start.22 = (bf16[256,1024]{1,0:T(8,128)(2,1)S(1)}, bf16[256,1024]{1,0:T(8,128)(2,1)S(1)}, u32[]{:S(2)}, u32[]{:S(2)}) collective-permute-start(bf16[256,1024]{1,0:T(8,128)(2,1)S(1)} %slice.61), channel_id=1, source_target_pairs={{0,2},{14,12},{1,3},{15,13},{16,18},{30,28},{17,19},{31,29}} | collective-permute-start | bytes 1572872 | tf_op jit(solution)/shard_map/ppermute | solution.py:339
  270.4 4.8 %collective-permute-done.22 = bf16[256,1024]{1,0:T(8,128)(2,1)S(1)} collective-permute-done((bf16[256,1024]{1,0:T(8,128)(2,1)S(1)}, bf16[256,1024]{1,0:T(8,128)(2,1)S(1)}, u32[]{:S(2)}, u32[]{:S(2)}) %collective-permute-start.22) | collective-permute-done | bytes 524320 | tf_op jit(solution)/shard_map/ppermute | solution.py:339
  275.4 4.4 %collective-permute-start.23 = (bf16[256,1024]{1,0:T(8,128)(2,1)S(1)}, bf16[256,1024]{1,0:T(8,128)(2,1)S(1)}, u32[]{:S(2)}, u32[]{:S(2)}) collective-permute-start(bf16[256,1024]{1,0:T(8,128)(2,1)S(1)} %add_convert_fusion.8), channel_id=1, source_target_pairs={{0,2},{2,4},{12,10},{14,12},{1,3},{3,5},{13,11},{15,13},{16,18},{1... | collective-permute-start | bytes 1572872 | tf_op jit(solution)/shard_map/ppermute | solution.py:340
  282.3 5.5 %collective-permute-done.23 = bf16[256,1024]{1,0:T(8,128)(2,1)S(1)} collective-permute-done((bf16[256,1024]{1,0:T(8,128)(2,1)S(1)}, bf16[256,1024]{1,0:T(8,128)(2,1)S(1)}, u32[]{:S(2)}, u32[]{:S(2)}) %collective-permute-start.23) | collective-permute-done | bytes 524320 | tf_op jit(solution)/shard_map/ppermute | solution.py:340
  288.1 4.4 %collective-permute-start.24 = (bf16[256,1024]{1,0:T(8,128)(2,1)S(1)}, bf16[256,1024]{1,0:T(8,128)(2,1)S(1)}, u32[]{:S(2)}, u32[]{:S(2)}) collective-permute-start(bf16[256,1024]{1,0:T(8,128)(2,1)S(1)} %add_convert_fusion.7), channel_id=1, source_target_pairs={{0,2},{2,4},{4,6},{10,8},{12,10},{14,12},{1,3},{3,5},{5,7},{11,9},... | collective-permute-start | bytes 1572872 | tf_op jit(solution)/shard_map/ppermute | solution.py:341
  295.0 4.4 %collective-permute-start.37 = (bf16[256,1280]{1,0:T(8,128)(2,1)S(1)}, bf16[256,1280]{1,0:T(8,128)(2,1)S(1)}, u32[]{:S(2)}, u32[]{:S(2)}) collective-permute-start(bf16[256,1280]{1,0:T(8,128)(2,1)S(1)} %add_convert_fusion.4), channel_id=1, source_target_pairs={{0,2},{2,4},{12,10},{14,12},{1,3},{3,5},{13,11},{15,13},{16,18},{1... | collective-permute-start | bytes 1966088 | tf_op jit(solution)/shard_map/ppermute | solution.py:340
  300.8 6.7 %collective-permute-done.30 = bf16[256,1280]{1,0:T(8,128)(2,1)S(1)} collective-permute-done((bf16[256,1280]{1,0:T(8,128)(2,1)S(1)}, bf16[256,1280]{1,0:T(8,128)(2,1)S(1)}, u32[]{:S(2)}, u32[]{:S(2)}) %collective-permute-start.30) | collective-permute-done | bytes 655392 | tf_op jit(solution)/shard_map/ppermute | solution.py:340
  307.8 4.4 %collective-permute-start.31 = (bf16[256,1280]{1,0:T(8,128)(2,1)S(1)}, bf16[256,1280]{1,0:T(8,128)(2,1)S(1)}, u32[]{:S(2)}, u32[]{:S(2)}) collective-permute-start(bf16[256,1280]{1,0:T(8,128)(2,1)S(1)} %add_convert_fusion.5), channel_id=1, source_target_pairs={{0,2},{2,4},{4,6},{10,8},{12,10},{14,12},{1,3},{3,5},{5,7},{11,9},... | collective-permute-start | bytes 1966088 | tf_op jit(solution)/shard_map/ppermute | solution.py:341
  314.8 4.4 %collective-permute-start.38 = (bf16[256,1280]{1,0:T(8,128)(2,1)S(1)}, bf16[256,1280]{1,0:T(8,128)(2,1)S(1)}, u32[]{:S(2)}, u32[]{:S(2)}) collective-permute-start(bf16[256,1280]{1,0:T(8,128)(2,1)S(1)} %add_convert_fusion.3), channel_id=1, source_target_pairs={{0,2},{2,4},{4,6},{10,8},{12,10},{14,12},{1,3},{3,5},{5,7},{11,9},... | collective-permute-start | bytes 1966088 | tf_op jit(solution)/shard_map/ppermute | solution.py:341
  321.9 6.7 %collective-permute-done.38 = bf16[256,1280]{1,0:T(8,128)(2,1)S(1)} collective-permute-done((bf16[256,1280]{1,0:T(8,128)(2,1)S(1)}, bf16[256,1280]{1,0:T(8,128)(2,1)S(1)}, u32[]{:S(2)}, u32[]{:S(2)}) %collective-permute-start.38) | collective-permute-done | bytes 655392 | tf_op jit(solution)/shard_map/ppermute | solution.py:341
  (123 shorter events, 84.6 us)
Async XLA Ops:
  7.3 26.9 %collective-permute-start.1 = (bf16[256,3712]{1,0:T(8,128)(2,1)S(1)}, bf16[256,3712]{1,0:T(8,128)(2,1)}, u32[]{:S(2)}, u32[]{:S(2)}) collective-permute-start(bf16[256,3712]{1,0:T(8,128)(2,1)S(1)} %pad_maximum_fusion.2), channel_id=1, source_target_pairs={{2,0},{4,2},{6,4},{8,10},{10,12},{12,14},{3,1},{5,3},{7,5},{9,11},... | collective-permute-start | bytes 5701640 | tf_op jit(solution)/shard_map/ppermute | solution.py:313
  34.1 37.5 %collective-permute-start.3 = (bf16[256,3712]{1,0:T(8,128)(2,1)}, bf16[256,3712]{1,0:T(8,128)(2,1)}, u32[]{:S(2)}, u32[]{:S(2)}) collective-permute-start(bf16[256,3712]{1,0:T(8,128)(2,1)} %collective-permute-done.1), channel_id=1, source_target_pairs={{2,0},{4,2},{10,12},{12,14},{3,1},{5,3},{11,13},{13,15},{18,16},{2... | collective-permute-start | bytes 5701640 | tf_op jit(solution)/shard_map/ppermute | solution.py:313
  37.7 92.0 %collective-permute-start.9 = (bf16[1024,512]{1,0:T(8,128)(2,1)}, bf16[1024,512]{1,0:T(8,128)(2,1)S(1)}, u32[]{:S(2)}, u32[]{:S(2)}) collective-permute-start(bf16[1024,512]{1,0:T(8,128)(2,1)} %dynamic-slice_bitcast_fusion.1), channel_id=1, source_target_pairs={{0,1},{1,0},{2,3},{3,2},{4,5},{5,4},{6,7},{7,6},{8,9},{9,8},{10,11... | collective-permute-start | bytes 3145736 | tf_op jit(solution)/shard_map/ppermute | solution.py:284
  41.3 28.4 %collective-permute-start.7 = (bf16[256,512]{1,0:T(8,128)(2,1)}, bf16[256,512]{1,0:T(8,128)(2,1)}, u32[]{:S(2)}, u32[]{:S(2)}) collective-permute-start(bf16[256,512]{1,0:T(8,128)(2,1)} %dynamic-slice_bitcast_fusion.8), channel_id=1, source_target_pairs={{0,1},{1,0},{2,3},{3,2},{4,5},{5,4},{6,7},{7,6},{8,9},{9,8},{10,11... | collective-permute-start | bytes 786440 | tf_op jit(solution)/shard_map/ppermute | solution.py:284
  43.2 45.3 %collective-permute-start.8 = (bf16[512,512]{1,0:T(8,128)(2,1)}, bf16[512,512]{1,0:T(8,128)(2,1)S(1)}, u32[]{:S(2)}, u32[]{:S(2)}) collective-permute-start(bf16[512,512]{1,0:T(8,128)(2,1)} %dynamic-slice_bitcast_fusion.6), channel_id=1, source_target_pairs={{0,1},{1,0},{2,3},{3,2},{4,5},{5,4},{6,7},{7,6},{8,9},{9,8},{10,11... | collective-permute-start | bytes 1572872 | tf_op jit(solution)/shard_map/ppermute | solution.py:284
  46.9 39.7 %collective-permute-start.15 = (bf16[256,512]{1,0:T(8,128)(2,1)}, bf16[256,512]{1,0:T(8,128)(2,1)}, u32[]{:S(2)}, u32[]{:S(2)}) collective-permute-start(bf16[256,512]{1,0:T(8,128)(2,1)} %dynamic-slice_bitcast_fusion.7), channel_id=1, source_target_pairs={{0,1},{1,0},{2,3},{3,2},{4,5},{5,4},{6,7},{7,6},{8,9},{9,8},{10,11... | collective-permute-start | bytes 786440 | tf_op jit(solution)/shard_map/ppermute | solution.py:284
  69.7 28.1 %collective-permute-start.14 = (bf16[512,512]{1,0:T(8,128)(2,1)}, bf16[512,512]{1,0:T(8,128)(2,1)}, u32[]{:S(2)}, u32[]{:S(2)}) collective-permute-start(bf16[512,512]{1,0:T(8,128)(2,1)} %dynamic-slice_bitcast_fusion.5), channel_id=1, source_target_pairs={{0,1},{1,0},{2,3},{3,2},{4,5},{5,4},{6,7},{7,6},{8,9},{9,8},{10,11... | collective-permute-start | bytes 1572872 | tf_op jit(solution)/shard_map/ppermute | solution.py:284
  71.7 117.4 %collective-permute-start.5 = (bf16[256,3712]{1,0:T(8,128)(2,1)}, bf16[256,3712]{1,0:T(8,128)(2,1)}, u32[]{:S(2)}, u32[]{:S(2)}) collective-permute-start(bf16[256,3712]{1,0:T(8,128)(2,1)} %collective-permute-done.3), channel_id=1, source_target_pairs={{2,0},{12,14},{3,1},{13,15},{18,16},{28,30},{19,17},{29,31}} | collective-permute-start | bytes 5701640 | tf_op jit(solution)/shard_map/ppermute | solution.py:313
  86.6 44.7 %collective-permute-start.13 = (bf16[1024,512]{1,0:T(8,128)(2,1)}, bf16[1024,512]{1,0:T(8,128)(2,1)}, u32[]{:S(2)}, u32[]{:S(2)}) collective-permute-start(bf16[1024,512]{1,0:T(8,128)(2,1)} %dynamic-slice_bitcast_fusion), channel_id=1, source_target_pairs={{0,1},{1,0},{2,3},{3,2},{4,5},{5,4},{6,7},{7,6},{8,9},{9,8},{10,11... | collective-permute-start | bytes 3145736 | tf_op jit(solution)/shard_map/ppermute | solution.py:284
  95.2 34.5 %collective-permute-start.19 = (bf16[512,512]{1,0:T(8,128)(2,1)S(1)}, bf16[512,512]{1,0:T(8,128)(2,1)S(1)}, u32[]{:S(2)}, u32[]{:S(2)}) collective-permute-start(bf16[512,512]{1,0:T(8,128)(2,1)S(1)} %dynamic-slice_bitcast_fusion.4), channel_id=1, source_target_pairs={{0,1},{1,0},{2,3},{3,2},{4,5},{5,4},{6,7},{7,6},{8,9},{9,8},{10,11... | collective-permute-start | bytes 1572872 | tf_op jit(solution)/shard_map/ppermute | solution.py:284
  106.2 25.6 %collective-permute-start.11 = (bf16[512,512]{1,0:T(8,128)(2,1)}, bf16[512,512]{1,0:T(8,128)(2,1)}, u32[]{:S(2)}, u32[]{:S(2)}) collective-permute-start(bf16[512,512]{1,0:T(8,128)(2,1)} %copy-done.4), channel_id=1, source_target_pairs={{0,16},{16,0},{1,17},{17,1},{2,18},{18,2},{3,19},{19,3},{4,20},{20... | collective-permute-start | bytes 1572872 | tf_op jit(solution)/shard_map/ppermute | solution.py:285
  129.7 93.2 %collective-permute-start.4 = (bf16[256,3712]{1,0:T(8,128)(2,1)}, bf16[256,3712]{1,0:T(8,128)(2,1)}, u32[]{:S(2)}, u32[]{:S(2)}) collective-permute-start(bf16[256,3712]{1,0:T(8,128)(2,1)} %collective-permute-done.3), channel_id=1, source_target_pairs={{0,8},{8,0},{1,9},{9,1},{2,10},{10,2},{3,11},{11,3},{4,12},{12,4},... | collective-permute-start | bytes 5701640 | tf_op jit(solution)/shard_map/ppermute | solution.py:273
  129.7 61.0 %collective-permute-start.12 = (bf16[1024,512]{1,0:T(8,128)(2,1)S(1)}, bf16[1024,512]{1,0:T(8,128)(2,1)}, u32[]{:S(2)}, u32[]{:S(2)}) collective-permute-start(bf16[1024,512]{1,0:T(8,128)(2,1)S(1)} %collective-permute-done.9), channel_id=1, source_target_pairs={{0,16},{16,0},{1,17},{17,1},{2,18},{18,2},{3,19},{19,3},{4,20},{20... | collective-permute-start | bytes 3145736 | tf_op jit(solution)/shard_map/ppermute | solution.py:285
  131.2 61.0 %collective-permute-start.16 = (bf16[1024,512]{1,0:T(8,128)(2,1)}, bf16[1024,512]{1,0:T(8,128)(2,1)}, u32[]{:S(2)}, u32[]{:S(2)}) collective-permute-start(bf16[1024,512]{1,0:T(8,128)(2,1)} %collective-permute-done.13), channel_id=1, source_target_pairs={{0,16},{16,0},{1,17},{17,1},{2,18},{18,2},{3,19},{19,3},{4,20},{20... | collective-permute-start | bytes 3145736 | tf_op jit(solution)/shard_map/ppermute | solution.py:285
  131.8 57.3 %collective-permute-start.17 = (bf16[512,512]{1,0:T(8,128)(2,1)}, bf16[512,512]{1,0:T(8,128)(2,1)}, u32[]{:S(2)}, u32[]{:S(2)}) collective-permute-start(bf16[512,512]{1,0:T(8,128)(2,1)} %collective-permute-done.14), channel_id=1, source_target_pairs={{0,16},{16,0},{1,17},{17,1},{2,18},{18,2},{3,19},{19,3},{4,20},{20... | collective-permute-start | bytes 1572872 | tf_op jit(solution)/shard_map/ppermute | solution.py:285
  189.1 36.1 %collective-permute-start.2 = (bf16[256,3712]{1,0:T(8,128)(2,1)}, bf16[256,3712]{1,0:T(8,128)(2,1)S(1)}, u32[]{:S(2)}, u32[]{:S(2)}) collective-permute-start(bf16[256,3712]{1,0:T(8,128)(2,1)} %collective-permute-done.1), channel_id=1, source_target_pairs={{0,8},{8,0},{1,9},{9,1},{2,10},{10,2},{3,11},{11,3},{4,12},{12,4},... | collective-permute-start | bytes 5701640 | tf_op jit(solution)/shard_map/ppermute | solution.py:273
  189.1 36.1 %collective-permute-start.6 = (bf16[256,3712]{1,0:T(8,128)(2,1)}, bf16[256,3712]{1,0:T(8,128)(2,1)S(1)}, u32[]{:S(2)}, u32[]{:S(2)}) collective-permute-start(bf16[256,3712]{1,0:T(8,128)(2,1)} %collective-permute-done.5), channel_id=1, source_target_pairs={{0,8},{8,0},{1,9},{9,1},{2,10},{10,2},{3,11},{11,3},{4,12},{12,4},... | collective-permute-start | bytes 5701640 | tf_op jit(solution)/shard_map/ppermute | solution.py:273
  192.3 29.2 %collective-permute-start.33 = (bf16[512,640]{1,0:T(8,128)(2,1)S(1)}, bf16[512,640]{1,0:T(8,128)(2,1)S(1)}, u32[]{:S(2)}, u32[]{:S(2)}) collective-permute-start(bf16[512,640]{1,0:T(8,128)(2,1)S(1)} %get-tuple-element.20), channel_id=1, source_target_pairs={{0,1},{1,0},{2,3},{3,2},{4,5},{5,4},{6,7},{7,6},{8,9},{9,8},{10,11... | collective-permute-start | bytes 1966088 | tf_op jit(solution)/shard_map/ppermute | solution.py:284
  208.3 43.9 %collective-permute-start.20 = (bf16[512,512]{1,0:T(8,128)(2,1)S(1)}, bf16[512,512]{1,0:T(8,128)(2,1)S(1)}, u32[]{:S(2)}, u32[]{:S(2)}) collective-permute-start(bf16[512,512]{1,0:T(8,128)(2,1)S(1)} %collective-permute-done.19.refs_6_), channel_id=1, source_target_pairs={{0,16},{16,0},{1,17},{17,1},{2,18},{18,2},{3,19},{19,3},{4,20},{20... | collective-permute-start | bytes 1572872 | tf_op jit(solution)/shard_map/ppermute | solution.py:285
  221.4 26.0 %collective-permute-start.27 = (bf16[512,640]{1,0:T(8,128)(2,1)S(1)}, bf16[512,640]{1,0:T(8,128)(2,1)S(1)}, u32[]{:S(2)}, u32[]{:S(2)}) collective-permute-start(bf16[512,640]{1,0:T(8,128)(2,1)S(1)} %collective-permute-done.26.refs_6_), channel_id=1, source_target_pairs={{0,16},{16,0},{1,17},{17,1},{2,18},{18,2},{3,19},{19,3},{4,20},{20... | collective-permute-start | bytes 1966088 | tf_op jit(solution)/shard_map/ppermute | solution.py:285
  222.9 33.6 %collective-permute-start.34 = (bf16[512,640]{1,0:T(8,128)(2,1)S(1)}, bf16[512,640]{1,0:T(8,128)(2,1)S(1)}, u32[]{:S(2)}, u32[]{:S(2)}) collective-permute-start(bf16[512,640]{1,0:T(8,128)(2,1)S(1)} %collective-permute-done.33.refs_6_), channel_id=1, source_target_pairs={{0,16},{16,0},{1,17},{17,1},{2,18},{18,2},{3,19},{19,3},{4,20},{20... | collective-permute-start | bytes 1966088 | tf_op jit(solution)/shard_map/ppermute | solution.py:285
  269.1 23.4 %collective-permute-start.29 = (bf16[256,1280]{1,0:T(8,128)(2,1)S(1)}, bf16[256,1280]{1,0:T(8,128)(2,1)S(1)}, u32[]{:S(2)}, u32[]{:S(2)}) collective-permute-start(bf16[256,1280]{1,0:T(8,128)(2,1)S(1)} %slice.66), channel_id=1, source_target_pairs={{0,2},{14,12},{1,3},{15,13},{16,18},{30,28},{17,19},{31,29}} | collective-permute-start | bytes 1966088 | tf_op jit(solution)/shard_map/ppermute | solution.py:339
  295.0 19.5 %collective-permute-start.37 = (bf16[256,1280]{1,0:T(8,128)(2,1)S(1)}, bf16[256,1280]{1,0:T(8,128)(2,1)S(1)}, u32[]{:S(2)}, u32[]{:S(2)}) collective-permute-start(bf16[256,1280]{1,0:T(8,128)(2,1)S(1)} %add_convert_fusion.4), channel_id=1, source_target_pairs={{0,2},{2,4},{12,10},{14,12},{1,3},{3,5},{13,11},{15,13},{16,18},{1... | collective-permute-start | bytes 1966088 | tf_op jit(solution)/shard_map/ppermute | solution.py:340
  300.7 18.5 %collective-permute-start.25 = (bf16[128,1024]{1,0:T(8,128)(2,1)S(1)}, bf16[128,1024]{1,0:T(8,128)(2,1)S(1)}, u32[]{:S(2)}, u32[]{:S(2)}) collective-permute-start(bf16[128,1024]{1,0:T(8,128)(2,1)S(1)} %select_convert_fusion.2), channel_id=1, source_target_pairs={{0,8},{8,0},{1,9},{9,1},{2,10},{10,2},{3,11},{11,3},{4,12},{12,4},... | collective-permute-start | bytes 786440 | tf_op jit(solution)/shard_map/ppermute | solution.py:273
  (24 other events, 291.4 us)

commit v3 on v2

--- a/solution.py
+++ b/solution.py
@@ -9,6 +9,10 @@
 
 TILE = 256
 LANES = 128
+STEPS = 4
+GATE_ROWS = (512, 768, 512)
+UP_ROWS = (512, 896, 384)
+DOWN_COLUMNS = (768, 1536, 1280)
 
 
 def slot_tables(routes, first_expert, expert_count, capacity, expert_total):
@@ -113,36 +117,46 @@
     return (first.astype(jnp.float32) + second.astype(jnp.float32)).astype(jnp.bfloat16)
 
 
+def after(x, *earlier):
+    return lax.optimization_barrier((x, *earlier))[0] if earlier else x
+
+
 def dot32(a, b):
     return jnp.dot(a, b, preferred_element_type=jnp.float32)
 
 
-def hidden_kernel(batches, pieces, where_ref, *refs):
+def hidden_kernel(batches, gate_pieces, up_pieces, where_ref, *refs):
     rows_refs = refs[:batches]
-    gates = refs[batches : batches + len(pieces)]
-    ups = refs[batches + len(pieces) : batches + 2 * len(pieces)]
+    gates = refs[batches : batches + len(gate_pieces)]
+    ups = refs[batches + len(gate_pieces) : -1]
     out_ref = refs[-1]
     step = pl.program_id(0)
     steps_each = pl.num_programs(0) // batches
 
+    def product(rows, pieces, weights):
+        total = None
+        for (offset, kind), w in zip(pieces, weights):
+            if kind < 0:
+                columns = slice(offset, offset + w.shape[0])
+            else:
+                columns = pl.ds(pl.multiple_of(where_ref[kind] + offset, LANES), w.shape[0])
+            value = dot32(rows[:, columns], w[...])
+            total = value if total is None else total + value
+        return total
+
     def work(rows):
-        gate_value, up_value = None, None
-        for (offset, length, kind), g, u in zip(pieces, gates, ups):
-            if kind < 0:
-                columns = slice(offset, offset + length)
-            else:
-                columns = pl.ds(pl.multiple_of(where_ref[kind] + offset, LANES), length)
-            part = rows[:, columns]
-            gate_part, up_part = dot32(part, g[...]), dot32(part, u[...])
-            gate_value = gate_part if gate_value is None else gate_value + gate_part
-            up_value = up_part if up_value is None else up_value + up_part
+        gate_value = product(rows, gate_pieces, gates)
+        up_value = product(rows, up_pieces, ups)
         out_ref[...] = (gate_value / (1.0 + jnp.exp(-gate_value)) * up_value).astype(jnp.bfloat16)
 
     for b in range(batches):
         pl.when(step // steps_each == b)(functools.partial(work, rows_refs[b]))
 
 
-def hidden_call(where, rows, pieces, gates, ups):
+def hidden_call(where, rows, gate_parts, up_parts):
+    gate_pieces, up_pieces = [p[:2] for p in gate_parts], [p[:2] for p in up_parts]
+    gates, ups = [p[2] for p in gate_parts], [p[2] for p in up_parts]
+    blocks = [(p[3], p[4]) if len(p) > 3 else (0, p[2].shape[0]) for p in gate_parts + up_parts]
     batches = len(rows)
     steps_each = rows[0].shape[0] // TILE
     width = rows[0].shape[1]
@@ -152,16 +166,22 @@
         return lambda i, w: (jnp.clip(i - b * steps_each, 0, steps_each - 1), 0)
 
     total = batches * steps_each * TILE
-    depth = sum(g.shape[0] for g in gates)
+    depth = width - LANES
     once = pl.Buffered(1)
+
+    def block_map(block):
+        return lambda i, w: (block, 0)
+
     return pl.pallas_call(
-        functools.partial(hidden_kernel, batches, pieces),
+        functools.partial(hidden_kernel, batches, gate_pieces, up_pieces),
         grid_spec=pltpu.PrefetchScalarGridSpec(
             num_scalar_prefetch=1,
             grid=(batches * steps_each,),
             in_specs=[pl.BlockSpec((TILE, width), rows_map(b)) for b in range(batches)]
-            + [pl.BlockSpec(g.shape, lambda i, w: (0, 0), pipeline_mode=once) for g in gates]
-            + [pl.BlockSpec(u.shape, lambda i, w: (0, 0), pipeline_mode=once) for u in ups],
+            + [
+                pl.BlockSpec((length, units), block_map(block), pipeline_mode=once)
+                for block, length in blocks
+            ],
             out_specs=pl.BlockSpec((TILE, units), lambda i, w: (i, 0)),
         ),
         out_shape=jax.ShapeDtypeStruct((total, units), jnp.bfloat16),
@@ -179,7 +199,6 @@
     own_refs = refs[batches : 2 * batches]
     other_ref, down_ref, near_ref, far_ref, home_ref, away_ref = refs[2 * batches :]
     step = pl.program_id(0)
-    steps_each = pl.num_programs(0) // batches
     half = width // 2
 
     def work(spread, own, out_ref):
@@ -191,8 +210,8 @@
             value = dot32(own[...], down_ref[:, source]) + dot32(other_ref[...], piece[...])
             out_ref[:, target] = (value * scale).astype(jnp.bfloat16)
 
-    for i in range(batches * steps_each if False else 4):
-        b = i * batches // 4
+    for i in range(STEPS):
+        b = i * batches // STEPS
         pl.when(step == i)(
             functools.partial(work, spread_refs[b], own_refs[b], home_ref if i == 0 else away_ref)
         )
@@ -276,83 +295,121 @@
     where = jnp.stack([part * half_depth, (1 - part) * half_depth, node * planes + plane, part])
     where = where.astype(jnp.int32)
 
-    pieces, own_pieces = [], [(0, model_width, -1)]
-    sizes = GATE_ROWS, UP_ROWS
-    near, far = ([], []), ([], [])
-
-    def fetch(piece):
-        first = lax.ppermute(piece, "local", swap_half)
-        return first, lax.ppermute(first, "parts", swap_two)
-
-    for m, (array, rows_of) in enumerate(zip((gate_local, up_local), sizes)):
-        offset = 0
-        for length in rows_of:
-            a, b = fetch(lax.dynamic_slice_in_dim(array, part * half_depth + offset, length, 0))
-            near[m].append(a)
-            far[m].append(b)
-            offset += length
-    down_near, down_far, firsts = [], [], []
-    first = 0
-    for width in DOWN_COLUMNS:
-        half = width // 2
-        a, b = fetch(lax.dynamic_slice_in_dim(down_local, first + part * half, half, 1))
-        down_near.append(a)
-        down_far.append(b)
-        firsts.append(first)
-        first += width
+    def cut(array, offset, length, dim=0):
+        begin = part * (half_depth if dim == 0 else length) + offset
+        return lax.dynamic_slice_in_dim(array, begin, length, dim)
+
+    def swap(x):
+        return lax.ppermute(x, "local", swap_half)
+
+    def relay(x):
+        return lax.ppermute(x, "parts", swap_two)
+
+    def line(x, step):
+        return lax.ppermute(x, both, line_pairs(step))
+
+    together = lax.optimization_barrier
+    g0, g1, g2 = GATE_ROWS
+    u0, u1, u2 = UP_ROWS
+    d0, d1, d2 = (w // 2 for w in DOWN_COLUMNS)
 
     table = expert_weights(expert_ids, combine_weights, expert_total)
     table = jnp.pad(table, ((0, 0), (0, LANES - expert_total)))
     mine = jnp.concatenate([tokens, table], axis=1)
+
+    gate_a = swap(cut(gate_local, 0, g0))
     theirs = across(mine)
     pair = jnp.concatenate(
         [jnp.where(node == 0, mine, theirs), jnp.where(node == 0, theirs, mine)], axis=0
     )
-    got, other = [pair], [None]
-    for step in range(1, planes):
-        got.append(lax.ppermute(got[-1], both, line_pairs(step)))
-        other.append(across(got[-1]))
-    slot1 = jnp.where(match, got[1], other[1])
-    slot2 = jnp.where(match, got[2], other[2])
+    pair, piece = together((pair, cut(gate_local, g0, g1)))
+    got1, gate_b, gate_ax = line(pair, 1), swap(piece), relay(gate_a)
+    piece = jnp.concatenate([cut(gate_local, g0 + g1, g2), cut(up_local, 0, u0)], axis=0)
+    got1, gate_b, gate_ax, piece = together((got1, gate_b, gate_ax, piece))
+    got2, both_c, gate_bx = line(got1, 2), swap(piece), relay(gate_b)
+    other1 = across(got1)
+    pieces = cut(up_local, u0, u1), cut(down_local, 0, d0, 1)
+    got2, both_c, gate_bx, other1, pieces = together((got2, both_c, gate_bx, other1, pieces))
+    got3, up_b, both_cx, down_a = line(got2, 3), swap(pieces[0]), relay(both_c), swap(pieces[1])
+    other2 = across(got2)
+    slot1 = jnp.where(match, got1, other1)
+    early = jnp.concatenate([pair, slot1], axis=0)
+    own = [(0, -1, gate_local)], [(0, -1, up_local)]
+    own_early = hidden_call(where, [early], *own)
+    rest = u0 + u1
+    piece = jnp.concatenate([up_local[rest:half_depth], up_local[half_depth + rest :]], axis=0)
+    got3, up_b, both_cx, other2, own_early, piece = together(
+        (got3, up_b, both_cx, other2, own_early, piece)
+    )
+    up_bx, up_c = relay(up_b), swap(piece)
+    other3 = across(got3)
+    slot2 = jnp.where(match, got2, other2)
     slot3 = jnp.where(
-        end, jnp.where(match, got[3], other[3]), jnp.where(match, other[1], got[1])
-    )
-    early = jnp.concatenate([pair, slot1], axis=0)
+        end,
+        jnp.where(match, got3, other3),
+        jnp.where(match, after(other1, got3), after(got1, got3)),
+    )
     late = jnp.concatenate([slot2, slot3], axis=0)
-
-    own_early = hidden_call(where, [early], own_pieces, [gate_local], [up_local])
-    own_late = hidden_call(where, [late], own_pieces, [gate_local], [up_local])
-    gates = cut_alike(near[0], far[0], sizes[0])
-    ups = cut_alike(near[1], far[1], sizes[0])
-    offset = 0
-    pieces = [(0, half_depth, 0), (0, half_depth, 1)]
-    crossed = hidden_call(where, [early, late], pieces, gates, ups)
-
-    results = []
-    for k in range(len(DOWN_COLUMNS)):
-        home, away = down_call(
-            where, [early, late], [own_early, own_late], crossed,
-            down_local, down_near[k], down_far[k], firsts[k],
+    own_late = hidden_call(where, [late], *own)
+    pieces = cut(down_local, 2 * d0, d1, 1), cut(down_local, 2 * (d0 + d1), d2, 1)
+    up_bx, up_c, down_a, own_late, pieces = together((up_bx, up_c, down_a, own_late, pieces))
+    down_ax, down_b = relay(down_a), swap(pieces[0])
+    crossed = hidden_call(
+        where, [early, late],
+        [
+            (0, 0, gate_a), (g0, 0, gate_b), (g0 + g1, 0, both_c, 0, g2),
+            (0, 1, gate_ax), (g0, 1, gate_bx), (g0 + g1, 1, both_cx, 0, g2),
+        ],
+        [
+            (0, 0, both_c, g2 // u0, u0), (u0, 0, up_b),
+            (0, 1, both_cx, g2 // u0, u0), (u0, 1, up_bx),
+            (rest, -1, up_c, 0, u2), (half_depth + rest, -1, up_c, 1, u2),
+        ],
+    )
+    down_ax, crossed, piece = together((down_ax, crossed, pieces[1]))
+
+    def expert(first, near, far, *earlier):
+        return down_call(
+            after(where, *earlier), [early, late], [own_early, own_late], crossed,
+            down_local, near, far, first,
         )
-        away = add_rounded(away, across(away))
+
+    def step(rows, moving, k):
+        rows = rows if moving is None else add_rounded(rows, moving)
+        return lax.ppermute(rows, both, back_pairs(k))
+
+    def thirds(away, arrived):
+        away = add_rounded(away, arrived)
         s1, s2, s3 = (away[i * TILE : (i + 1) * TILE] for i in range(3))
-        moving = lax.ppermute(s3, both, back_pairs(3))
-        moving = lax.ppermute(add_rounded(s2, moving), both, back_pairs(2))
-        moving = lax.ppermute(add_rounded(jnp.where(match, s1, s3), moving), both, back_pairs(1))
+        return jnp.where(match, s1, s3), s2, s3
+
+    def finish(home, moving):
         kept = moving.astype(jnp.float32) + home.astype(jnp.float32)
         low, high = kept[:token_count], kept[token_count:]
-        sent = jnp.where(node == 0, high, low).astype(jnp.bfloat16)
-        results.append((jnp.where(node == 0, low, high) + across(sent).astype(jnp.float32)).astype(jnp.bfloat16))
+        sent = across(jnp.where(node == 0, high, low).astype(jnp.bfloat16))
+        return (jnp.where(node == 0, low, high) + sent.astype(jnp.float32)).astype(jnp.bfloat16)
+
+    home_a, away_a = expert(0, down_a, down_ax)
+    down_bx = relay(down_b)
+    down_c = swap(piece)
+    a1, a2, a3 = thirds(away_a, across(after(away_a, down_b)))
+    moving_a = step(a3, None, 3)
+    moving_a = step(after(a2, down_c), moving_a, 2)
+    down_bx, down_c, a1 = together((down_bx, down_c, a1))
+    down_cx = relay(down_c)
+    home_b, away_b = expert(2 * d0, down_b, down_bx, moving_a)
+    moving_a = step(a1, moving_a, 1)
+    b1, b2, b3 = thirds(away_b, across(away_b))
+    moving_b = step(b3, None, 3)
+    home_c, away_c = expert(2 * (d0 + d1), down_c, down_cx, b3)
+    c1, c2, c3 = thirds(away_c, across(away_c))
+    moving_c = step(c3, None, 3)
+    moving_b = step(b2, moving_b, 2)
+    moving_c = step(c2, moving_c, 2)
+    moving_b = step(b1, moving_b, 1)
+    moving_c = step(c1, moving_c, 1)
+    results = [finish(home_a, moving_a), finish(home_b, moving_b), finish(home_c, moving_c)]
     return jnp.concatenate(results, axis=1)
-
-
-GATE_ROWS = (256, 512, 1024)
-UP_ROWS = (1024, 512, 256)
-DOWN_COLUMNS = (1024, 1280, 1280)
-
-
-def cut_alike(near, far, sizes):
-    return [jnp.concatenate(near, axis=0), jnp.concatenate(far, axis=0)]
 
 
 def on_device(tokens, expert_ids, combine_weights, gate_weight, up_weight, down_weight):

time: 332 us -> 265 us (0.80)
  waiting for transfers between devices: 202 us -> 130 us
  starting transfers between devices: 62.3 us -> 67.7 us
    ppermute x30 -> x27, waiting for transfers between devices: 198 us -> 123 us  [the longest x8 55.4 us: swap(): return lax.ppermute(x, 'local', swap_half)]
    dynamic_slice x8 -> x7, local copies, waits for them, and re-layouts: 14.1 us -> 8.86 us  [cut(): return lax.dynamic_slice_in_dim(array, begin, length, dim)]
    unnamed x16 -> x38, local copies, waits for them, and re-layouts: 0.04 us -> 5.29 us
    concatenate x4 -> x2, other arithmetic: 5.75 us -> 1.98 us  [the longest x1 1.04 us: line_exchange(): jnp.concatenate([cut(gate_local, g0 + g1, g2), cut(up_local, 0, u0)], axi...]
    ppermute x30 -> x27, starting transfers between devices: 60.4 us -> 63.4 us  [the longest x9 37.8 us: step(): return lax.ppermute(rows, both, back_pairs(k))]
  transfers between devices with their start and end apart: 40 -> 37, of which waited for: 20 -> 24; matrix products, arithmetic and copies ran while one was open for 9% -> 9% of each run, Pallas kernels for 10% -> 9%
where the time goes in v3:
time: 265 us
  waiting for transfers between devices  130 us (49%)
  starting transfers between devices  67.7 us (26%)
  Pallas kernels  32.2 us (12%)
  other arithmetic  19.1 us (7%)
  local copies, waits for them, and re-layouts  15.5 us (6%)
    ppermute x8, waiting for transfers between devices, swap(): return lax.ppermute(x, 'local', swap_half)  55.4 us
    ppermute x9, starting transfers between devices, step(): return lax.ppermute(rows, both, back_pairs(k))  37.8 us
    ppermute x7, waiting for transfers between devices, relay(): return lax.ppermute(x, 'parts', swap_two)  33.2 us
    ppermute x9, waiting for transfers between devices, step(): return lax.ppermute(rows, both, back_pairs(k))  32.4 us
    pallas_call x3, Pallas kernels, hidden_call(): pl.pallas_call(functools.partial(hidden_kernel, batches, gate_pieces, up_...  18.9 us
    pallas_call x3, Pallas kernels, down_call(): pl.pallas_call(functools.partial(down_kernel, batches, first, width), gri...  13.3 us
    ppermute x8, starting transfers between devices, swap(): return lax.ppermute(x, 'local', swap_half)  11.7 us
    ppermute x7, starting transfers between devices, relay(): return lax.ppermute(x, 'parts', swap_two)  9.92 us
  transfers between devices with their start and end apart: 37, of which 24 were waited for; matrix products, arithmetic and copies ran while one was open for 9% of the time, Pallas kernels for 9%

profile of v3, /device:TPU:0, one launch (start us, length us, event | category | flops | bytes accessed | tf_op | source)
XLA Modules:
  0.0 264.7 jit_solution(13095325105311394373)
XLA Ops:
  13.0 9.8 %collective-permute-done.3.refs_2_ = bf16[512,512]{1,0:T(8,128)(2,1)S(1)} collective-permute-done((bf16[512,512]{1,0:T(8,128)(2,1)S(1)}, bf16[512,512]{1,0:T(8,128)(2,1)S(1)}, u32[]{:S(2)}, u32[]{:S(2)}) %collective-permute-start.3) | collective-permute-done | bytes 524320 | tf_op jit(solution)/shard_map/ppermute | solution.py:303
  27.4 6.1 %collective-permute-done.4.refs_5_ = bf16[512,512]{1,0:T(8,128)(2,1)S(1)} collective-permute-done((bf16[512,512]{1,0:T(8,128)(2,1)S(1)}, bf16[512,512]{1,0:T(8,128)(2,1)S(1)}, u32[]{:S(2)}, u32[]{:S(2)}) %collective-permute-start.4) | collective-permute-done | bytes 524320 | tf_op jit(solution)/shard_map/ppermute | solution.py:306
  34.2 5.4 %collective-permute-done.2.refs_3_ = bf16[768,512]{1,0:T(8,128)(2,1)S(1)} collective-permute-done((bf16[768,512]{1,0:T(8,128)(2,1)S(1)}, bf16[768,512]{1,0:T(8,128)(2,1)S(1)}, u32[]{:S(2)}, u32[]{:S(2)}) %collective-permute-start.2) | collective-permute-done | bytes 786464 | tf_op jit(solution)/shard_map/ppermute | solution.py:303
  52.0 13.5 %collective-permute-done.7.refs_6_ = bf16[768,512]{1,0:T(8,128)(2,1)S(1)} collective-permute-done((bf16[768,512]{1,0:T(8,128)(2,1)S(1)}, bf16[768,512]{1,0:T(8,128)(2,1)S(1)}, u32[]{:S(2)}, u32[]{:S(2)}) %collective-permute-start.7) | collective-permute-done | bytes 786464 | tf_op jit(solution)/shard_map/ppermute | solution.py:306
  78.8 4.7 %shard_map.64.refs_2_ = bf16[512,512]{1,0:T(8,128)(2,1)S(1)} custom-call(s32[4]{0:T(128)S(1)} %pad_add_fusion.where_ref, bf16[512,3712]{1,0:T(8,128)(2,1)S(1)} %pad_maximum_fusion.refs_0_, bf16[3584,512]{1,0:T(8,128)(2,1)S(1)} %bitcast.32, bf16[3584,512]{1,0:T(8,128)(2,1)S(1)} %bitcast.30), custom_call_target="tpu_custom_call" | custom-call | flops 3758096384 | bytes 11665408 | tf_op jit(solution)/shard_map/pallas_call | solution.py:175
  83.5 12.4 %collective-permute-done.10.refs_9_ = bf16[896,512]{1,0:T(8,128)(2,1)S(1)} collective-permute-done((bf16[896,512]{1,0:T(8,128)(2,1)S(1)}, bf16[896,512]{1,0:T(8,128)(2,1)S(1)}, u32[]{:S(2)}, u32[]{:S(2)}) %collective-permute-start.10) | collective-permute-done | bytes 917536 | tf_op jit(solution)/shard_map/ppermute | solution.py:303
  112.5 4.7 %shard_map.65.refs_3_ = bf16[512,512]{1,0:T(8,128)(2,1)S(1)} custom-call(s32[4]{0:T(128)S(1)} %pad_add_fusion.where_ref, bf16[512,3712]{1,0:T(8,128)(2,1)S(1)} %pad_maximum_fusion.1.refs_0_.refs_1_, bf16[3584,512]{1,0:T(8,128)(2,1)S(1)} %bitcast.33, bf16[3584,512]{1,0:T(8,128)(2,1)S(1)} %bitcast.31), custom_call_target="tpu_custom_call" | custom-call | flops 3758096384 | bytes 11665408 | tf_op jit(solution)/shard_map/pallas_call | solution.py:175
  117.2 12.7 %collective-permute-done.14.refs_12_.refs_13_ = bf16[768,512]{1,0:T(8,128)(2,1)S(1)} collective-permute-done((bf16[768,512]{1,0:T(8,128)(2,1)S(1)}, bf16[768,512]{1,0:T(8,128)(2,1)S(1)}, u32[]{:S(2)}, u32[]{:S(2)}) %collective-permute-start.14) | collective-permute-done | bytes 786464 | tf_op jit(solution)/shard_map/ppermute | solution.py:303
  133.0 9.5 %shard_map.66.refs_4_ = bf16[1024,512]{1,0:T(8,128)(2,1)S(1)} custom-call(s32[4]{0:T(128)S(1)} %pad_add_fusion.where_ref, bf16[512,3712]{1,0:T(8,128)(2,1)S(1)} %copy-done.1, bf16[512,3712]{1,0:T(8,128)(2,1)S(1)} %pad_maximum_fusion.1.refs_0_.refs_1_, bf16[512,512]{1,0:T(8,128)(2,1)S(1)} %copy-done.12, bf16[768,512]{1,0:T(8,128)(2,1)S(1)} %copy-done.8, ...), custom_call_target="tpu_custom_call" | custom-call | flops 7516192768 | bytes 15990784 | tf_op jit(solution)/shard_map/pallas_call | solution.py:175
  153.6 5.9 %collective-permute-start.22 = (bf16[256,768]{1,0:T(8,128)(2,1)S(1)}, bf16[256,768]{1,0:T(8,128)(2,1)S(1)}, u32[]{:S(2)}, u32[]{:S(2)}) collective-permute-start(bf16[256,768]{1,0:T(8,128)(2,1)S(1)} %get-tuple-element.97), channel_id=1, source_target_pairs={{0,2},{14,12},{1,3},{15,13},{16,18},{30,28},{17,19},{31,29}} | collective-permute-start | bytes 1179656 | tf_op jit(solution)/shard_map/ppermute | solution.py:379
  160.1 7.4 %collective-permute-done.20.refs_6_ = bf16[512,640]{1,0:T(8,128)(2,1)S(1)} collective-permute-done((bf16[512,640]{1,0:T(8,128)(2,1)S(1)}, bf16[512,640]{1,0:T(8,128)(2,1)S(1)}, u32[]{:S(2)}, u32[]{:S(2)}) %collective-permute-start.20) | collective-permute-done | bytes 655392 | tf_op jit(solution)/shard_map/ppermute | solution.py:303
  167.6 5.9 %collective-permute-start.23 = (bf16[256,768]{1,0:T(8,128)(2,1)S(1)}, bf16[256,768]{1,0:T(8,128)(2,1)S(1)}, u32[]{:S(2)}, u32[]{:S(2)}) collective-permute-start(bf16[256,768]{1,0:T(8,128)(2,1)S(1)} %add_convert_fusion.9), channel_id=1, source_target_pairs={{0,2},{2,4},{12,10},{14,12},{1,3},{3,5},{13,11},{15,13},{16,18},{1... | collective-permute-start | bytes 1179656 | tf_op jit(solution)/shard_map/ppermute | solution.py:379
  173.9 4.8 %collective-permute-done.23 = bf16[256,768]{1,0:T(8,128)(2,1)S(1)} collective-permute-done((bf16[256,768]{1,0:T(8,128)(2,1)S(1)}, bf16[256,768]{1,0:T(8,128)(2,1)S(1)}, u32[]{:S(2)}, u32[]{:S(2)}) %collective-permute-start.23) | collective-permute-done | bytes 393248 | tf_op jit(solution)/shard_map/ppermute | solution.py:379
  178.7 4.8 %shard_map.68 = (bf16[256,1536]{1,0:T(8,128)(2,1)S(1)}, bf16[768,1536]{1,0:T(8,128)(2,1)S(1)}) custom-call(s32[4]{0:T(128)S(1)} %pad_add_fusion.where_ref, bf16[512,3712]{1,0:T(8,128)(2,1)S(1)} %copy-done.1, bf16[512,3712]{1,0:T(8,128)(2,1)S(1)} %pad_maximum_fusion.1.refs_0_.refs_1_, bf16[512,512]{1,0:T(8,128)(2,1)S(1)} %shard_map.64.refs_2_, ...), custom_call_target="tpu_custom_call" | custom-call | flops 3221225472 | bytes 8388608 | tf_op jit(solution)/shard_map/pallas_call | solution.py:232
  188.8 11.9 %collective-permute-done.31.refs_7_ = bf16[512,640]{1,0:T(8,128)(2,1)S(1)} collective-permute-done((bf16[512,640]{1,0:T(8,128)(2,1)S(1)}, bf16[512,640]{1,0:T(8,128)(2,1)S(1)}, u32[]{:S(2)}, u32[]{:S(2)}) %collective-permute-start.31) | collective-permute-done | bytes 655392 | tf_op jit(solution)/shard_map/ppermute | solution.py:306
  200.8 4.8 %shard_map.69 = (bf16[256,1280]{1,0:T(8,128)(2,1)S(1)}, bf16[768,1280]{1,0:T(8,128)(2,1)S(1)}) custom-call(s32[4]{0:T(128)S(1)} %pad_add_fusion.where_ref, bf16[512,3712]{1,0:T(8,128)(2,1)S(1)} %copy-done.1, bf16[512,3712]{1,0:T(8,128)(2,1)S(1)} %pad_maximum_fusion.1.refs_0_.refs_1_, bf16[512,512]{1,0:T(8,128)(2,1)S(1)} %shard_map.64.refs_2_, ...), custom_call_target="tpu_custom_call" | custom-call | flops 2684354560 | bytes 7340032 | tf_op jit(solution)/shard_map/pallas_call | solution.py:232
  205.6 4.4 %collective-permute-start.27 = (bf16[256,1536]{1,0:T(8,128)(2,1)S(1)}, bf16[256,1536]{1,0:T(8,128)(2,1)S(1)}, u32[]{:S(2)}, u32[]{:S(2)}) collective-permute-start(bf16[256,1536]{1,0:T(8,128)(2,1)S(1)} %slice.82), channel_id=1, source_target_pairs={{0,2},{14,12},{1,3},{15,13},{16,18},{30,28},{17,19},{31,29}} | collective-permute-start | bytes 2359304 | tf_op jit(solution)/shard_map/ppermute | solution.py:379
  214.7 4.8 %collective-permute-done.27 = bf16[256,1536]{1,0:T(8,128)(2,1)S(1)} collective-permute-done((bf16[256,1536]{1,0:T(8,128)(2,1)S(1)}, bf16[256,1536]{1,0:T(8,128)(2,1)S(1)}, u32[]{:S(2)}, u32[]{:S(2)}) %collective-permute-start.27) | collective-permute-done | bytes 786464 | tf_op jit(solution)/shard_map/ppermute | solution.py:379
  219.7 4.4 %collective-permute-start.28 = (bf16[256,1536]{1,0:T(8,128)(2,1)S(1)}, bf16[256,1536]{1,0:T(8,128)(2,1)S(1)}, u32[]{:S(2)}, u32[]{:S(2)}) collective-permute-start(bf16[256,1536]{1,0:T(8,128)(2,1)S(1)} %add_convert_fusion.4), channel_id=1, source_target_pairs={{0,2},{2,4},{12,10},{14,12},{1,3},{3,5},{13,11},{15,13},{16,18},{1... | collective-permute-start | bytes 2359304 | tf_op jit(solution)/shard_map/ppermute | solution.py:379
  224.4 6.4 %collective-permute-done.33 = bf16[256,1280]{1,0:T(8,128)(2,1)S(1)} collective-permute-done((bf16[256,1280]{1,0:T(8,128)(2,1)S(1)}, bf16[256,1280]{1,0:T(8,128)(2,1)S(1)}, u32[]{:S(2)}, u32[]{:S(2)}) %collective-permute-start.33) | collective-permute-done | bytes 655392 | tf_op jit(solution)/shard_map/ppermute | solution.py:379
  230.9 4.4 %collective-permute-start.34 = (bf16[256,1280]{1,0:T(8,128)(2,1)S(1)}, bf16[256,1280]{1,0:T(8,128)(2,1)S(1)}, u32[]{:S(2)}, u32[]{:S(2)}) collective-permute-start(bf16[256,1280]{1,0:T(8,128)(2,1)S(1)} %add_convert_fusion.6), channel_id=1, source_target_pairs={{0,2},{2,4},{12,10},{14,12},{1,3},{3,5},{13,11},{15,13},{16,18},{1... | collective-permute-start | bytes 1966088 | tf_op jit(solution)/shard_map/ppermute | solution.py:379
  239.5 4.4 %collective-permute-start.29 = (bf16[256,1536]{1,0:T(8,128)(2,1)S(1)}, bf16[256,1536]{1,0:T(8,128)(2,1)S(1)}, u32[]{:S(2)}, u32[]{:S(2)}) collective-permute-start(bf16[256,1536]{1,0:T(8,128)(2,1)S(1)} %add_convert_fusion.3), channel_id=1, source_target_pairs={{0,2},{2,4},{4,6},{10,8},{12,10},{14,12},{1,3},{3,5},{5,7},{11,9},... | collective-permute-start | bytes 2359304 | tf_op jit(solution)/shard_map/ppermute | solution.py:379
  246.5 4.4 %collective-permute-start.35 = (bf16[256,1280]{1,0:T(8,128)(2,1)S(1)}, bf16[256,1280]{1,0:T(8,128)(2,1)S(1)}, u32[]{:S(2)}, u32[]{:S(2)}) collective-permute-start(bf16[256,1280]{1,0:T(8,128)(2,1)S(1)} %add_convert_fusion.5), channel_id=1, source_target_pairs={{0,2},{2,4},{4,6},{10,8},{12,10},{14,12},{1,3},{3,5},{5,7},{11,9},... | collective-permute-start | bytes 1966088 | tf_op jit(solution)/shard_map/ppermute | solution.py:379
  255.0 6.6 %collective-permute-done.35 = bf16[256,1280]{1,0:T(8,128)(2,1)S(1)} collective-permute-done((bf16[256,1280]{1,0:T(8,128)(2,1)S(1)}, bf16[256,1280]{1,0:T(8,128)(2,1)S(1)}, u32[]{:S(2)}, u32[]{:S(2)}) %collective-permute-start.35) | collective-permute-done | bytes 655392 | tf_op jit(solution)/shard_map/ppermute | solution.py:379
  (138 shorter events, 99.8 us)
Async XLA Ops:
  7.2 32.4 %collective-permute-start.1 = (bf16[256,3712]{1,0:T(8,128)(2,1)}, bf16[256,3712]{1,0:T(8,128)(2,1)}, u32[]{:S(2)}, u32[]{:S(2)}) collective-permute-start(bf16[256,3712]{1,0:T(8,128)(2,1)} %pad_maximum_fusion.2), channel_id=1, source_target_pairs={{2,0},{4,2},{6,4},{8,10},{10,12},{12,14},{3,1},{5,3},{7,5},{9,11},... | collective-permute-start | bytes 5701640 | tf_op jit(solution)/shard_map/ppermute | solution.py:309
  12.9 26.8 %collective-permute-start.2 = (bf16[768,512]{1,0:T(8,128)(2,1)S(1)}, bf16[768,512]{1,0:T(8,128)(2,1)S(1)}, u32[]{:S(2)}, u32[]{:S(2)}) collective-permute-start(bf16[768,512]{1,0:T(8,128)(2,1)S(1)} %copy-done.17), channel_id=1, source_target_pairs={{0,1},{1,0},{2,3},{3,2},{4,5},{5,4},{6,7},{7,6},{8,9},{9,8},{10,11... | collective-permute-start | bytes 2359304 | tf_op jit(solution)/shard_map/ppermute | solution.py:303
  39.6 30.2 %collective-permute-start.5 = (bf16[256,3712]{1,0:T(8,128)(2,1)}, bf16[256,3712]{1,0:T(8,128)(2,1)}, u32[]{:S(2)}, u32[]{:S(2)}) collective-permute-start(bf16[256,3712]{1,0:T(8,128)(2,1)} %collective-permute-done.1), channel_id=1, source_target_pairs={{2,0},{4,2},{10,12},{12,14},{3,1},{5,3},{11,13},{13,15},{18,16},{2... | collective-permute-start | bytes 5701640 | tf_op jit(solution)/shard_map/ppermute | solution.py:309
  40.9 28.9 %collective-permute-start.8 = (bf16[256,3712]{1,0:T(8,128)(2,1)}, bf16[256,3712]{1,0:T(8,128)(2,1)}, u32[]{:S(2)}, u32[]{:S(2)}) collective-permute-start(bf16[256,3712]{1,0:T(8,128)(2,1)} %collective-permute-done.1), channel_id=1, source_target_pairs={{0,8},{8,0},{1,9},{9,1},{2,10},{10,2},{3,11},{11,3},{4,12},{12,4},... | collective-permute-start | bytes 5701640 | tf_op jit(solution)/shard_map/ppermute | solution.py:292
  44.3 25.6 %collective-permute-start.6 = (bf16[1024,512]{1,0:T(8,128)(2,1)}, bf16[1024,512]{1,0:T(8,128)(2,1)S(1)}, u32[]{:S(2)}, u32[]{:S(2)}) collective-permute-start(bf16[1024,512]{1,0:T(8,128)(2,1)} %pad_maximum_fusion.3), channel_id=1, source_target_pairs={{0,1},{1,0},{2,3},{3,2},{4,5},{5,4},{6,7},{7,6},{8,9},{9,8},{10,11... | collective-permute-start | bytes 3145736 | tf_op jit(solution)/shard_map/ppermute | solution.py:303
  46.3 19.2 %collective-permute-start.7 = (bf16[768,512]{1,0:T(8,128)(2,1)S(1)}, bf16[768,512]{1,0:T(8,128)(2,1)S(1)}, u32[]{:S(2)}, u32[]{:S(2)}) collective-permute-start(bf16[768,512]{1,0:T(8,128)(2,1)S(1)} %collective-permute-done.2.refs_3_), channel_id=1, source_target_pairs={{0,16},{16,0},{1,17},{17,1},{2,18},{18,2},{3,19},{19,3},{4,20},{20... | collective-permute-start | bytes 2359304 | tf_op jit(solution)/shard_map/ppermute | solution.py:306
  69.9 27.3 %collective-permute-start.12 = (bf16[256,3712]{1,0:T(8,128)(2,1)}, bf16[256,3712]{1,0:T(8,128)(2,1)}, u32[]{:S(2)}, u32[]{:S(2)}) collective-permute-start(bf16[256,3712]{1,0:T(8,128)(2,1)} %collective-permute-done.5), channel_id=1, source_target_pairs={{0,8},{8,0},{1,9},{9,1},{2,10},{10,2},{3,11},{11,3},{4,12},{12,4},... | collective-permute-start | bytes 5701640 | tf_op jit(solution)/shard_map/ppermute | solution.py:292
  69.9 29.2 %collective-permute-start.9 = (bf16[256,3712]{1,0:T(8,128)(2,1)}, bf16[256,3712]{1,0:T(8,128)(2,1)}, u32[]{:S(2)}, u32[]{:S(2)}) collective-permute-start(bf16[256,3712]{1,0:T(8,128)(2,1)} %collective-permute-done.5), channel_id=1, source_target_pairs={{2,0},{12,14},{3,1},{13,15},{18,16},{28,30},{19,17},{29,31}} | collective-permute-start | bytes 5701640 | tf_op jit(solution)/shard_map/ppermute | solution.py:309
  71.2 26.0 %collective-permute-start.11 = (bf16[1024,512]{1,0:T(8,128)(2,1)S(1)}, bf16[1024,512]{1,0:T(8,128)(2,1)S(1)}, u32[]{:S(2)}, u32[]{:S(2)}) collective-permute-start(bf16[1024,512]{1,0:T(8,128)(2,1)S(1)} %collective-permute-done.6.refs_4_.refs_8_), channel_id=1, source_target_pairs={{0,16},{16,0},{1,17},{17,1},{2,18},{18,2},{3,19},{19,3},{4,20},{20... | collective-permute-start | bytes 3145736 | tf_op jit(solution)/shard_map/ppermute | solution.py:306
  73.0 23.0 %collective-permute-start.10 = (bf16[896,512]{1,0:T(8,128)(2,1)S(1)}, bf16[896,512]{1,0:T(8,128)(2,1)S(1)}, u32[]{:S(2)}, u32[]{:S(2)}) collective-permute-start(bf16[896,512]{1,0:T(8,128)(2,1)S(1)} %dynamic-slice_bitcast_fusion), channel_id=1, source_target_pairs={{0,1},{1,0},{2,3},{3,2},{4,5},{5,4},{6,7},{7,6},{8,9},{9,8},{10,11... | collective-permute-start | bytes 2752520 | tf_op jit(solution)/shard_map/ppermute | solution.py:303
  101.5 15.7 %collective-permute-start.15 = (bf16[512,384]{1,0:T(8,128)(2,1)S(1)}, bf16[512,384]{1,0:T(8,128)(2,1)S(1)}, u32[]{:S(2)}, u32[]{:S(2)}) collective-permute-start(bf16[512,384]{1,0:T(8,128)(2,1)S(1)} %copy-done.18), channel_id=1, source_target_pairs={{0,1},{1,0},{2,3},{3,2},{4,5},{5,4},{6,7},{7,6},{8,9},{9,8},{10,11... | collective-permute-start | bytes 1179656 | tf_op jit(solution)/shard_map/ppermute | solution.py:303
  103.1 26.9 %collective-permute-start.13 = (bf16[896,512]{1,0:T(8,128)(2,1)S(1)}, bf16[896,512]{1,0:T(8,128)(2,1)S(1)}, u32[]{:S(2)}, u32[]{:S(2)}) collective-permute-start(bf16[896,512]{1,0:T(8,128)(2,1)S(1)} %collective-permute-done.10.refs_9_), channel_id=1, source_target_pairs={{0,16},{16,0},{1,17},{17,1},{2,18},{18,2},{3,19},{19,3},{4,20},{20... | collective-permute-start | bytes 2752520 | tf_op jit(solution)/shard_map/ppermute | solution.py:306
  104.6 25.4 %collective-permute-start.14 = (bf16[768,512]{1,0:T(8,128)(2,1)S(1)}, bf16[768,512]{1,0:T(8,128)(2,1)S(1)}, u32[]{:S(2)}, u32[]{:S(2)}) collective-permute-start(bf16[768,512]{1,0:T(8,128)(2,1)S(1)} %copy-done.16), channel_id=1, source_target_pairs={{0,1},{1,0},{2,3},{3,2},{4,5},{5,4},{6,7},{7,6},{8,9},{9,8},{10,11... | collective-permute-start | bytes 2359304 | tf_op jit(solution)/shard_map/ppermute | solution.py:303
  131.5 18.9 %collective-permute-start.17 = (bf16[512,768]{1,0:T(8,128)(2,1)S(1)}, bf16[512,768]{1,0:T(8,128)(2,1)S(1)}, u32[]{:S(2)}, u32[]{:S(2)}) collective-permute-start(bf16[512,768]{1,0:T(8,128)(2,1)S(1)} %dynamic-slice_bitcast_fusion.1), channel_id=1, source_target_pairs={{0,1},{1,0},{2,3},{3,2},{4,5},{5,4},{6,7},{7,6},{8,9},{9,8},{10,11... | collective-permute-start | bytes 2359304 | tf_op jit(solution)/shard_map/ppermute | solution.py:303
  150.4 17.1 %collective-permute-start.20 = (bf16[512,640]{1,0:T(8,128)(2,1)S(1)}, bf16[512,640]{1,0:T(8,128)(2,1)S(1)}, u32[]{:S(2)}, u32[]{:S(2)}) collective-permute-start(bf16[512,640]{1,0:T(8,128)(2,1)S(1)} %dynamic-slice_bitcast_fusion.3), channel_id=1, source_target_pairs={{0,1},{1,0},{2,3},{3,2},{4,5},{5,4},{6,7},{7,6},{8,9},{9,8},{10,11... | collective-permute-start | bytes 1966088 | tf_op jit(solution)/shard_map/ppermute | solution.py:303
  159.5 14.5 %collective-permute-start.18 = (bf16[512,768]{1,0:T(8,128)(2,1)S(1)}, bf16[512,768]{1,0:T(8,128)(2,1)S(1)}, u32[]{:S(2)}, u32[]{:S(2)}) collective-permute-start(bf16[512,768]{1,0:T(8,128)(2,1)S(1)} %collective-permute-done.17.refs_6_), channel_id=1, source_target_pairs={{0,16},{16,0},{1,17},{17,1},{2,18},{18,2},{3,19},{19,3},{4,20},{20... | collective-permute-start | bytes 2359304 | tf_op jit(solution)/shard_map/ppermute | solution.py:306
  183.6 17.1 %collective-permute-start.31 = (bf16[512,640]{1,0:T(8,128)(2,1)S(1)}, bf16[512,640]{1,0:T(8,128)(2,1)S(1)}, u32[]{:S(2)}, u32[]{:S(2)}) collective-permute-start(bf16[512,640]{1,0:T(8,128)(2,1)S(1)} %collective-permute-done.20.refs_6_), channel_id=1, source_target_pairs={{0,16},{16,0},{1,17},{17,1},{2,18},{18,2},{3,19},{19,3},{4,20},{20... | collective-permute-start | bytes 1966088 | tf_op jit(solution)/shard_map/ppermute | solution.py:306
  210.2 14.0 %collective-permute-start.24 = (bf16[256,768]{1,0:T(8,128)(2,1)S(1)}, bf16[256,768]{1,0:T(8,128)(2,1)S(1)}, u32[]{:S(2)}, u32[]{:S(2)}) collective-permute-start(bf16[256,768]{1,0:T(8,128)(2,1)S(1)} %add_convert_fusion.8), channel_id=1, source_target_pairs={{0,2},{2,4},{4,6},{10,8},{12,10},{14,12},{1,3},{3,5},{5,7},{11,9},... | collective-permute-start | bytes 1179656 | tf_op jit(solution)/shard_map/ppermute | solution.py:379
  212.1 18.7 %collective-permute-start.33 = (bf16[256,1280]{1,0:T(8,128)(2,1)S(1)}, bf16[256,1280]{1,0:T(8,128)(2,1)S(1)}, u32[]{:S(2)}, u32[]{:S(2)}) collective-permute-start(bf16[256,1280]{1,0:T(8,128)(2,1)S(1)} %slice.87), channel_id=1, source_target_pairs={{0,2},{14,12},{1,3},{15,13},{16,18},{30,28},{17,19},{31,29}} | collective-permute-start | bytes 1966088 | tf_op jit(solution)/shard_map/ppermute | solution.py:379
  219.7 19.5 %collective-permute-start.28 = (bf16[256,1536]{1,0:T(8,128)(2,1)S(1)}, bf16[256,1536]{1,0:T(8,128)(2,1)S(1)}, u32[]{:S(2)}, u32[]{:S(2)}) collective-permute-start(bf16[256,1536]{1,0:T(8,128)(2,1)S(1)} %add_convert_fusion.4), channel_id=1, source_target_pairs={{0,2},{2,4},{12,10},{14,12},{1,3},{3,5},{13,11},{15,13},{16,18},{1... | collective-permute-start | bytes 2359304 | tf_op jit(solution)/shard_map/ppermute | solution.py:379
  224.3 19.6 %collective-permute-start.25 = (bf16[128,768]{1,0:T(8,128)(2,1)S(1)}, bf16[128,768]{1,0:T(8,128)(2,1)S(1)}, u32[]{:S(2)}, u32[]{:S(2)}) collective-permute-start(bf16[128,768]{1,0:T(8,128)(2,1)S(1)} %select_convert_fusion.2), channel_id=1, source_target_pairs={{0,8},{8,0},{1,9},{9,1},{2,10},{10,2},{3,11},{11,3},{4,12},{12,4},... | collective-permute-start | bytes 589832 | tf_op jit(solution)/shard_map/ppermute | solution.py:292
  230.9 15.3 %collective-permute-start.34 = (bf16[256,1280]{1,0:T(8,128)(2,1)S(1)}, bf16[256,1280]{1,0:T(8,128)(2,1)S(1)}, u32[]{:S(2)}, u32[]{:S(2)}) collective-permute-start(bf16[256,1280]{1,0:T(8,128)(2,1)S(1)} %add_convert_fusion.6), channel_id=1, source_target_pairs={{0,2},{2,4},{12,10},{14,12},{1,3},{3,5},{13,11},{15,13},{16,18},{1... | collective-permute-start | bytes 1966088 | tf_op jit(solution)/shard_map/ppermute | solution.py:379
  239.5 15.2 %collective-permute-start.29 = (bf16[256,1536]{1,0:T(8,128)(2,1)S(1)}, bf16[256,1536]{1,0:T(8,128)(2,1)S(1)}, u32[]{:S(2)}, u32[]{:S(2)}) collective-permute-start(bf16[256,1536]{1,0:T(8,128)(2,1)S(1)} %add_convert_fusion.3), channel_id=1, source_target_pairs={{0,2},{2,4},{4,6},{10,8},{12,10},{14,12},{1,3},{3,5},{5,7},{11,9},... | collective-permute-start | bytes 2359304 | tf_op jit(solution)/shard_map/ppermute | solution.py:379
  246.5 15.2 %collective-permute-start.35 = (bf16[256,1280]{1,0:T(8,128)(2,1)S(1)}, bf16[256,1280]{1,0:T(8,128)(2,1)S(1)}, u32[]{:S(2)}, u32[]{:S(2)}) collective-permute-start(bf16[256,1280]{1,0:T(8,128)(2,1)S(1)} %add_convert_fusion.5), channel_id=1, source_target_pairs={{0,2},{2,4},{4,6},{10,8},{12,10},{14,12},{1,3},{3,5},{5,7},{11,9},... | collective-permute-start | bytes 1966088 | tf_op jit(solution)/shard_map/ppermute | solution.py:379
  (32 other events, 291.6 us)

commit v4 on v3

--- a/solution.py
+++ b/solution.py
@@ -12,7 +12,7 @@
 STEPS = 4
 GATE_ROWS = (512, 768, 512)
 UP_ROWS = (512, 896, 384)
-DOWN_COLUMNS = (768, 1536, 1280)
+DOWN_COLUMNS = (1024, 1536, 1024)
 
 
 def slot_tables(routes, first_expert, expert_count, capacity, expert_total):
@@ -330,18 +330,18 @@
     other1 = across(got1)
     pieces = cut(up_local, u0, u1), cut(down_local, 0, d0, 1)
     got2, both_c, gate_bx, other1, pieces = together((got2, both_c, gate_bx, other1, pieces))
-    got3, up_b, both_cx, down_a = line(got2, 3), swap(pieces[0]), relay(both_c), swap(pieces[1])
+    got3, up_b, both_cx = line(got2, 3), swap(pieces[0]), relay(both_c)
     other2 = across(got2)
     slot1 = jnp.where(match, got1, other1)
     early = jnp.concatenate([pair, slot1], axis=0)
     own = [(0, -1, gate_local)], [(0, -1, up_local)]
     own_early = hidden_call(where, [early], *own)
     rest = u0 + u1
-    piece = jnp.concatenate([up_local[rest:half_depth], up_local[half_depth + rest :]], axis=0)
-    got3, up_b, both_cx, other2, own_early, piece = together(
-        (got3, up_b, both_cx, other2, own_early, piece)
-    )
-    up_bx, up_c = relay(up_b), swap(piece)
+    pieces = cut(up_local, rest, u2), pieces[1]
+    got3, up_b, both_cx, other2, own_early, pieces = together(
+        (got3, up_b, both_cx, other2, own_early, pieces)
+    )
+    up_bx, up_c, down_a = relay(up_b), swap(pieces[0]), swap(pieces[1])
     other3 = across(got3)
     slot2 = jnp.where(match, got2, other2)
     slot3 = jnp.where(
@@ -353,20 +353,21 @@
     own_late = hidden_call(where, [late], *own)
     pieces = cut(down_local, 2 * d0, d1, 1), cut(down_local, 2 * (d0 + d1), d2, 1)
     up_bx, up_c, down_a, own_late, pieces = together((up_bx, up_c, down_a, own_late, pieces))
-    down_ax, down_b = relay(down_a), swap(pieces[0])
+    up_cx, down_b = relay(up_c), swap(pieces[0])
+    up_cx, down_a = together((up_cx, down_a))
+    down_ax = relay(down_a)
     crossed = hidden_call(
-        where, [early, late],
+        after(where, up_cx), [early, late],
         [
             (0, 0, gate_a), (g0, 0, gate_b), (g0 + g1, 0, both_c, 0, g2),
             (0, 1, gate_ax), (g0, 1, gate_bx), (g0 + g1, 1, both_cx, 0, g2),
         ],
         [
-            (0, 0, both_c, g2 // u0, u0), (u0, 0, up_b),
-            (0, 1, both_cx, g2 // u0, u0), (u0, 1, up_bx),
-            (rest, -1, up_c, 0, u2), (half_depth + rest, -1, up_c, 1, u2),
+            (0, 0, both_c, g2 // u0, u0), (u0, 0, up_b), (rest, 0, up_c),
+            (0, 1, both_cx, g2 // u0, u0), (u0, 1, up_bx), (rest, 1, up_cx),
         ],
     )
-    down_ax, crossed, piece = together((down_ax, crossed, pieces[1]))
+    down_ax, down_b, crossed, piece = together((down_ax, down_b, crossed, pieces[1]))
 
     def expert(first, near, far, *earlier):
         return down_call(
@@ -389,24 +390,22 @@
         sent = across(jnp.where(node == 0, high, low).astype(jnp.bfloat16))
         return (jnp.where(node == 0, low, high) + sent.astype(jnp.float32)).astype(jnp.bfloat16)
 
+    down_bx, down_c = relay(down_b), swap(piece)
     home_a, away_a = expert(0, down_a, down_ax)
-    down_bx = relay(down_b)
-    down_c = swap(piece)
-    a1, a2, a3 = thirds(away_a, across(after(away_a, down_b)))
-    moving_a = step(a3, None, 3)
-    moving_a = step(after(a2, down_c), moving_a, 2)
-    down_bx, down_c, a1 = together((down_bx, down_c, a1))
+    a1, a2, a3 = thirds(away_a, across(away_a))
+    moving_a = step(after(a3, down_c), None, 3)
+    home_b, away_b = expert(2 * d0, down_b, down_bx, moving_a, down_c)
     down_cx = relay(down_c)
-    home_b, away_b = expert(2 * d0, down_b, down_bx, moving_a)
+    moving_a = step(after(a2, down_bx), moving_a, 2)
+    b1, b2, b3 = thirds(away_b, across(after(away_b, moving_a, down_cx)))
     moving_a = step(a1, moving_a, 1)
-    b1, b2, b3 = thirds(away_b, across(away_b))
     moving_b = step(b3, None, 3)
     home_c, away_c = expert(2 * (d0 + d1), down_c, down_cx, b3)
-    c1, c2, c3 = thirds(away_c, across(away_c))
+    c1, c2, c3 = thirds(away_c, across(after(away_c, moving_a)))
+    moving_b = step(b2, moving_b, 2)
     moving_c = step(c3, None, 3)
-    moving_b = step(b2, moving_b, 2)
+    moving_b = step(b1, moving_b, 1)
     moving_c = step(c2, moving_c, 2)
-    moving_b = step(b1, moving_b, 1)
     moving_c = step(c1, moving_c, 1)
     results = [finish(home_a, moving_a), finish(home_b, moving_b), finish(home_c, moving_c)]
     return jnp.concatenate(results, axis=1)

time: 265 us -> 258 us (0.974)
  waiting for transfers between devices: 130 us -> 119 us
  local copies, waits for them, and re-layouts: 15.5 us -> 18.9 us
    ppermute x8, waiting for transfers between devices: 55.4 us -> 47.6 us  [swap(): return lax.ppermute(x, 'local', swap_half)]
    ppermute x7 -> x8, waiting for transfers between devices: 33.2 us -> 30.2 us  [relay(): return lax.ppermute(x, 'parts', swap_two)]
    unnamed x38 -> x36, local copies, waits for them, and re-layouts: 5.29 us -> 7.76 us
    ppermute x7 -> x8, starting transfers between devices: 9.92 us -> 10.5 us  [relay(): return lax.ppermute(x, 'parts', swap_two)]
  transfers between devices with their start and end apart: 37 -> 38, of which waited for: 24 -> 23; matrix products, arithmetic and copies ran while one was open for 9% -> 10% of each run, Pallas kernels for 9% -> 11%
where the time goes in v4:
time: 258 us; the launch traced here: 257 us
  waiting for transfers between devices  119 us (46%)
  starting transfers between devices  69.1 us (27%)
  Pallas kernels  31.1 us (12%)
  other arithmetic  19.1 us (7%)
  local copies, waits for them, and re-layouts  18.9 us (7%)
    ppermute x8, waiting for transfers between devices, swap(): return lax.ppermute(x, 'local', swap_half)  47.6 us
    ppermute x9, starting transfers between devices, step(): return lax.ppermute(rows, both, back_pairs(k))  38.7 us
    ppermute x9, waiting for transfers between devices, step(): return lax.ppermute(rows, both, back_pairs(k))  34.6 us
    ppermute x8, waiting for transfers between devices, relay(): return lax.ppermute(x, 'parts', swap_two)  30.2 us
    pallas_call x3, Pallas kernels, hidden_call(): pl.pallas_call(functools.partial(hidden_kernel, batches, gate_pieces, up_...  18.9 us
    pallas_call x3, Pallas kernels, down_call(): pl.pallas_call(functools.partial(down_kernel, batches, first, width), gri...  12.2 us
    ppermute x8, starting transfers between devices, swap(): return lax.ppermute(x, 'local', swap_half)  11.6 us
    dynamic_slice x7, local copies, waits for them, and re-layouts, cut(): return lax.dynamic_slice_in_dim(array, begin, length, dim)  10.9 us
  transfers between devices with their start and end apart: 38, of which 23 were waited for; matrix products, arithmetic and copies ran while one was open for 10% of the time, Pallas kernels for 11%

profile of v4, /device:TPU:0, one launch (start us, length us, event | category | flops | bytes accessed | tf_op | source)
XLA Modules:
  0.0 257.3 jit_solution(4237931999580929391)
XLA Ops:
  13.0 9.8 %collective-permute-done.3.refs_2_ = bf16[512,512]{1,0:T(8,128)(2,1)S(1)} collective-permute-done((bf16[512,512]{1,0:T(8,128)(2,1)S(1)}, bf16[512,512]{1,0:T(8,128)(2,1)S(1)}, u32[]{:S(2)}, u32[]{:S(2)}) %collective-permute-start.3) | collective-permute-done | bytes 524320 | tf_op jit(solution)/shard_map/ppermute | solution.py:303
  27.4 6.1 %collective-permute-done.4.refs_5_ = bf16[512,512]{1,0:T(8,128)(2,1)S(1)} collective-permute-done((bf16[512,512]{1,0:T(8,128)(2,1)S(1)}, bf16[512,512]{1,0:T(8,128)(2,1)S(1)}, u32[]{:S(2)}, u32[]{:S(2)}) %collective-permute-start.4) | collective-permute-done | bytes 524320 | tf_op jit(solution)/shard_map/ppermute | solution.py:306
  34.2 5.4 %collective-permute-done.2.refs_3_ = bf16[768,512]{1,0:T(8,128)(2,1)S(1)} collective-permute-done((bf16[768,512]{1,0:T(8,128)(2,1)S(1)}, bf16[768,512]{1,0:T(8,128)(2,1)S(1)}, u32[]{:S(2)}, u32[]{:S(2)}) %collective-permute-start.2) | collective-permute-done | bytes 786464 | tf_op jit(solution)/shard_map/ppermute | solution.py:303
  53.2 12.3 %collective-permute-done.7.refs_6_ = bf16[768,512]{1,0:T(8,128)(2,1)S(1)} collective-permute-done((bf16[768,512]{1,0:T(8,128)(2,1)S(1)}, bf16[768,512]{1,0:T(8,128)(2,1)S(1)}, u32[]{:S(2)}, u32[]{:S(2)}) %collective-permute-start.7) | collective-permute-done | bytes 786464 | tf_op jit(solution)/shard_map/ppermute | solution.py:306
  81.3 4.7 %shard_map.64.refs_2_ = bf16[512,512]{1,0:T(8,128)(2,1)S(1)} custom-call(s32[4]{0:T(128)S(1)} %pad_add_fusion.where_ref, bf16[512,3712]{1,0:T(8,128)(2,1)S(1)} %pad_maximum_fusion.refs_0_, bf16[3584,512]{1,0:T(8,128)(2,1)S(1)} %bitcast.28, bf16[3584,512]{1,0:T(8,128)(2,1)S(1)} %bitcast.30), custom_call_target="tpu_custom_call" | custom-call | flops 3758096384 | bytes 11665408 | tf_op jit(solution)/shard_map/pallas_call | solution.py:175
  86.0 9.9 %collective-permute-done.10.refs_9_ = bf16[896,512]{1,0:T(8,128)(2,1)S(1)} collective-permute-done((bf16[896,512]{1,0:T(8,128)(2,1)S(1)}, bf16[896,512]{1,0:T(8,128)(2,1)S(1)}, u32[]{:S(2)}, u32[]{:S(2)}) %collective-permute-start.10) | collective-permute-done | bytes 917536 | tf_op jit(solution)/shard_map/ppermute | solution.py:303
  111.2 4.7 %shard_map.65.refs_3_ = bf16[512,512]{1,0:T(8,128)(2,1)S(1)} custom-call(s32[4]{0:T(128)S(1)} %pad_add_fusion.where_ref, bf16[512,3712]{1,0:T(8,128)(2,1)S(1)} %pad_maximum_fusion.1.refs_0_.refs_1_, bf16[3584,512]{1,0:T(8,128)(2,1)S(1)} %bitcast.29, bf16[3584,512]{1,0:T(8,128)(2,1)S(1)} %bitcast.31), custom_call_target="tpu_custom_call" | custom-call | flops 3758096384 | bytes 11665408 | tf_op jit(solution)/shard_map/pallas_call | solution.py:175
  115.9 8.6 %collective-permute-done.15.refs_10_ = bf16[384,512]{1,0:T(8,128)(2,1)S(1)} collective-permute-done((bf16[384,512]{1,0:T(8,128)(2,1)}, bf16[384,512]{1,0:T(8,128)(2,1)S(1)}, u32[]{:S(2)}, u32[]{:S(2)}) %collective-permute-start.15) | collective-permute-done | bytes 393248 | tf_op jit(solution)/shard_map/ppermute | solution.py:303
  126.6 8.4 %collective-permute-done.17.refs_13_ = bf16[384,512]{1,0:T(8,128)(2,1)S(1)} collective-permute-done((bf16[384,512]{1,0:T(8,128)(2,1)S(1)}, bf16[384,512]{1,0:T(8,128)(2,1)S(1)}, u32[]{:S(2)}, u32[]{:S(2)}) %collective-permute-start.17) | collective-permute-done | bytes 393248 | tf_op jit(solution)/shard_map/ppermute | solution.py:306
  135.5 9.5 %shard_map.66.refs_4_ = bf16[1024,512]{1,0:T(8,128)(2,1)S(1)} custom-call(s32[4]{0:T(128)S(1)} %pad_add_fusion.where_ref, bf16[512,3712]{1,0:T(8,128)(2,1)S(1)} %copy-done.1, bf16[512,3712]{1,0:T(8,128)(2,1)S(1)} %pad_maximum_fusion.1.refs_0_.refs_1_, bf16[512,512]{1,0:T(8,128)(2,1)S(1)} %copy-done.12, bf16[768,512]{1,0:T(8,128)(2,1)S(1)} %copy-done.8, ...), custom_call_target="tpu_custom_call" | custom-call | flops 7516192768 | bytes 15990784 | tf_op jit(solution)/shard_map/pallas_call | solution.py:175
  155.2 10.4 %collective-permute-done.22.refs_6_ = bf16[512,512]{1,0:T(8,128)(2,1)S(1)} collective-permute-done((bf16[512,512]{1,0:T(8,128)(2,1)S(1)}, bf16[512,512]{1,0:T(8,128)(2,1)S(1)}, u32[]{:S(2)}, u32[]{:S(2)}) %collective-permute-start.22) | collective-permute-done | bytes 524320 | tf_op jit(solution)/shard_map/ppermute | solution.py:303
  165.6 5.8 %collective-permute-start.23 = (bf16[256,1024]{1,0:T(8,128)(2,1)S(1)}, bf16[256,1024]{1,0:T(8,128)(2,1)S(1)}, u32[]{:S(2)}, u32[]{:S(2)}) collective-permute-start(bf16[256,1024]{1,0:T(8,128)(2,1)S(1)} %get-tuple-element.87), channel_id=1, source_target_pairs={{0,2},{14,12},{1,3},{15,13},{16,18},{30,28},{17,19},{31,29}} | collective-permute-start | bytes 1572872 | tf_op jit(solution)/shard_map/ppermute | solution.py:380
  173.0 5.1 %collective-permute-done.23 = bf16[256,1024]{1,0:T(8,128)(2,1)S(1)} collective-permute-done((bf16[256,1024]{1,0:T(8,128)(2,1)S(1)}, bf16[256,1024]{1,0:T(8,128)(2,1)S(1)}, u32[]{:S(2)}, u32[]{:S(2)}) %collective-permute-start.23) | collective-permute-done | bytes 524320 | tf_op jit(solution)/shard_map/ppermute | solution.py:380
  178.3 4.6 %collective-permute-start.24 = (bf16[256,1024]{1,0:T(8,128)(2,1)S(1)}, bf16[256,1024]{1,0:T(8,128)(2,1)S(1)}, u32[]{:S(2)}, u32[]{:S(2)}) collective-permute-start(bf16[256,1024]{1,0:T(8,128)(2,1)S(1)} %add_convert_fusion.8), channel_id=1, source_target_pairs={{0,2},{2,4},{12,10},{14,12},{1,3},{3,5},{13,11},{15,13},{16,18},{1... | collective-permute-start | bytes 1572872 | tf_op jit(solution)/shard_map/ppermute | solution.py:380
  182.9 4.8 %shard_map.68 = (bf16[256,1536]{1,0:T(8,128)(2,1)S(1)}, bf16[768,1536]{1,0:T(8,128)(2,1)S(1)}) custom-call(s32[4]{0:T(128)S(1)} %pad_add_fusion.where_ref, bf16[512,3712]{1,0:T(8,128)(2,1)S(1)} %copy-done.1, bf16[512,3712]{1,0:T(8,128)(2,1)S(1)} %pad_maximum_fusion.1.refs_0_.refs_1_, bf16[512,512]{1,0:T(8,128)(2,1)S(1)} %shard_map.64.refs_2_, ...), custom_call_target="tpu_custom_call" | custom-call | flops 3221225472 | bytes 8388608 | tf_op jit(solution)/shard_map/pallas_call | solution.py:232
  189.7 4.4 %collective-permute-start.25 = (bf16[256,1024]{1,0:T(8,128)(2,1)S(1)}, bf16[256,1024]{1,0:T(8,128)(2,1)S(1)}, u32[]{:S(2)}, u32[]{:S(2)}) collective-permute-start(bf16[256,1024]{1,0:T(8,128)(2,1)S(1)} %add_convert_fusion.7), channel_id=1, source_target_pairs={{0,2},{2,4},{4,6},{10,8},{12,10},{14,12},{1,3},{3,5},{5,7},{11,9},... | collective-permute-start | bytes 1572872 | tf_op jit(solution)/shard_map/ppermute | solution.py:380
  202.8 6.3 %collective-permute-done.29 = bf16[256,1536]{1,0:T(8,128)(2,1)S(1)} collective-permute-done((bf16[256,1536]{1,0:T(8,128)(2,1)S(1)}, bf16[256,1536]{1,0:T(8,128)(2,1)S(1)}, u32[]{:S(2)}, u32[]{:S(2)}) %collective-permute-start.29) | collective-permute-done | bytes 786464 | tf_op jit(solution)/shard_map/ppermute | solution.py:380
  209.4 4.4 %collective-permute-start.30 = (bf16[256,1536]{1,0:T(8,128)(2,1)S(1)}, bf16[256,1536]{1,0:T(8,128)(2,1)S(1)}, u32[]{:S(2)}, u32[]{:S(2)}) collective-permute-start(bf16[256,1536]{1,0:T(8,128)(2,1)S(1)} %add_convert_fusion.4), channel_id=1, source_target_pairs={{0,2},{2,4},{12,10},{14,12},{1,3},{3,5},{13,11},{15,13},{16,18},{1... | collective-permute-start | bytes 2359304 | tf_op jit(solution)/shard_map/ppermute | solution.py:380
  216.7 6.6 %collective-permute-done.30 = bf16[256,1536]{1,0:T(8,128)(2,1)S(1)} collective-permute-done((bf16[256,1536]{1,0:T(8,128)(2,1)S(1)}, bf16[256,1536]{1,0:T(8,128)(2,1)S(1)}, u32[]{:S(2)}, u32[]{:S(2)}) %collective-permute-start.30) | collective-permute-done | bytes 786464 | tf_op jit(solution)/shard_map/ppermute | solution.py:380
  223.5 4.4 %collective-permute-start.31 = (bf16[256,1536]{1,0:T(8,128)(2,1)S(1)}, bf16[256,1536]{1,0:T(8,128)(2,1)S(1)}, u32[]{:S(2)}, u32[]{:S(2)}) collective-permute-start(bf16[256,1536]{1,0:T(8,128)(2,1)S(1)} %add_convert_fusion.3), channel_id=1, source_target_pairs={{0,2},{2,4},{4,6},{10,8},{12,10},{14,12},{1,3},{3,5},{5,7},{11,9},... | collective-permute-start | bytes 2359304 | tf_op jit(solution)/shard_map/ppermute | solution.py:380
  229.1 4.4 %collective-permute-start.35 = (bf16[256,1024]{1,0:T(8,128)(2,1)S(1)}, bf16[256,1024]{1,0:T(8,128)(2,1)S(1)}, u32[]{:S(2)}, u32[]{:S(2)}) collective-permute-start(bf16[256,1024]{1,0:T(8,128)(2,1)S(1)} %add_convert_fusion.6), channel_id=1, source_target_pairs={{0,2},{2,4},{12,10},{14,12},{1,3},{3,5},{13,11},{15,13},{16,18},{1... | collective-permute-start | bytes 1572872 | tf_op jit(solution)/shard_map/ppermute | solution.py:380
  235.2 7.8 %collective-permute-done.35 = bf16[256,1024]{1,0:T(8,128)(2,1)S(1)} collective-permute-done((bf16[256,1024]{1,0:T(8,128)(2,1)S(1)}, bf16[256,1024]{1,0:T(8,128)(2,1)S(1)}, u32[]{:S(2)}, u32[]{:S(2)}) %collective-permute-start.35) | collective-permute-done | bytes 524320 | tf_op jit(solution)/shard_map/ppermute | solution.py:380
  243.3 4.4 %collective-permute-start.36 = (bf16[256,1024]{1,0:T(8,128)(2,1)S(1)}, bf16[256,1024]{1,0:T(8,128)(2,1)S(1)}, u32[]{:S(2)}, u32[]{:S(2)}) collective-permute-start(bf16[256,1024]{1,0:T(8,128)(2,1)S(1)} %add_convert_fusion.5), channel_id=1, source_target_pairs={{0,2},{2,4},{4,6},{10,8},{12,10},{14,12},{1,3},{3,5},{5,7},{11,9},... | collective-permute-start | bytes 1572872 | tf_op jit(solution)/shard_map/ppermute | solution.py:380
  248.1 6.3 %collective-permute-done.36 = bf16[256,1024]{1,0:T(8,128)(2,1)S(1)} collective-permute-done((bf16[256,1024]{1,0:T(8,128)(2,1)S(1)}, bf16[256,1024]{1,0:T(8,128)(2,1)S(1)}, u32[]{:S(2)}, u32[]{:S(2)}) %collective-permute-start.36) | collective-permute-done | bytes 524320 | tf_op jit(solution)/shard_map/ppermute | solution.py:380
  (136 shorter events, 97.5 us)
Async XLA Ops:
  7.2 32.4 %collective-permute-start.1 = (bf16[256,3712]{1,0:T(8,128)(2,1)}, bf16[256,3712]{1,0:T(8,128)(2,1)}, u32[]{:S(2)}, u32[]{:S(2)}) collective-permute-start(bf16[256,3712]{1,0:T(8,128)(2,1)} %pad_maximum_fusion.2), channel_id=1, source_target_pairs={{2,0},{4,2},{6,4},{8,10},{10,12},{12,14},{3,1},{5,3},{7,5},{9,11},... | collective-permute-start | bytes 5701640 | tf_op jit(solution)/shard_map/ppermute | solution.py:309
  9.9 12.9 %collective-permute-start.3 = (bf16[512,512]{1,0:T(8,128)(2,1)S(1)}, bf16[512,512]{1,0:T(8,128)(2,1)S(1)}, u32[]{:S(2)}, u32[]{:S(2)}) collective-permute-start(bf16[512,512]{1,0:T(8,128)(2,1)S(1)} %get-tuple-element.100), channel_id=1, source_target_pairs={{0,1},{1,0},{2,3},{3,2},{4,5},{5,4},{6,7},{7,6},{8,9},{9,8},{10,11... | collective-permute-start | bytes 1572872 | tf_op jit(solution)/shard_map/ppermute | solution.py:303
  12.9 26.8 %collective-permute-start.2 = (bf16[768,512]{1,0:T(8,128)(2,1)S(1)}, bf16[768,512]{1,0:T(8,128)(2,1)S(1)}, u32[]{:S(2)}, u32[]{:S(2)}) collective-permute-start(bf16[768,512]{1,0:T(8,128)(2,1)S(1)} %copy-done.16), channel_id=1, source_target_pairs={{0,1},{1,0},{2,3},{3,2},{4,5},{5,4},{6,7},{7,6},{8,9},{9,8},{10,11... | collective-permute-start | bytes 2359304 | tf_op jit(solution)/shard_map/ppermute | solution.py:303
  39.6 30.2 %collective-permute-start.5 = (bf16[256,3712]{1,0:T(8,128)(2,1)}, bf16[256,3712]{1,0:T(8,128)(2,1)}, u32[]{:S(2)}, u32[]{:S(2)}) collective-permute-start(bf16[256,3712]{1,0:T(8,128)(2,1)} %collective-permute-done.1), channel_id=1, source_target_pairs={{2,0},{4,2},{10,12},{12,14},{3,1},{5,3},{11,13},{13,15},{18,16},{2... | collective-permute-start | bytes 5701640 | tf_op jit(solution)/shard_map/ppermute | solution.py:309
  40.9 28.9 %collective-permute-start.8 = (bf16[256,3712]{1,0:T(8,128)(2,1)}, bf16[256,3712]{1,0:T(8,128)(2,1)}, u32[]{:S(2)}, u32[]{:S(2)}) collective-permute-start(bf16[256,3712]{1,0:T(8,128)(2,1)} %collective-permute-done.1), channel_id=1, source_target_pairs={{0,8},{8,0},{1,9},{9,1},{2,10},{10,2},{3,11},{11,3},{4,12},{12,4},... | collective-permute-start | bytes 5701640 | tf_op jit(solution)/shard_map/ppermute | solution.py:292
  44.3 25.6 %collective-permute-start.6 = (bf16[1024,512]{1,0:T(8,128)(2,1)}, bf16[1024,512]{1,0:T(8,128)(2,1)S(1)}, u32[]{:S(2)}, u32[]{:S(2)}) collective-permute-start(bf16[1024,512]{1,0:T(8,128)(2,1)} %pad_maximum_fusion.3), channel_id=1, source_target_pairs={{0,1},{1,0},{2,3},{3,2},{4,5},{5,4},{6,7},{7,6},{8,9},{9,8},{10,11... | collective-permute-start | bytes 3145736 | tf_op jit(solution)/shard_map/ppermute | solution.py:303
  46.3 19.2 %collective-permute-start.7 = (bf16[768,512]{1,0:T(8,128)(2,1)S(1)}, bf16[768,512]{1,0:T(8,128)(2,1)S(1)}, u32[]{:S(2)}, u32[]{:S(2)}) collective-permute-start(bf16[768,512]{1,0:T(8,128)(2,1)S(1)} %collective-permute-done.2.refs_3_), channel_id=1, source_target_pairs={{0,16},{16,0},{1,17},{17,1},{2,18},{18,2},{3,19},{19,3},{4,20},{20... | collective-permute-start | bytes 2359304 | tf_op jit(solution)/shard_map/ppermute | solution.py:306
  69.9 27.3 %collective-permute-start.12 = (bf16[256,3712]{1,0:T(8,128)(2,1)}, bf16[256,3712]{1,0:T(8,128)(2,1)}, u32[]{:S(2)}, u32[]{:S(2)}) collective-permute-start(bf16[256,3712]{1,0:T(8,128)(2,1)} %collective-permute-done.5), channel_id=1, source_target_pairs={{0,8},{8,0},{1,9},{9,1},{2,10},{10,2},{3,11},{11,3},{4,12},{12,4},... | collective-permute-start | bytes 5701640 | tf_op jit(solution)/shard_map/ppermute | solution.py:292
  69.9 29.2 %collective-permute-start.9 = (bf16[256,3712]{1,0:T(8,128)(2,1)}, bf16[256,3712]{1,0:T(8,128)(2,1)}, u32[]{:S(2)}, u32[]{:S(2)}) collective-permute-start(bf16[256,3712]{1,0:T(8,128)(2,1)} %collective-permute-done.5), channel_id=1, source_target_pairs={{2,0},{12,14},{3,1},{13,15},{18,16},{28,30},{19,17},{29,31}} | collective-permute-start | bytes 5701640 | tf_op jit(solution)/shard_map/ppermute | solution.py:309
  71.2 26.0 %collective-permute-start.11 = (bf16[1024,512]{1,0:T(8,128)(2,1)S(1)}, bf16[1024,512]{1,0:T(8,128)(2,1)S(1)}, u32[]{:S(2)}, u32[]{:S(2)}) collective-permute-start(bf16[1024,512]{1,0:T(8,128)(2,1)S(1)} %collective-permute-done.6.refs_4_.refs_8_), channel_id=1, source_target_pairs={{0,16},{16,0},{1,17},{17,1},{2,18},{18,2},{3,19},{19,3},{4,20},{20... | collective-permute-start | bytes 3145736 | tf_op jit(solution)/shard_map/ppermute | solution.py:306
  73.0 23.0 %collective-permute-start.10 = (bf16[896,512]{1,0:T(8,128)(2,1)S(1)}, bf16[896,512]{1,0:T(8,128)(2,1)S(1)}, u32[]{:S(2)}, u32[]{:S(2)}) collective-permute-start(bf16[896,512]{1,0:T(8,128)(2,1)S(1)} %dynamic-slice_bitcast_fusion), channel_id=1, source_target_pairs={{0,1},{1,0},{2,3},{3,2},{4,5},{5,4},{6,7},{7,6},{8,9},{9,8},{10,11... | collective-permute-start | bytes 2752520 | tf_op jit(solution)/shard_map/ppermute | solution.py:303
  100.3 24.3 %collective-permute-start.14 = (bf16[896,512]{1,0:T(8,128)(2,1)S(1)}, bf16[896,512]{1,0:T(8,128)(2,1)S(1)}, u32[]{:S(2)}, u32[]{:S(2)}) collective-permute-start(bf16[896,512]{1,0:T(8,128)(2,1)S(1)} %collective-permute-done.10.refs_9_), channel_id=1, source_target_pairs={{0,16},{16,0},{1,17},{17,1},{2,18},{18,2},{3,19},{19,3},{4,20},{20... | collective-permute-start | bytes 2752520 | tf_op jit(solution)/shard_map/ppermute | solution.py:306
  101.8 22.7 %collective-permute-start.16 = (bf16[512,512]{1,0:T(8,128)(2,1)}, bf16[512,512]{1,0:T(8,128)(2,1)S(1)}, u32[]{:S(2)}, u32[]{:S(2)}) collective-permute-start(bf16[512,512]{1,0:T(8,128)(2,1)} %get-tuple-element.68), channel_id=1, source_target_pairs={{0,1},{1,0},{2,3},{3,2},{4,5},{5,4},{6,7},{7,6},{8,9},{9,8},{10,11... | collective-permute-start | bytes 1572872 | tf_op jit(solution)/shard_map/ppermute | solution.py:303
  103.3 21.2 %collective-permute-start.15 = (bf16[384,512]{1,0:T(8,128)(2,1)}, bf16[384,512]{1,0:T(8,128)(2,1)S(1)}, u32[]{:S(2)}, u32[]{:S(2)}) collective-permute-start(bf16[384,512]{1,0:T(8,128)(2,1)} %dynamic-slice_bitcast_fusion.8), channel_id=1, source_target_pairs={{0,1},{1,0},{2,3},{3,2},{4,5},{5,4},{6,7},{7,6},{8,9},{9,8},{10,11... | collective-permute-start | bytes 1179656 | tf_op jit(solution)/shard_map/ppermute | solution.py:303
  125.1 20.0 %collective-permute-start.19 = (bf16[512,768]{1,0:T(8,128)(2,1)S(1)}, bf16[512,768]{1,0:T(8,128)(2,1)S(1)}, u32[]{:S(2)}, u32[]{:S(2)}) collective-permute-start(bf16[512,768]{1,0:T(8,128)(2,1)S(1)} %dynamic-slice_bitcast_fusion.1), channel_id=1, source_target_pairs={{0,1},{1,0},{2,3},{3,2},{4,5},{5,4},{6,7},{7,6},{8,9},{9,8},{10,11... | collective-permute-start | bytes 2359304 | tf_op jit(solution)/shard_map/ppermute | solution.py:303
  151.0 22.0 %collective-permute-start.21 = (bf16[512,768]{1,0:T(8,128)(2,1)S(1)}, bf16[512,768]{1,0:T(8,128)(2,1)S(1)}, u32[]{:S(2)}, u32[]{:S(2)}) collective-permute-start(bf16[512,768]{1,0:T(8,128)(2,1)S(1)} %collective-permute-done.19.refs_6_), channel_id=1, source_target_pairs={{0,16},{16,0},{1,17},{17,1},{2,18},{18,2},{3,19},{19,3},{4,20},{20... | collective-permute-start | bytes 2359304 | tf_op jit(solution)/shard_map/ppermute | solution.py:306
  151.6 14.0 %collective-permute-start.22 = (bf16[512,512]{1,0:T(8,128)(2,1)S(1)}, bf16[512,512]{1,0:T(8,128)(2,1)S(1)}, u32[]{:S(2)}, u32[]{:S(2)}) collective-permute-start(bf16[512,512]{1,0:T(8,128)(2,1)S(1)} %copy-done.17), channel_id=1, source_target_pairs={{0,1},{1,0},{2,3},{3,2},{4,5},{5,4},{6,7},{7,6},{8,9},{9,8},{10,11... | collective-permute-start | bytes 1572872 | tf_op jit(solution)/shard_map/ppermute | solution.py:303
  171.5 16.3 %collective-permute-start.27 = (bf16[512,512]{1,0:T(8,128)(2,1)S(1)}, bf16[512,512]{1,0:T(8,128)(2,1)S(1)}, u32[]{:S(2)}, u32[]{:S(2)}) collective-permute-start(bf16[512,512]{1,0:T(8,128)(2,1)S(1)} %collective-permute-done.22.refs_6_), channel_id=1, source_target_pairs={{0,16},{16,0},{1,17},{17,1},{2,18},{18,2},{3,19},{19,3},{4,20},{20... | collective-permute-start | bytes 1572872 | tf_op jit(solution)/shard_map/ppermute | solution.py:306
  189.7 13.1 %collective-permute-start.25 = (bf16[256,1024]{1,0:T(8,128)(2,1)S(1)}, bf16[256,1024]{1,0:T(8,128)(2,1)S(1)}, u32[]{:S(2)}, u32[]{:S(2)}) collective-permute-start(bf16[256,1024]{1,0:T(8,128)(2,1)S(1)} %add_convert_fusion.7), channel_id=1, source_target_pairs={{0,2},{2,4},{4,6},{10,8},{12,10},{14,12},{1,3},{3,5},{5,7},{11,9},... | collective-permute-start | bytes 1572872 | tf_op jit(solution)/shard_map/ppermute | solution.py:380
  194.8 14.4 %collective-permute-start.29 = (bf16[256,1536]{1,0:T(8,128)(2,1)S(1)}, bf16[256,1536]{1,0:T(8,128)(2,1)S(1)}, u32[]{:S(2)}, u32[]{:S(2)}) collective-permute-start(bf16[256,1536]{1,0:T(8,128)(2,1)S(1)} %slice.66), channel_id=1, source_target_pairs={{0,2},{14,12},{1,3},{15,13},{16,18},{30,28},{17,19},{31,29}} | collective-permute-start | bytes 2359304 | tf_op jit(solution)/shard_map/ppermute | solution.py:380
  209.4 13.9 %collective-permute-start.30 = (bf16[256,1536]{1,0:T(8,128)(2,1)S(1)}, bf16[256,1536]{1,0:T(8,128)(2,1)S(1)}, u32[]{:S(2)}, u32[]{:S(2)}) collective-permute-start(bf16[256,1536]{1,0:T(8,128)(2,1)S(1)} %add_convert_fusion.4), channel_id=1, source_target_pairs={{0,2},{2,4},{12,10},{14,12},{1,3},{3,5},{13,11},{15,13},{16,18},{1... | collective-permute-start | bytes 2359304 | tf_op jit(solution)/shard_map/ppermute | solution.py:380
  214.7 14.1 %collective-permute-start.34 = (bf16[256,1024]{1,0:T(8,128)(2,1)S(1)}, bf16[256,1024]{1,0:T(8,128)(2,1)S(1)}, u32[]{:S(2)}, u32[]{:S(2)}) collective-permute-start(bf16[256,1024]{1,0:T(8,128)(2,1)S(1)} %slice.71), channel_id=1, source_target_pairs={{0,2},{14,12},{1,3},{15,13},{16,18},{30,28},{17,19},{31,29}} | collective-permute-start | bytes 1572872 | tf_op jit(solution)/shard_map/ppermute | solution.py:380
  223.5 24.2 %collective-permute-start.31 = (bf16[256,1536]{1,0:T(8,128)(2,1)S(1)}, bf16[256,1536]{1,0:T(8,128)(2,1)S(1)}, u32[]{:S(2)}, u32[]{:S(2)}) collective-permute-start(bf16[256,1536]{1,0:T(8,128)(2,1)S(1)} %add_convert_fusion.3), channel_id=1, source_target_pairs={{0,2},{2,4},{4,6},{10,8},{12,10},{14,12},{1,3},{3,5},{5,7},{11,9},... | collective-permute-start | bytes 2359304 | tf_op jit(solution)/shard_map/ppermute | solution.py:380
  229.1 14.0 %collective-permute-start.35 = (bf16[256,1024]{1,0:T(8,128)(2,1)S(1)}, bf16[256,1024]{1,0:T(8,128)(2,1)S(1)}, u32[]{:S(2)}, u32[]{:S(2)}) collective-permute-start(bf16[256,1024]{1,0:T(8,128)(2,1)S(1)} %add_convert_fusion.6), channel_id=1, source_target_pairs={{0,2},{2,4},{12,10},{14,12},{1,3},{3,5},{13,11},{15,13},{16,18},{1... | collective-permute-start | bytes 1572872 | tf_op jit(solution)/shard_map/ppermute | solution.py:380
  (32 other events, 312.7 us)

commit v5 on v4

--- a/solution.py
+++ b/solution.py
@@ -11,8 +11,8 @@
 LANES = 128
 STEPS = 4
 GATE_ROWS = (512, 768, 512)
-UP_ROWS = (512, 896, 384)
-DOWN_COLUMNS = (1024, 1536, 1024)
+UP_ROWS = (512, 1024, 256)
+DOWN_COLUMNS = (1024, 1280, 1280)
 
 
 def slot_tables(routes, first_expert, expert_count, capacity, expert_total):
@@ -337,7 +337,8 @@
     own = [(0, -1, gate_local)], [(0, -1, up_local)]
     own_early = hidden_call(where, [early], *own)
     rest = u0 + u1
-    pieces = cut(up_local, rest, u2), pieces[1]
+    piece = jnp.concatenate([up_local[rest:half_depth], up_local[half_depth + rest :]], axis=0)
+    pieces = piece, pieces[1]
     got3, up_b, both_cx, other2, own_early, pieces = together(
         (got3, up_b, both_cx, other2, own_early, pieces)
     )
@@ -353,18 +354,17 @@
     own_late = hidden_call(where, [late], *own)
     pieces = cut(down_local, 2 * d0, d1, 1), cut(down_local, 2 * (d0 + d1), d2, 1)
     up_bx, up_c, down_a, own_late, pieces = together((up_bx, up_c, down_a, own_late, pieces))
-    up_cx, down_b = relay(up_c), swap(pieces[0])
-    up_cx, down_a = together((up_cx, down_a))
-    down_ax = relay(down_a)
+    down_ax, down_b = relay(down_a), swap(pieces[0])
     crossed = hidden_call(
-        after(where, up_cx), [early, late],
+        where, [early, late],
         [
             (0, 0, gate_a), (g0, 0, gate_b), (g0 + g1, 0, both_c, 0, g2),
             (0, 1, gate_ax), (g0, 1, gate_bx), (g0 + g1, 1, both_cx, 0, g2),
         ],
         [
-            (0, 0, both_c, g2 // u0, u0), (u0, 0, up_b), (rest, 0, up_c),
-            (0, 1, both_cx, g2 // u0, u0), (u0, 1, up_bx), (rest, 1, up_cx),
+            (0, 0, both_c, g2 // u0, u0), (u0, 0, up_b),
+            (0, 1, both_cx, g2 // u0, u0), (u0, 1, up_bx),
+            (rest, -1, up_c, 0, u2), (half_depth + rest, -1, up_c, 1, u2),
         ],
     )
     down_ax, down_b, crossed, piece = together((down_ax, down_b, crossed, pieces[1]))
@@ -393,10 +393,10 @@
     down_bx, down_c = relay(down_b), swap(piece)
     home_a, away_a = expert(0, down_a, down_ax)
     a1, a2, a3 = thirds(away_a, across(away_a))
-    moving_a = step(after(a3, down_c), None, 3)
+    moving_a = step(a3, None, 3)
     home_b, away_b = expert(2 * d0, down_b, down_bx, moving_a, down_c)
     down_cx = relay(down_c)
-    moving_a = step(after(a2, down_bx), moving_a, 2)
+    moving_a = step(after(a2, down_bx, down_c), moving_a, 2)
     b1, b2, b3 = thirds(away_b, across(after(away_b, moving_a, down_cx)))
     moving_a = step(a1, moving_a, 1)
     moving_b = step(b3, None, 3)

time: 258 us -> 246 us (0.953)
  waiting for transfers between devices: 119 us -> 99.8 us
  starting transfers between devices: 69.1 us -> 76.7 us
  other arithmetic: 19.1 us -> 16.4 us
    ppermute x9, waiting for transfers between devices: 34.6 us -> 21 us  [step(): return lax.ppermute(rows, both, back_pairs(k))]
    ppermute x9, starting transfers between devices: 38.7 us -> 48.2 us  [step(): return lax.ppermute(rows, both, back_pairs(k))]
    ppermute x8 -> x7, waiting for transfers between devices: 30.2 us -> 25.5 us  [relay(): return lax.ppermute(x, 'parts', swap_two)]
    unnamed x36 -> x42, local copies, waits for them, and re-layouts: 7.76 us -> 9.87 us
    dynamic_slice x7 -> x6, local copies, waits for them, and re-layouts: 10.9 us -> 9.09 us  [cut(): return lax.dynamic_slice_in_dim(array, begin, length, dim)]
    ppermute x8 -> x7, starting transfers between devices: 10.5 us -> 9.62 us  [relay(): return lax.ppermute(x, 'parts', swap_two)]
  transfers between devices with their start and end apart: 38 -> 37, of which waited for: 23 -> 23; matrix products, arithmetic and copies ran while one was open for 10% -> 9% of each run, Pallas kernels for 11% -> 11%
where the time goes in v5:
time: 246 us; the launch traced here: 245 us
  waiting for transfers between devices  99.8 us (41%)
  starting transfers between devices  76.7 us (31%)
  Pallas kernels  31.6 us (13%)
  local copies, waits for them, and re-layouts  20.3 us (8%)
  other arithmetic  16.4 us (7%)
    ppermute x8, waiting for transfers between devices, swap(): return lax.ppermute(x, 'local', swap_half)  49.7 us
    ppermute x9, starting transfers between devices, step(): return lax.ppermute(rows, both, back_pairs(k))  48.2 us
    ppermute x7, waiting for transfers between devices, relay(): return lax.ppermute(x, 'parts', swap_two)  25.5 us
    ppermute x9, waiting for transfers between devices, step(): return lax.ppermute(rows, both, back_pairs(k))  21 us
    pallas_call x3, Pallas kernels, hidden_call(): pl.pallas_call(functools.partial(hidden_kernel, batches, gate_pieces, up_...  18.4 us
    pallas_call x3, Pallas kernels, down_call(): pl.pallas_call(functools.partial(down_kernel, batches, first, width), gri...  13.2 us
    ppermute x8, starting transfers between devices, swap(): return lax.ppermute(x, 'local', swap_half)  10.5 us
    unnamed x42, local copies, waits for them, and re-layouts  9.87 us
  transfers between devices with their start and end apart: 37, of which 23 were waited for; matrix products, arithmetic and copies ran while one was open for 9% of the time, Pallas kernels for 11%

profile of v5, /device:TPU:0, one launch (start us, length us, event | category | flops | bytes accessed | tf_op | source)
XLA Modules:
  0.0 245.4 jit_solution(8476818600076351642)
XLA Ops:
  11.9 9.8 %collective-permute-done.3.refs_2_ = bf16[512,512]{1,0:T(8,128)(2,1)S(1)} collective-permute-done((bf16[512,512]{1,0:T(8,128)(2,1)S(1)}, bf16[512,512]{1,0:T(8,128)(2,1)S(1)}, u32[]{:S(2)}, u32[]{:S(2)}) %collective-permute-start.3) | collective-permute-done | bytes 524320 | tf_op jit(solution)/shard_map/ppermute | solution.py:303
  26.2 6.0 %collective-permute-done.4.refs_5_ = bf16[512,512]{1,0:T(8,128)(2,1)S(1)} collective-permute-done((bf16[512,512]{1,0:T(8,128)(2,1)S(1)}, bf16[512,512]{1,0:T(8,128)(2,1)S(1)}, u32[]{:S(2)}, u32[]{:S(2)}) %collective-permute-start.4) | collective-permute-done | bytes 524320 | tf_op jit(solution)/shard_map/ppermute | solution.py:306
  33.1 5.4 %collective-permute-done.2.refs_3_ = bf16[768,512]{1,0:T(8,128)(2,1)S(1)} collective-permute-done((bf16[768,512]{1,0:T(8,128)(2,1)S(1)}, bf16[768,512]{1,0:T(8,128)(2,1)S(1)}, u32[]{:S(2)}, u32[]{:S(2)}) %collective-permute-start.2) | collective-permute-done | bytes 786464 | tf_op jit(solution)/shard_map/ppermute | solution.py:303
  51.9 12.5 %collective-permute-done.7.refs_6_ = bf16[768,512]{1,0:T(8,128)(2,1)S(1)} collective-permute-done((bf16[768,512]{1,0:T(8,128)(2,1)S(1)}, bf16[768,512]{1,0:T(8,128)(2,1)S(1)}, u32[]{:S(2)}, u32[]{:S(2)}) %collective-permute-start.7) | collective-permute-done | bytes 786464 | tf_op jit(solution)/shard_map/ppermute | solution.py:306
  79.6 4.7 %shard_map.64.refs_2_ = bf16[512,512]{1,0:T(8,128)(2,1)S(1)} custom-call(s32[4]{0:T(128)S(1)} %pad_add_fusion.where_ref, bf16[512,3712]{1,0:T(8,128)(2,1)S(1)} %pad_maximum_fusion.refs_0_, bf16[3584,512]{1,0:T(8,128)(2,1)S(1)} %bitcast.32, bf16[3584,512]{1,0:T(8,128)(2,1)S(1)} %bitcast.30), custom_call_target="tpu_custom_call" | custom-call | flops 3758096384 | bytes 11665408 | tf_op jit(solution)/shard_map/pallas_call | solution.py:175
  84.4 11.7 %collective-permute-done.10.refs_9_ = bf16[1024,512]{1,0:T(8,128)(2,1)S(1)} collective-permute-done((bf16[1024,512]{1,0:T(8,128)(2,1)S(1)}, bf16[1024,512]{1,0:T(8,128)(2,1)S(1)}, u32[]{:S(2)}, u32[]{:S(2)}) %collective-permute-start.10) | collective-permute-done | bytes 1048608 | tf_op jit(solution)/shard_map/ppermute | solution.py:303
  111.2 4.7 %shard_map.65.refs_3_ = bf16[512,512]{1,0:T(8,128)(2,1)S(1)} custom-call(s32[4]{0:T(128)S(1)} %pad_add_fusion.where_ref, bf16[512,3712]{1,0:T(8,128)(2,1)S(1)} %pad_maximum_fusion.1.refs_0_.refs_1_, bf16[3584,512]{1,0:T(8,128)(2,1)S(1)} %bitcast.33, bf16[3584,512]{1,0:T(8,128)(2,1)S(1)} %bitcast.31), custom_call_target="tpu_custom_call" | custom-call | flops 3758096384 | bytes 11665408 | tf_op jit(solution)/shard_map/pallas_call | solution.py:175
  116.5 10.5 %collective-permute-done.16.refs_6_ = bf16[512,512]{1,0:T(8,128)(2,1)S(1)} collective-permute-done((bf16[512,512]{1,0:T(8,128)(2,1)S(1)}, bf16[512,512]{1,0:T(8,128)(2,1)S(1)}, u32[]{:S(2)}, u32[]{:S(2)}) %collective-permute-start.16) | collective-permute-done | bytes 524320 | tf_op jit(solution)/shard_map/ppermute | solution.py:303
  128.4 9.0 %shard_map.66.refs_4_ = bf16[1024,512]{1,0:T(8,128)(2,1)S(1)} custom-call(s32[4]{0:T(128)S(1)} %pad_add_fusion.where_ref, bf16[512,3712]{1,0:T(8,128)(2,1)S(1)} %copy-done.1, bf16[512,3712]{1,0:T(8,128)(2,1)S(1)} %pad_maximum_fusion.1.refs_0_.refs_1_, bf16[512,512]{1,0:T(8,128)(2,1)S(1)} %copy-done.12, bf16[768,512]{1,0:T(8,128)(2,1)S(1)} %collective-permute-done.2.refs_3_, ...), custom_call_target="tpu_custom_call" | custom-call | flops 7516192768 | bytes 15990784 | tf_op jit(solution)/shard_map/pallas_call | solution.py:175
  143.1 3.7 %shard_map.67 = (bf16[256,1024]{1,0:T(8,128)(2,1)S(1)}, bf16[768,1024]{1,0:T(8,128)(2,1)S(1)}) custom-call(s32[4]{0:T(128)S(1)} %pad_add_fusion.where_ref, bf16[512,3712]{1,0:T(8,128)(2,1)S(1)} %copy-done.1, bf16[512,3712]{1,0:T(8,128)(2,1)S(1)} %pad_maximum_fusion.1.refs_0_.refs_1_, bf16[512,512]{1,0:T(8,128)(2,1)S(1)} %shard_map.64.refs_2_, ...), custom_call_target="tpu_custom_call" | custom-call | flops 2147483648 | bytes 6291456 | tf_op jit(solution)/shard_map/pallas_call | solution.py:232
  151.0 7.4 %collective-permute-start.22 = (bf16[256,1024]{1,0:T(8,128)(2,1)S(1)}, bf16[256,1024]{1,0:T(8,128)(2,1)S(1)}, u32[]{:S(2)}, u32[]{:S(2)}) collective-permute-start(bf16[256,1024]{1,0:T(8,128)(2,1)S(1)} %get-tuple-element.98), channel_id=1, source_target_pairs={{0,2},{14,12},{1,3},{15,13},{16,18},{30,28},{17,19},{31,29}} | collective-permute-start | bytes 1572872 | tf_op jit(solution)/shard_map/ppermute | solution.py:380
  158.4 5.9 %collective-permute-done.21.refs_6_ = bf16[512,640]{1,0:T(8,128)(2,1)S(1)} collective-permute-done((bf16[512,640]{1,0:T(8,128)(2,1)S(1)}, bf16[512,640]{1,0:T(8,128)(2,1)S(1)}, u32[]{:S(2)}, u32[]{:S(2)}) %collective-permute-start.21) | collective-permute-done | bytes 655392 | tf_op jit(solution)/shard_map/ppermute | solution.py:303
  165.9 7.6 %collective-permute-start.23 = (bf16[256,1024]{1,0:T(8,128)(2,1)S(1)}, bf16[256,1024]{1,0:T(8,128)(2,1)S(1)}, u32[]{:S(2)}, u32[]{:S(2)}) collective-permute-start(bf16[256,1024]{1,0:T(8,128)(2,1)S(1)} %add_convert_fusion.8), channel_id=1, source_target_pairs={{0,2},{2,4},{12,10},{14,12},{1,3},{3,5},{13,11},{15,13},{16,18},{1... | collective-permute-start | bytes 1572872 | tf_op jit(solution)/shard_map/ppermute | solution.py:380
  173.5 4.8 %shard_map.68 = (bf16[256,1280]{1,0:T(8,128)(2,1)S(1)}, bf16[768,1280]{1,0:T(8,128)(2,1)S(1)}) custom-call(s32[4]{0:T(128)S(1)} %pad_add_fusion.where_ref, bf16[512,3712]{1,0:T(8,128)(2,1)S(1)} %copy-done.1, bf16[512,3712]{1,0:T(8,128)(2,1)S(1)} %pad_maximum_fusion.1.refs_0_.refs_1_, bf16[512,512]{1,0:T(8,128)(2,1)S(1)} %shard_map.64.refs_2_, ...), custom_call_target="tpu_custom_call" | custom-call | flops 2684354560 | bytes 7340032 | tf_op jit(solution)/shard_map/pallas_call | solution.py:232
  180.5 7.4 %collective-permute-start.24 = (bf16[256,1024]{1,0:T(8,128)(2,1)S(1)}, bf16[256,1024]{1,0:T(8,128)(2,1)S(1)}, u32[]{:S(2)}, u32[]{:S(2)}) collective-permute-start(bf16[256,1024]{1,0:T(8,128)(2,1)S(1)} %add_convert_fusion.7), channel_id=1, source_target_pairs={{0,2},{2,4},{4,6},{10,8},{12,10},{14,12},{1,3},{3,5},{5,7},{11,9},... | collective-permute-start | bytes 1572872 | tf_op jit(solution)/shard_map/ppermute | solution.py:380
  188.5 4.8 %shard_map.69 = (bf16[256,1280]{1,0:T(8,128)(2,1)S(1)}, bf16[768,1280]{1,0:T(8,128)(2,1)S(1)}) custom-call(s32[4]{0:T(128)S(1)} %pad_add_fusion.where_ref, bf16[512,3712]{1,0:T(8,128)(2,1)S(1)} %copy-done.1, bf16[512,3712]{1,0:T(8,128)(2,1)S(1)} %pad_maximum_fusion.1.refs_0_.refs_1_, bf16[512,512]{1,0:T(8,128)(2,1)S(1)} %shard_map.64.refs_2_, ...), custom_call_target="tpu_custom_call" | custom-call | flops 2684354560 | bytes 7340032 | tf_op jit(solution)/shard_map/pallas_call | solution.py:232
  194.9 4.3 %collective-permute-start.28 = (bf16[256,1280]{1,0:T(8,128)(2,1)S(1)}, bf16[256,1280]{1,0:T(8,128)(2,1)S(1)}, u32[]{:S(2)}, u32[]{:S(2)}) collective-permute-start(bf16[256,1280]{1,0:T(8,128)(2,1)S(1)} %slice.82), channel_id=1, source_target_pairs={{0,2},{14,12},{1,3},{15,13},{16,18},{30,28},{17,19},{31,29}} | collective-permute-start | bytes 1966088 | tf_op jit(solution)/shard_map/ppermute | solution.py:380
  199.8 3.8 %collective-permute-start.33 = (bf16[256,1280]{1,0:T(8,128)(2,1)S(1)}, bf16[256,1280]{1,0:T(8,128)(2,1)S(1)}, u32[]{:S(2)}, u32[]{:S(2)}) collective-permute-start(bf16[256,1280]{1,0:T(8,128)(2,1)S(1)} %slice.87), channel_id=1, source_target_pairs={{0,2},{14,12},{1,3},{15,13},{16,18},{30,28},{17,19},{31,29}} | collective-permute-start | bytes 1966088 | tf_op jit(solution)/shard_map/ppermute | solution.py:380
  203.5 3.7 %collective-permute-done.28 = bf16[256,1280]{1,0:T(8,128)(2,1)S(1)} collective-permute-done((bf16[256,1280]{1,0:T(8,128)(2,1)S(1)}, bf16[256,1280]{1,0:T(8,128)(2,1)S(1)}, u32[]{:S(2)}, u32[]{:S(2)}) %collective-permute-start.28) | collective-permute-done | bytes 655392 | tf_op jit(solution)/shard_map/ppermute | solution.py:380
  207.4 4.4 %collective-permute-start.29 = (bf16[256,1280]{1,0:T(8,128)(2,1)S(1)}, bf16[256,1280]{1,0:T(8,128)(2,1)S(1)}, u32[]{:S(2)}, u32[]{:S(2)}) collective-permute-start(bf16[256,1280]{1,0:T(8,128)(2,1)S(1)} %add_convert_fusion.6), channel_id=1, source_target_pairs={{0,2},{2,4},{12,10},{14,12},{1,3},{3,5},{13,11},{15,13},{16,18},{1... | collective-permute-start | bytes 1966088 | tf_op jit(solution)/shard_map/ppermute | solution.py:380
  214.4 4.4 %collective-permute-start.34 = (bf16[256,1280]{1,0:T(8,128)(2,1)S(1)}, bf16[256,1280]{1,0:T(8,128)(2,1)S(1)}, u32[]{:S(2)}, u32[]{:S(2)}) collective-permute-start(bf16[256,1280]{1,0:T(8,128)(2,1)S(1)} %add_convert_fusion.4), channel_id=1, source_target_pairs={{0,2},{2,4},{12,10},{14,12},{1,3},{3,5},{13,11},{15,13},{16,18},{1... | collective-permute-start | bytes 1966088 | tf_op jit(solution)/shard_map/ppermute | solution.py:380
  221.5 4.4 %collective-permute-start.30 = (bf16[256,1280]{1,0:T(8,128)(2,1)S(1)}, bf16[256,1280]{1,0:T(8,128)(2,1)S(1)}, u32[]{:S(2)}, u32[]{:S(2)}) collective-permute-start(bf16[256,1280]{1,0:T(8,128)(2,1)S(1)} %add_convert_fusion.5), channel_id=1, source_target_pairs={{0,2},{2,4},{4,6},{10,8},{12,10},{14,12},{1,3},{3,5},{5,7},{11,9},... | collective-permute-start | bytes 1966088 | tf_op jit(solution)/shard_map/ppermute | solution.py:380
  228.6 4.4 %collective-permute-start.35 = (bf16[256,1280]{1,0:T(8,128)(2,1)S(1)}, bf16[256,1280]{1,0:T(8,128)(2,1)S(1)}, u32[]{:S(2)}, u32[]{:S(2)}) collective-permute-start(bf16[256,1280]{1,0:T(8,128)(2,1)S(1)} %add_convert_fusion.3), channel_id=1, source_target_pairs={{0,2},{2,4},{4,6},{10,8},{12,10},{14,12},{1,3},{3,5},{5,7},{11,9},... | collective-permute-start | bytes 1966088 | tf_op jit(solution)/shard_map/ppermute | solution.py:380
  235.6 6.7 %collective-permute-done.35 = bf16[256,1280]{1,0:T(8,128)(2,1)S(1)} collective-permute-done((bf16[256,1280]{1,0:T(8,128)(2,1)S(1)}, bf16[256,1280]{1,0:T(8,128)(2,1)S(1)}, u32[]{:S(2)}, u32[]{:S(2)}) %collective-permute-start.35) | collective-permute-done | bytes 655392 | tf_op jit(solution)/shard_map/ppermute | solution.py:380
  (141 shorter events, 92.6 us)
Async XLA Ops:
  6.0 32.5 %collective-permute-start.1 = (bf16[256,3712]{1,0:T(8,128)(2,1)S(1)}, bf16[256,3712]{1,0:T(8,128)(2,1)}, u32[]{:S(2)}, u32[]{:S(2)}) collective-permute-start(bf16[256,3712]{1,0:T(8,128)(2,1)S(1)} %pad_maximum_fusion.2), channel_id=1, source_target_pairs={{2,0},{4,2},{6,4},{8,10},{10,12},{12,14},{3,1},{5,3},{7,5},{9,11},... | collective-permute-start | bytes 5701640 | tf_op jit(solution)/shard_map/ppermute | solution.py:309
  11.8 26.7 %collective-permute-start.2 = (bf16[768,512]{1,0:T(8,128)(2,1)S(1)}, bf16[768,512]{1,0:T(8,128)(2,1)S(1)}, u32[]{:S(2)}, u32[]{:S(2)}) collective-permute-start(bf16[768,512]{1,0:T(8,128)(2,1)S(1)} %copy-done.18), channel_id=1, source_target_pairs={{0,1},{1,0},{2,3},{3,2},{4,5},{5,4},{6,7},{7,6},{8,9},{9,8},{10,11... | collective-permute-start | bytes 2359304 | tf_op jit(solution)/shard_map/ppermute | solution.py:303
  38.5 30.2 %collective-permute-start.5 = (bf16[256,3712]{1,0:T(8,128)(2,1)}, bf16[256,3712]{1,0:T(8,128)(2,1)}, u32[]{:S(2)}, u32[]{:S(2)}) collective-permute-start(bf16[256,3712]{1,0:T(8,128)(2,1)} %collective-permute-done.1), channel_id=1, source_target_pairs={{2,0},{4,2},{10,12},{12,14},{3,1},{5,3},{11,13},{13,15},{18,16},{2... | collective-permute-start | bytes 5701640 | tf_op jit(solution)/shard_map/ppermute | solution.py:309
  39.8 28.9 %collective-permute-start.8 = (bf16[256,3712]{1,0:T(8,128)(2,1)}, bf16[256,3712]{1,0:T(8,128)(2,1)}, u32[]{:S(2)}, u32[]{:S(2)}) collective-permute-start(bf16[256,3712]{1,0:T(8,128)(2,1)} %collective-permute-done.1), channel_id=1, source_target_pairs={{0,8},{8,0},{1,9},{9,1},{2,10},{10,2},{3,11},{11,3},{4,12},{12,4},... | collective-permute-start | bytes 5701640 | tf_op jit(solution)/shard_map/ppermute | solution.py:292
  43.2 25.6 %collective-permute-start.6 = (bf16[1024,512]{1,0:T(8,128)(2,1)}, bf16[1024,512]{1,0:T(8,128)(2,1)S(1)}, u32[]{:S(2)}, u32[]{:S(2)}) collective-permute-start(bf16[1024,512]{1,0:T(8,128)(2,1)} %pad_maximum_fusion.3), channel_id=1, source_target_pairs={{0,1},{1,0},{2,3},{3,2},{4,5},{5,4},{6,7},{7,6},{8,9},{9,8},{10,11... | collective-permute-start | bytes 3145736 | tf_op jit(solution)/shard_map/ppermute | solution.py:303
  45.2 19.2 %collective-permute-start.7 = (bf16[768,512]{1,0:T(8,128)(2,1)S(1)}, bf16[768,512]{1,0:T(8,128)(2,1)S(1)}, u32[]{:S(2)}, u32[]{:S(2)}) collective-permute-start(bf16[768,512]{1,0:T(8,128)(2,1)S(1)} %collective-permute-done.2.refs_3_), channel_id=1, source_target_pairs={{0,16},{16,0},{1,17},{17,1},{2,18},{18,2},{3,19},{19,3},{4,20},{20... | collective-permute-start | bytes 2359304 | tf_op jit(solution)/shard_map/ppermute | solution.py:306
  68.8 29.9 %collective-permute-start.12 = (bf16[256,3712]{1,0:T(8,128)(2,1)}, bf16[256,3712]{1,0:T(8,128)(2,1)}, u32[]{:S(2)}, u32[]{:S(2)}) collective-permute-start(bf16[256,3712]{1,0:T(8,128)(2,1)} %collective-permute-done.5), channel_id=1, source_target_pairs={{0,8},{8,0},{1,9},{9,1},{2,10},{10,2},{3,11},{11,3},{4,12},{12,4},... | collective-permute-start | bytes 5701640 | tf_op jit(solution)/shard_map/ppermute | solution.py:292
  68.8 29.9 %collective-permute-start.9 = (bf16[256,3712]{1,0:T(8,128)(2,1)}, bf16[256,3712]{1,0:T(8,128)(2,1)}, u32[]{:S(2)}, u32[]{:S(2)}) collective-permute-start(bf16[256,3712]{1,0:T(8,128)(2,1)} %collective-permute-done.5), channel_id=1, source_target_pairs={{2,0},{12,14},{3,1},{13,15},{18,16},{28,30},{19,17},{29,31}} | collective-permute-start | bytes 5701640 | tf_op jit(solution)/shard_map/ppermute | solution.py:309
  70.1 26.0 %collective-permute-start.10 = (bf16[1024,512]{1,0:T(8,128)(2,1)S(1)}, bf16[1024,512]{1,0:T(8,128)(2,1)S(1)}, u32[]{:S(2)}, u32[]{:S(2)}) collective-permute-start(bf16[1024,512]{1,0:T(8,128)(2,1)S(1)} %dynamic-slice_bitcast_fusion), channel_id=1, source_target_pairs={{0,1},{1,0},{2,3},{3,2},{4,5},{5,4},{6,7},{7,6},{8,9},{9,8},{10,11... | collective-permute-start | bytes 3145736 | tf_op jit(solution)/shard_map/ppermute | solution.py:303
  71.9 25.8 %collective-permute-start.11 = (bf16[1024,512]{1,0:T(8,128)(2,1)S(1)}, bf16[1024,512]{1,0:T(8,128)(2,1)S(1)}, u32[]{:S(2)}, u32[]{:S(2)}) collective-permute-start(bf16[1024,512]{1,0:T(8,128)(2,1)S(1)} %collective-permute-done.6.refs_4_.refs_8_), channel_id=1, source_target_pairs={{0,16},{16,0},{1,17},{17,1},{2,18},{18,2},{3,19},{19,3},{4,20},{20... | collective-permute-start | bytes 3145736 | tf_op jit(solution)/shard_map/ppermute | solution.py:306
  100.2 26.8 %collective-permute-start.14 = (bf16[1024,512]{1,0:T(8,128)(2,1)S(1)}, bf16[1024,512]{1,0:T(8,128)(2,1)S(1)}, u32[]{:S(2)}, u32[]{:S(2)}) collective-permute-start(bf16[1024,512]{1,0:T(8,128)(2,1)S(1)} %collective-permute-done.10.refs_9_), channel_id=1, source_target_pairs={{0,16},{16,0},{1,17},{17,1},{2,18},{18,2},{3,19},{19,3},{4,20},{20... | collective-permute-start | bytes 3145736 | tf_op jit(solution)/shard_map/ppermute | solution.py:306
  101.8 14.8 %collective-permute-start.15 = (bf16[512,512]{1,0:T(8,128)(2,1)S(1)}, bf16[512,512]{1,0:T(8,128)(2,1)S(1)}, u32[]{:S(2)}, u32[]{:S(2)}) collective-permute-start(bf16[512,512]{1,0:T(8,128)(2,1)S(1)} %copy-done.19), channel_id=1, source_target_pairs={{0,1},{1,0},{2,3},{3,2},{4,5},{5,4},{6,7},{7,6},{8,9},{9,8},{10,11... | collective-permute-start | bytes 1572872 | tf_op jit(solution)/shard_map/ppermute | solution.py:303
  102.5 24.5 %collective-permute-start.16 = (bf16[512,512]{1,0:T(8,128)(2,1)S(1)}, bf16[512,512]{1,0:T(8,128)(2,1)S(1)}, u32[]{:S(2)}, u32[]{:S(2)}) collective-permute-start(bf16[512,512]{1,0:T(8,128)(2,1)S(1)} %copy-done.20), channel_id=1, source_target_pairs={{0,1},{1,0},{2,3},{3,2},{4,5},{5,4},{6,7},{7,6},{8,9},{9,8},{10,11... | collective-permute-start | bytes 1572872 | tf_op jit(solution)/shard_map/ppermute | solution.py:303
  127.0 16.0 %collective-permute-start.18 = (bf16[512,640]{1,0:T(8,128)(2,1)S(1)}, bf16[512,640]{1,0:T(8,128)(2,1)S(1)}, u32[]{:S(2)}, u32[]{:S(2)}) collective-permute-start(bf16[512,640]{1,0:T(8,128)(2,1)S(1)} %get-tuple-element.67), channel_id=1, source_target_pairs={{0,1},{1,0},{2,3},{3,2},{4,5},{5,4},{6,7},{7,6},{8,9},{9,8},{10,11... | collective-permute-start | bytes 1966088 | tf_op jit(solution)/shard_map/ppermute | solution.py:303
  146.8 18.9 %collective-permute-start.20 = (bf16[512,640]{1,0:T(8,128)(2,1)S(1)}, bf16[512,640]{1,0:T(8,128)(2,1)S(1)}, u32[]{:S(2)}, u32[]{:S(2)}) collective-permute-start(bf16[512,640]{1,0:T(8,128)(2,1)S(1)} %collective-permute-done.18.refs_6_), channel_id=1, source_target_pairs={{0,16},{16,0},{1,17},{17,1},{2,18},{18,2},{3,19},{19,3},{4,20},{20... | collective-permute-start | bytes 1966088 | tf_op jit(solution)/shard_map/ppermute | solution.py:306
  147.5 16.8 %collective-permute-start.21 = (bf16[512,640]{1,0:T(8,128)(2,1)S(1)}, bf16[512,640]{1,0:T(8,128)(2,1)S(1)}, u32[]{:S(2)}, u32[]{:S(2)}) collective-permute-start(bf16[512,640]{1,0:T(8,128)(2,1)S(1)} %get-tuple-element.78), channel_id=1, source_target_pairs={{0,1},{1,0},{2,3},{3,2},{4,5},{5,4},{6,7},{7,6},{8,9},{9,8},{10,11... | collective-permute-start | bytes 1966088 | tf_op jit(solution)/shard_map/ppermute | solution.py:303
  151.0 14.7 %collective-permute-start.22 = (bf16[256,1024]{1,0:T(8,128)(2,1)S(1)}, bf16[256,1024]{1,0:T(8,128)(2,1)S(1)}, u32[]{:S(2)}, u32[]{:S(2)}) collective-permute-start(bf16[256,1024]{1,0:T(8,128)(2,1)S(1)} %get-tuple-element.98), channel_id=1, source_target_pairs={{0,2},{14,12},{1,3},{15,13},{16,18},{30,28},{17,19},{31,29}} | collective-permute-start | bytes 1572872 | tf_op jit(solution)/shard_map/ppermute | solution.py:380
  164.3 16.0 %collective-permute-start.26 = (bf16[512,640]{1,0:T(8,128)(2,1)S(1)}, bf16[512,640]{1,0:T(8,128)(2,1)S(1)}, u32[]{:S(2)}, u32[]{:S(2)}) collective-permute-start(bf16[512,640]{1,0:T(8,128)(2,1)S(1)} %collective-permute-done.21.refs_6_), channel_id=1, source_target_pairs={{0,16},{16,0},{1,17},{17,1},{2,18},{18,2},{3,19},{19,3},{4,20},{20... | collective-permute-start | bytes 1966088 | tf_op jit(solution)/shard_map/ppermute | solution.py:306
  165.9 14.3 %collective-permute-start.23 = (bf16[256,1024]{1,0:T(8,128)(2,1)S(1)}, bf16[256,1024]{1,0:T(8,128)(2,1)S(1)}, u32[]{:S(2)}, u32[]{:S(2)}) collective-permute-start(bf16[256,1024]{1,0:T(8,128)(2,1)S(1)} %add_convert_fusion.8), channel_id=1, source_target_pairs={{0,2},{2,4},{12,10},{14,12},{1,3},{3,5},{13,11},{15,13},{16,18},{1... | collective-permute-start | bytes 1572872 | tf_op jit(solution)/shard_map/ppermute | solution.py:380
  180.5 14.1 %collective-permute-start.24 = (bf16[256,1024]{1,0:T(8,128)(2,1)S(1)}, bf16[256,1024]{1,0:T(8,128)(2,1)S(1)}, u32[]{:S(2)}, u32[]{:S(2)}) collective-permute-start(bf16[256,1024]{1,0:T(8,128)(2,1)S(1)} %add_convert_fusion.7), channel_id=1, source_target_pairs={{0,2},{2,4},{4,6},{10,8},{12,10},{14,12},{1,3},{3,5},{5,7},{11,9},... | collective-permute-start | bytes 1572872 | tf_op jit(solution)/shard_map/ppermute | solution.py:380
  199.8 14.5 %collective-permute-start.33 = (bf16[256,1280]{1,0:T(8,128)(2,1)S(1)}, bf16[256,1280]{1,0:T(8,128)(2,1)S(1)}, u32[]{:S(2)}, u32[]{:S(2)}) collective-permute-start(bf16[256,1280]{1,0:T(8,128)(2,1)S(1)} %slice.87), channel_id=1, source_target_pairs={{0,2},{14,12},{1,3},{15,13},{16,18},{30,28},{17,19},{31,29}} | collective-permute-start | bytes 1966088 | tf_op jit(solution)/shard_map/ppermute | solution.py:380
  207.4 13.9 %collective-permute-start.29 = (bf16[256,1280]{1,0:T(8,128)(2,1)S(1)}, bf16[256,1280]{1,0:T(8,128)(2,1)S(1)}, u32[]{:S(2)}, u32[]{:S(2)}) collective-permute-start(bf16[256,1280]{1,0:T(8,128)(2,1)S(1)} %add_convert_fusion.6), channel_id=1, source_target_pairs={{0,2},{2,4},{12,10},{14,12},{1,3},{3,5},{13,11},{15,13},{16,18},{1... | collective-permute-start | bytes 1966088 | tf_op jit(solution)/shard_map/ppermute | solution.py:380
  211.9 14.1 %collective-permute-start.25 = (bf16[128,1024]{1,0:T(8,128)(2,1)S(1)}, bf16[128,1024]{1,0:T(8,128)(2,1)S(1)}, u32[]{:S(2)}, u32[]{:S(2)}) collective-permute-start(bf16[128,1024]{1,0:T(8,128)(2,1)S(1)} %select_convert_fusion.2), channel_id=1, source_target_pairs={{0,8},{8,0},{1,9},{9,1},{2,10},{10,2},{3,11},{11,3},{4,12},{12,4},... | collective-permute-start | bytes 786440 | tf_op jit(solution)/shard_map/ppermute | solution.py:292
  214.4 13.9 %collective-permute-start.34 = (bf16[256,1280]{1,0:T(8,128)(2,1)S(1)}, bf16[256,1280]{1,0:T(8,128)(2,1)S(1)}, u32[]{:S(2)}, u32[]{:S(2)}) collective-permute-start(bf16[256,1280]{1,0:T(8,128)(2,1)S(1)} %add_convert_fusion.4), channel_id=1, source_target_pairs={{0,2},{2,4},{12,10},{14,12},{1,3},{3,5},{13,11},{15,13},{16,18},{1... | collective-permute-start | bytes 1966088 | tf_op jit(solution)/shard_map/ppermute | solution.py:380
  (34 other events, 319.1 us)

commit v6 on v5

--- a/solution.py
+++ b/solution.py
@@ -338,7 +338,7 @@
     own_early = hidden_call(where, [early], *own)
     rest = u0 + u1
     piece = jnp.concatenate([up_local[rest:half_depth], up_local[half_depth + rest :]], axis=0)
-    pieces = piece, pieces[1]
+    pieces = piece, pieces[1], cut(down_local, 2 * d0, d1, 1), cut(down_local, 2 * (d0 + d1), d2, 1)
     got3, up_b, both_cx, other2, own_early, pieces = together(
         (got3, up_b, both_cx, other2, own_early, pieces)
     )
@@ -352,9 +352,8 @@
     )
     late = jnp.concatenate([slot2, slot3], axis=0)
     own_late = hidden_call(where, [late], *own)
-    pieces = cut(down_local, 2 * d0, d1, 1), cut(down_local, 2 * (d0 + d1), d2, 1)
     up_bx, up_c, down_a, own_late, pieces = together((up_bx, up_c, down_a, own_late, pieces))
-    down_ax, down_b = relay(down_a), swap(pieces[0])
+    down_ax, down_b = relay(down_a), swap(pieces[2])
     crossed = hidden_call(
         where, [early, late],
         [
@@ -367,7 +366,7 @@
             (rest, -1, up_c, 0, u2), (half_depth + rest, -1, up_c, 1, u2),
         ],
     )
-    down_ax, down_b, crossed, piece = together((down_ax, down_b, crossed, pieces[1]))
+    down_ax, down_b, crossed, piece = together((down_ax, down_b, crossed, pieces[3]))
 
     def expert(first, near, far, *earlier):
         return down_call(

time: 246 us -> 245 us (level)
  waiting for transfers between devices: 99.8 us -> 97.1 us
    ppermute x7, waiting for transfers between devices: 25.5 us -> 22.8 us  [relay(): return lax.ppermute(x, 'parts', swap_two)]
  transfers between devices with their start and end apart: 37 -> 37, of which waited for: 23 -> 23; matrix products, arithmetic and copies ran while one was open for 9% -> 10% of each run, Pallas kernels for 11% -> 11%
where the time goes in v6:
time: 245 us; the launch traced here: 244 us
  waiting for transfers between devices  97.1 us (40%)
  starting transfers between devices  76.8 us (31%)
  Pallas kernels  31.6 us (13%)
  local copies, waits for them, and re-layouts  21.3 us (9%)
  other arithmetic  16.4 us (7%)
    ppermute x8, waiting for transfers between devices, swap(): return lax.ppermute(x, 'local', swap_half)  49.8 us
    ppermute x9, starting transfers between devices, step(): return lax.ppermute(rows, both, back_pairs(k))  48.1 us
    ppermute x7, waiting for transfers between devices, relay(): return lax.ppermute(x, 'parts', swap_two)  22.8 us
    ppermute x9, waiting for transfers between devices, step(): return lax.ppermute(rows, both, back_pairs(k))  21 us
    pallas_call x3, Pallas kernels, hidden_call(): pl.pallas_call(functools.partial(hidden_kernel, batches, gate_pieces, up_...  18.4 us
    pallas_call x3, Pallas kernels, down_call(): pl.pallas_call(functools.partial(down_kernel, batches, first, width), gri...  13.3 us
    ppermute x8, starting transfers between devices, swap(): return lax.ppermute(x, 'local', swap_half)  10.5 us
    dynamic_slice x6, local copies, waits for them, and re-layouts, cut(): return lax.dynamic_slice_in_dim(array, begin, length, dim)  10.1 us
  transfers between devices with their start and end apart: 37, of which 23 were waited for; matrix products, arithmetic and copies ran while one was open for 10% of the time, Pallas kernels for 11%

profile of v6, /device:TPU:0, one launch (start us, length us, event | category | flops | bytes accessed | tf_op | source)
XLA Modules:
  0.0 243.9 jit_solution(7793337737696543019)
XLA Ops:
  11.9 9.8 %collective-permute-done.3.refs_2_ = bf16[512,512]{1,0:T(8,128)(2,1)S(1)} collective-permute-done((bf16[512,512]{1,0:T(8,128)(2,1)S(1)}, bf16[512,512]{1,0:T(8,128)(2,1)S(1)}, u32[]{:S(2)}, u32[]{:S(2)}) %collective-permute-start.3) | collective-permute-done | bytes 524320 | tf_op jit(solution)/shard_map/ppermute | solution.py:303
  26.2 6.0 %collective-permute-done.4.refs_5_ = bf16[512,512]{1,0:T(8,128)(2,1)S(1)} collective-permute-done((bf16[512,512]{1,0:T(8,128)(2,1)S(1)}, bf16[512,512]{1,0:T(8,128)(2,1)S(1)}, u32[]{:S(2)}, u32[]{:S(2)}) %collective-permute-start.4) | collective-permute-done | bytes 524320 | tf_op jit(solution)/shard_map/ppermute | solution.py:306
  33.1 5.4 %collective-permute-done.2.refs_3_ = bf16[768,512]{1,0:T(8,128)(2,1)S(1)} collective-permute-done((bf16[768,512]{1,0:T(8,128)(2,1)S(1)}, bf16[768,512]{1,0:T(8,128)(2,1)S(1)}, u32[]{:S(2)}, u32[]{:S(2)}) %collective-permute-start.2) | collective-permute-done | bytes 786464 | tf_op jit(solution)/shard_map/ppermute | solution.py:303
  54.4 10.0 %collective-permute-done.7.refs_6_ = bf16[768,512]{1,0:T(8,128)(2,1)S(1)} collective-permute-done((bf16[768,512]{1,0:T(8,128)(2,1)S(1)}, bf16[768,512]{1,0:T(8,128)(2,1)S(1)}, u32[]{:S(2)}, u32[]{:S(2)}) %collective-permute-start.7) | collective-permute-done | bytes 786464 | tf_op jit(solution)/shard_map/ppermute | solution.py:306
  79.8 4.7 %shard_map.64.refs_2_ = bf16[512,512]{1,0:T(8,128)(2,1)S(1)} custom-call(s32[4]{0:T(128)S(1)} %pad_add_fusion.where_ref, bf16[512,3712]{1,0:T(8,128)(2,1)S(1)} %pad_maximum_fusion.refs_0_, bf16[3584,512]{1,0:T(8,128)(2,1)S(1)} %bitcast.32, bf16[3584,512]{1,0:T(8,128)(2,1)S(1)} %bitcast.30), custom_call_target="tpu_custom_call" | custom-call | flops 3758096384 | bytes 11665408 | tf_op jit(solution)/shard_map/pallas_call | solution.py:175
  84.5 11.7 %collective-permute-done.10.refs_9_ = bf16[1024,512]{1,0:T(8,128)(2,1)S(1)} collective-permute-done((bf16[1024,512]{1,0:T(8,128)(2,1)S(1)}, bf16[1024,512]{1,0:T(8,128)(2,1)S(1)}, u32[]{:S(2)}, u32[]{:S(2)}) %collective-permute-start.10) | collective-permute-done | bytes 1048608 | tf_op jit(solution)/shard_map/ppermute | solution.py:303
  109.7 4.7 %shard_map.65.refs_3_ = bf16[512,512]{1,0:T(8,128)(2,1)S(1)} custom-call(s32[4]{0:T(128)S(1)} %pad_add_fusion.where_ref, bf16[512,3712]{1,0:T(8,128)(2,1)S(1)} %pad_maximum_fusion.1.refs_0_.refs_1_, bf16[3584,512]{1,0:T(8,128)(2,1)S(1)} %bitcast.33, bf16[3584,512]{1,0:T(8,128)(2,1)S(1)} %bitcast.31), custom_call_target="tpu_custom_call" | custom-call | flops 3758096384 | bytes 11665408 | tf_op jit(solution)/shard_map/pallas_call | solution.py:175
  115.2 10.5 %collective-permute-done.16.refs_6_ = bf16[512,512]{1,0:T(8,128)(2,1)S(1)} collective-permute-done((bf16[512,512]{1,0:T(8,128)(2,1)}, bf16[512,512]{1,0:T(8,128)(2,1)S(1)}, u32[]{:S(2)}, u32[]{:S(2)}) %collective-permute-start.16) | collective-permute-done | bytes 524320 | tf_op jit(solution)/shard_map/ppermute | solution.py:303
  127.0 9.0 %shard_map.66.refs_4_ = bf16[1024,512]{1,0:T(8,128)(2,1)S(1)} custom-call(s32[4]{0:T(128)S(1)} %pad_add_fusion.where_ref, bf16[512,3712]{1,0:T(8,128)(2,1)S(1)} %copy-done.1, bf16[512,3712]{1,0:T(8,128)(2,1)S(1)} %pad_maximum_fusion.1.refs_0_.refs_1_, bf16[512,512]{1,0:T(8,128)(2,1)S(1)} %copy-done.12, bf16[768,512]{1,0:T(8,128)(2,1)S(1)} %collective-permute-done.2.refs_3_, ...), custom_call_target="tpu_custom_call" | custom-call | flops 7516192768 | bytes 15990784 | tf_op jit(solution)/shard_map/pallas_call | solution.py:175
  141.7 3.7 %shard_map.67 = (bf16[256,1024]{1,0:T(8,128)(2,1)S(1)}, bf16[768,1024]{1,0:T(8,128)(2,1)S(1)}) custom-call(s32[4]{0:T(128)S(1)} %pad_add_fusion.where_ref, bf16[512,3712]{1,0:T(8,128)(2,1)S(1)} %copy-done.1, bf16[512,3712]{1,0:T(8,128)(2,1)S(1)} %pad_maximum_fusion.1.refs_0_.refs_1_, bf16[512,512]{1,0:T(8,128)(2,1)S(1)} %shard_map.64.refs_2_, ...), custom_call_target="tpu_custom_call" | custom-call | flops 2147483648 | bytes 6291456 | tf_op jit(solution)/shard_map/pallas_call | solution.py:232
  149.6 7.4 %collective-permute-start.22 = (bf16[256,1024]{1,0:T(8,128)(2,1)S(1)}, bf16[256,1024]{1,0:T(8,128)(2,1)S(1)}, u32[]{:S(2)}, u32[]{:S(2)}) collective-permute-start(bf16[256,1024]{1,0:T(8,128)(2,1)S(1)} %get-tuple-element.102), channel_id=1, source_target_pairs={{0,2},{14,12},{1,3},{15,13},{16,18},{30,28},{17,19},{31,29}} | collective-permute-start | bytes 1572872 | tf_op jit(solution)/shard_map/ppermute | solution.py:379
  157.0 5.8 %collective-permute-done.21.refs_6_ = bf16[512,640]{1,0:T(8,128)(2,1)S(1)} collective-permute-done((bf16[512,640]{1,0:T(8,128)(2,1)S(1)}, bf16[512,640]{1,0:T(8,128)(2,1)S(1)}, u32[]{:S(2)}, u32[]{:S(2)}) %collective-permute-start.21) | collective-permute-done | bytes 655392 | tf_op jit(solution)/shard_map/ppermute | solution.py:303
  164.5 7.6 %collective-permute-start.23 = (bf16[256,1024]{1,0:T(8,128)(2,1)S(1)}, bf16[256,1024]{1,0:T(8,128)(2,1)S(1)}, u32[]{:S(2)}, u32[]{:S(2)}) collective-permute-start(bf16[256,1024]{1,0:T(8,128)(2,1)S(1)} %add_convert_fusion.8), channel_id=1, source_target_pairs={{0,2},{2,4},{12,10},{14,12},{1,3},{3,5},{13,11},{15,13},{16,18},{1... | collective-permute-start | bytes 1572872 | tf_op jit(solution)/shard_map/ppermute | solution.py:379
  172.1 4.8 %shard_map.68 = (bf16[256,1280]{1,0:T(8,128)(2,1)S(1)}, bf16[768,1280]{1,0:T(8,128)(2,1)S(1)}) custom-call(s32[4]{0:T(128)S(1)} %pad_add_fusion.where_ref, bf16[512,3712]{1,0:T(8,128)(2,1)S(1)} %copy-done.1, bf16[512,3712]{1,0:T(8,128)(2,1)S(1)} %pad_maximum_fusion.1.refs_0_.refs_1_, bf16[512,512]{1,0:T(8,128)(2,1)S(1)} %shard_map.64.refs_2_, ...), custom_call_target="tpu_custom_call" | custom-call | flops 2684354560 | bytes 7340032 | tf_op jit(solution)/shard_map/pallas_call | solution.py:232
  179.1 7.4 %collective-permute-start.24 = (bf16[256,1024]{1,0:T(8,128)(2,1)S(1)}, bf16[256,1024]{1,0:T(8,128)(2,1)S(1)}, u32[]{:S(2)}, u32[]{:S(2)}) collective-permute-start(bf16[256,1024]{1,0:T(8,128)(2,1)S(1)} %add_convert_fusion.7), channel_id=1, source_target_pairs={{0,2},{2,4},{4,6},{10,8},{12,10},{14,12},{1,3},{3,5},{5,7},{11,9},... | collective-permute-start | bytes 1572872 | tf_op jit(solution)/shard_map/ppermute | solution.py:379
  187.0 4.8 %shard_map.69 = (bf16[256,1280]{1,0:T(8,128)(2,1)S(1)}, bf16[768,1280]{1,0:T(8,128)(2,1)S(1)}) custom-call(s32[4]{0:T(128)S(1)} %pad_add_fusion.where_ref, bf16[512,3712]{1,0:T(8,128)(2,1)S(1)} %copy-done.1, bf16[512,3712]{1,0:T(8,128)(2,1)S(1)} %pad_maximum_fusion.1.refs_0_.refs_1_, bf16[512,512]{1,0:T(8,128)(2,1)S(1)} %shard_map.64.refs_2_, ...), custom_call_target="tpu_custom_call" | custom-call | flops 2684354560 | bytes 7340032 | tf_op jit(solution)/shard_map/pallas_call | solution.py:232
  193.4 4.3 %collective-permute-start.28 = (bf16[256,1280]{1,0:T(8,128)(2,1)S(1)}, bf16[256,1280]{1,0:T(8,128)(2,1)S(1)}, u32[]{:S(2)}, u32[]{:S(2)}) collective-permute-start(bf16[256,1280]{1,0:T(8,128)(2,1)S(1)} %slice.82), channel_id=1, source_target_pairs={{0,2},{14,12},{1,3},{15,13},{16,18},{30,28},{17,19},{31,29}} | collective-permute-start | bytes 1966088 | tf_op jit(solution)/shard_map/ppermute | solution.py:379
  198.3 3.8 %collective-permute-start.33 = (bf16[256,1280]{1,0:T(8,128)(2,1)S(1)}, bf16[256,1280]{1,0:T(8,128)(2,1)S(1)}, u32[]{:S(2)}, u32[]{:S(2)}) collective-permute-start(bf16[256,1280]{1,0:T(8,128)(2,1)S(1)} %slice.87), channel_id=1, source_target_pairs={{0,2},{14,12},{1,3},{15,13},{16,18},{30,28},{17,19},{31,29}} | collective-permute-start | bytes 1966088 | tf_op jit(solution)/shard_map/ppermute | solution.py:379
  202.1 3.7 %collective-permute-done.28 = bf16[256,1280]{1,0:T(8,128)(2,1)S(1)} collective-permute-done((bf16[256,1280]{1,0:T(8,128)(2,1)S(1)}, bf16[256,1280]{1,0:T(8,128)(2,1)S(1)}, u32[]{:S(2)}, u32[]{:S(2)}) %collective-permute-start.28) | collective-permute-done | bytes 655392 | tf_op jit(solution)/shard_map/ppermute | solution.py:379
  205.9 4.4 %collective-permute-start.29 = (bf16[256,1280]{1,0:T(8,128)(2,1)S(1)}, bf16[256,1280]{1,0:T(8,128)(2,1)S(1)}, u32[]{:S(2)}, u32[]{:S(2)}) collective-permute-start(bf16[256,1280]{1,0:T(8,128)(2,1)S(1)} %add_convert_fusion.6), channel_id=1, source_target_pairs={{0,2},{2,4},{12,10},{14,12},{1,3},{3,5},{13,11},{15,13},{16,18},{1... | collective-permute-start | bytes 1966088 | tf_op jit(solution)/shard_map/ppermute | solution.py:379
  213.0 4.4 %collective-permute-start.34 = (bf16[256,1280]{1,0:T(8,128)(2,1)S(1)}, bf16[256,1280]{1,0:T(8,128)(2,1)S(1)}, u32[]{:S(2)}, u32[]{:S(2)}) collective-permute-start(bf16[256,1280]{1,0:T(8,128)(2,1)S(1)} %add_convert_fusion.4), channel_id=1, source_target_pairs={{0,2},{2,4},{12,10},{14,12},{1,3},{3,5},{13,11},{15,13},{16,18},{1... | collective-permute-start | bytes 1966088 | tf_op jit(solution)/shard_map/ppermute | solution.py:379
  220.1 4.4 %collective-permute-start.30 = (bf16[256,1280]{1,0:T(8,128)(2,1)S(1)}, bf16[256,1280]{1,0:T(8,128)(2,1)S(1)}, u32[]{:S(2)}, u32[]{:S(2)}) collective-permute-start(bf16[256,1280]{1,0:T(8,128)(2,1)S(1)} %add_convert_fusion.5), channel_id=1, source_target_pairs={{0,2},{2,4},{4,6},{10,8},{12,10},{14,12},{1,3},{3,5},{5,7},{11,9},... | collective-permute-start | bytes 1966088 | tf_op jit(solution)/shard_map/ppermute | solution.py:379
  227.1 4.4 %collective-permute-start.35 = (bf16[256,1280]{1,0:T(8,128)(2,1)S(1)}, bf16[256,1280]{1,0:T(8,128)(2,1)S(1)}, u32[]{:S(2)}, u32[]{:S(2)}) collective-permute-start(bf16[256,1280]{1,0:T(8,128)(2,1)S(1)} %add_convert_fusion.3), channel_id=1, source_target_pairs={{0,2},{2,4},{4,6},{10,8},{12,10},{14,12},{1,3},{3,5},{5,7},{11,9},... | collective-permute-start | bytes 1966088 | tf_op jit(solution)/shard_map/ppermute | solution.py:379
  234.2 6.7 %collective-permute-done.35 = bf16[256,1280]{1,0:T(8,128)(2,1)S(1)} collective-permute-done((bf16[256,1280]{1,0:T(8,128)(2,1)S(1)}, bf16[256,1280]{1,0:T(8,128)(2,1)S(1)}, u32[]{:S(2)}, u32[]{:S(2)}) %collective-permute-start.35) | collective-permute-done | bytes 655392 | tf_op jit(solution)/shard_map/ppermute | solution.py:379
  (141 shorter events, 93.9 us)
Async XLA Ops:
  6.0 32.5 %collective-permute-start.1 = (bf16[256,3712]{1,0:T(8,128)(2,1)S(1)}, bf16[256,3712]{1,0:T(8,128)(2,1)}, u32[]{:S(2)}, u32[]{:S(2)}) collective-permute-start(bf16[256,3712]{1,0:T(8,128)(2,1)S(1)} %pad_maximum_fusion.2), channel_id=1, source_target_pairs={{2,0},{4,2},{6,4},{8,10},{10,12},{12,14},{3,1},{5,3},{7,5},{9,11},... | collective-permute-start | bytes 5701640 | tf_op jit(solution)/shard_map/ppermute | solution.py:309
  11.8 26.7 %collective-permute-start.2 = (bf16[768,512]{1,0:T(8,128)(2,1)S(1)}, bf16[768,512]{1,0:T(8,128)(2,1)S(1)}, u32[]{:S(2)}, u32[]{:S(2)}) collective-permute-start(bf16[768,512]{1,0:T(8,128)(2,1)S(1)} %copy-done.18), channel_id=1, source_target_pairs={{0,1},{1,0},{2,3},{3,2},{4,5},{5,4},{6,7},{7,6},{8,9},{9,8},{10,11... | collective-permute-start | bytes 2359304 | tf_op jit(solution)/shard_map/ppermute | solution.py:303
  38.5 30.2 %collective-permute-start.5 = (bf16[256,3712]{1,0:T(8,128)(2,1)}, bf16[256,3712]{1,0:T(8,128)(2,1)}, u32[]{:S(2)}, u32[]{:S(2)}) collective-permute-start(bf16[256,3712]{1,0:T(8,128)(2,1)} %collective-permute-done.1), channel_id=1, source_target_pairs={{2,0},{4,2},{10,12},{12,14},{3,1},{5,3},{11,13},{13,15},{18,16},{2... | collective-permute-start | bytes 5701640 | tf_op jit(solution)/shard_map/ppermute | solution.py:309
  39.8 28.9 %collective-permute-start.8 = (bf16[256,3712]{1,0:T(8,128)(2,1)}, bf16[256,3712]{1,0:T(8,128)(2,1)}, u32[]{:S(2)}, u32[]{:S(2)}) collective-permute-start(bf16[256,3712]{1,0:T(8,128)(2,1)} %collective-permute-done.1), channel_id=1, source_target_pairs={{0,8},{8,0},{1,9},{9,1},{2,10},{10,2},{3,11},{11,3},{4,12},{12,4},... | collective-permute-start | bytes 5701640 | tf_op jit(solution)/shard_map/ppermute | solution.py:292
  43.2 25.6 %collective-permute-start.6 = (bf16[1024,512]{1,0:T(8,128)(2,1)}, bf16[1024,512]{1,0:T(8,128)(2,1)S(1)}, u32[]{:S(2)}, u32[]{:S(2)}) collective-permute-start(bf16[1024,512]{1,0:T(8,128)(2,1)} %pad_maximum_fusion.3), channel_id=1, source_target_pairs={{0,1},{1,0},{2,3},{3,2},{4,5},{5,4},{6,7},{7,6},{8,9},{9,8},{10,11... | collective-permute-start | bytes 3145736 | tf_op jit(solution)/shard_map/ppermute | solution.py:303
  45.2 19.2 %collective-permute-start.7 = (bf16[768,512]{1,0:T(8,128)(2,1)S(1)}, bf16[768,512]{1,0:T(8,128)(2,1)S(1)}, u32[]{:S(2)}, u32[]{:S(2)}) collective-permute-start(bf16[768,512]{1,0:T(8,128)(2,1)S(1)} %collective-permute-done.2.refs_3_), channel_id=1, source_target_pairs={{0,16},{16,0},{1,17},{17,1},{2,18},{18,2},{3,19},{19,3},{4,20},{20... | collective-permute-start | bytes 2359304 | tf_op jit(solution)/shard_map/ppermute | solution.py:306
  68.8 29.9 %collective-permute-start.12 = (bf16[256,3712]{1,0:T(8,128)(2,1)}, bf16[256,3712]{1,0:T(8,128)(2,1)}, u32[]{:S(2)}, u32[]{:S(2)}) collective-permute-start(bf16[256,3712]{1,0:T(8,128)(2,1)} %collective-permute-done.5), channel_id=1, source_target_pairs={{0,8},{8,0},{1,9},{9,1},{2,10},{10,2},{3,11},{11,3},{4,12},{12,4},... | collective-permute-start | bytes 5701640 | tf_op jit(solution)/shard_map/ppermute | solution.py:292
  68.8 29.9 %collective-permute-start.9 = (bf16[256,3712]{1,0:T(8,128)(2,1)}, bf16[256,3712]{1,0:T(8,128)(2,1)}, u32[]{:S(2)}, u32[]{:S(2)}) collective-permute-start(bf16[256,3712]{1,0:T(8,128)(2,1)} %collective-permute-done.5), channel_id=1, source_target_pairs={{2,0},{12,14},{3,1},{13,15},{18,16},{28,30},{19,17},{29,31}} | collective-permute-start | bytes 5701640 | tf_op jit(solution)/shard_map/ppermute | solution.py:309
  70.2 26.0 %collective-permute-start.10 = (bf16[1024,512]{1,0:T(8,128)(2,1)S(1)}, bf16[1024,512]{1,0:T(8,128)(2,1)S(1)}, u32[]{:S(2)}, u32[]{:S(2)}) collective-permute-start(bf16[1024,512]{1,0:T(8,128)(2,1)S(1)} %dynamic-slice_bitcast_fusion), channel_id=1, source_target_pairs={{0,1},{1,0},{2,3},{3,2},{4,5},{5,4},{6,7},{7,6},{8,9},{9,8},{10,11... | collective-permute-start | bytes 3145736 | tf_op jit(solution)/shard_map/ppermute | solution.py:303
  72.0 25.6 %collective-permute-start.11 = (bf16[1024,512]{1,0:T(8,128)(2,1)S(1)}, bf16[1024,512]{1,0:T(8,128)(2,1)S(1)}, u32[]{:S(2)}, u32[]{:S(2)}) collective-permute-start(bf16[1024,512]{1,0:T(8,128)(2,1)S(1)} %collective-permute-done.6.refs_4_.refs_8_), channel_id=1, source_target_pairs={{0,16},{16,0},{1,17},{17,1},{2,18},{18,2},{3,19},{19,3},{4,20},{20... | collective-permute-start | bytes 3145736 | tf_op jit(solution)/shard_map/ppermute | solution.py:306
  98.7 27.0 %collective-permute-start.14 = (bf16[1024,512]{1,0:T(8,128)(2,1)S(1)}, bf16[1024,512]{1,0:T(8,128)(2,1)S(1)}, u32[]{:S(2)}, u32[]{:S(2)}) collective-permute-start(bf16[1024,512]{1,0:T(8,128)(2,1)S(1)} %collective-permute-done.10.refs_9_), channel_id=1, source_target_pairs={{0,16},{16,0},{1,17},{17,1},{2,18},{18,2},{3,19},{19,3},{4,20},{20... | collective-permute-start | bytes 3145736 | tf_op jit(solution)/shard_map/ppermute | solution.py:306
  100.3 15.0 %collective-permute-start.15 = (bf16[512,512]{1,0:T(8,128)(2,1)}, bf16[512,512]{1,0:T(8,128)(2,1)S(1)}, u32[]{:S(2)}, u32[]{:S(2)}) collective-permute-start(bf16[512,512]{1,0:T(8,128)(2,1)} %pad_maximum_fusion.5), channel_id=1, source_target_pairs={{0,1},{1,0},{2,3},{3,2},{4,5},{5,4},{6,7},{7,6},{8,9},{9,8},{10,11... | collective-permute-start | bytes 1572872 | tf_op jit(solution)/shard_map/ppermute | solution.py:303
  101.0 24.7 %collective-permute-start.16 = (bf16[512,512]{1,0:T(8,128)(2,1)}, bf16[512,512]{1,0:T(8,128)(2,1)S(1)}, u32[]{:S(2)}, u32[]{:S(2)}) collective-permute-start(bf16[512,512]{1,0:T(8,128)(2,1)} %dynamic-slice_bitcast_fusion.4), channel_id=1, source_target_pairs={{0,1},{1,0},{2,3},{3,2},{4,5},{5,4},{6,7},{7,6},{8,9},{9,8},{10,11... | collective-permute-start | bytes 1572872 | tf_op jit(solution)/shard_map/ppermute | solution.py:303
  125.7 16.0 %collective-permute-start.18 = (bf16[512,640]{1,0:T(8,128)(2,1)S(1)}, bf16[512,640]{1,0:T(8,128)(2,1)S(1)}, u32[]{:S(2)}, u32[]{:S(2)}) collective-permute-start(bf16[512,640]{1,0:T(8,128)(2,1)S(1)} %copy-done.20), channel_id=1, source_target_pairs={{0,1},{1,0},{2,3},{3,2},{4,5},{5,4},{6,7},{7,6},{8,9},{9,8},{10,11... | collective-permute-start | bytes 1966088 | tf_op jit(solution)/shard_map/ppermute | solution.py:303
  145.4 18.9 %collective-permute-start.20 = (bf16[512,640]{1,0:T(8,128)(2,1)S(1)}, bf16[512,640]{1,0:T(8,128)(2,1)S(1)}, u32[]{:S(2)}, u32[]{:S(2)}) collective-permute-start(bf16[512,640]{1,0:T(8,128)(2,1)S(1)} %collective-permute-done.18.refs_6_), channel_id=1, source_target_pairs={{0,16},{16,0},{1,17},{17,1},{2,18},{18,2},{3,19},{19,3},{4,20},{20... | collective-permute-start | bytes 1966088 | tf_op jit(solution)/shard_map/ppermute | solution.py:306
  146.0 16.8 %collective-permute-start.21 = (bf16[512,640]{1,0:T(8,128)(2,1)S(1)}, bf16[512,640]{1,0:T(8,128)(2,1)S(1)}, u32[]{:S(2)}, u32[]{:S(2)}) collective-permute-start(bf16[512,640]{1,0:T(8,128)(2,1)S(1)} %copy-done.19), channel_id=1, source_target_pairs={{0,1},{1,0},{2,3},{3,2},{4,5},{5,4},{6,7},{7,6},{8,9},{9,8},{10,11... | collective-permute-start | bytes 1966088 | tf_op jit(solution)/shard_map/ppermute | solution.py:303
  149.6 14.7 %collective-permute-start.22 = (bf16[256,1024]{1,0:T(8,128)(2,1)S(1)}, bf16[256,1024]{1,0:T(8,128)(2,1)S(1)}, u32[]{:S(2)}, u32[]{:S(2)}) collective-permute-start(bf16[256,1024]{1,0:T(8,128)(2,1)S(1)} %get-tuple-element.102), channel_id=1, source_target_pairs={{0,2},{14,12},{1,3},{15,13},{16,18},{30,28},{17,19},{31,29}} | collective-permute-start | bytes 1572872 | tf_op jit(solution)/shard_map/ppermute | solution.py:379
  162.8 16.0 %collective-permute-start.26 = (bf16[512,640]{1,0:T(8,128)(2,1)S(1)}, bf16[512,640]{1,0:T(8,128)(2,1)S(1)}, u32[]{:S(2)}, u32[]{:S(2)}) collective-permute-start(bf16[512,640]{1,0:T(8,128)(2,1)S(1)} %collective-permute-done.21.refs_6_), channel_id=1, source_target_pairs={{0,16},{16,0},{1,17},{17,1},{2,18},{18,2},{3,19},{19,3},{4,20},{20... | collective-permute-start | bytes 1966088 | tf_op jit(solution)/shard_map/ppermute | solution.py:306
  164.5 14.3 %collective-permute-start.23 = (bf16[256,1024]{1,0:T(8,128)(2,1)S(1)}, bf16[256,1024]{1,0:T(8,128)(2,1)S(1)}, u32[]{:S(2)}, u32[]{:S(2)}) collective-permute-start(bf16[256,1024]{1,0:T(8,128)(2,1)S(1)} %add_convert_fusion.8), channel_id=1, source_target_pairs={{0,2},{2,4},{12,10},{14,12},{1,3},{3,5},{13,11},{15,13},{16,18},{1... | collective-permute-start | bytes 1572872 | tf_op jit(solution)/shard_map/ppermute | solution.py:379
  179.1 14.0 %collective-permute-start.24 = (bf16[256,1024]{1,0:T(8,128)(2,1)S(1)}, bf16[256,1024]{1,0:T(8,128)(2,1)S(1)}, u32[]{:S(2)}, u32[]{:S(2)}) collective-permute-start(bf16[256,1024]{1,0:T(8,128)(2,1)S(1)} %add_convert_fusion.7), channel_id=1, source_target_pairs={{0,2},{2,4},{4,6},{10,8},{12,10},{14,12},{1,3},{3,5},{5,7},{11,9},... | collective-permute-start | bytes 1572872 | tf_op jit(solution)/shard_map/ppermute | solution.py:379
  198.3 14.5 %collective-permute-start.33 = (bf16[256,1280]{1,0:T(8,128)(2,1)S(1)}, bf16[256,1280]{1,0:T(8,128)(2,1)S(1)}, u32[]{:S(2)}, u32[]{:S(2)}) collective-permute-start(bf16[256,1280]{1,0:T(8,128)(2,1)S(1)} %slice.87), channel_id=1, source_target_pairs={{0,2},{14,12},{1,3},{15,13},{16,18},{30,28},{17,19},{31,29}} | collective-permute-start | bytes 1966088 | tf_op jit(solution)/shard_map/ppermute | solution.py:379
  205.9 13.9 %collective-permute-start.29 = (bf16[256,1280]{1,0:T(8,128)(2,1)S(1)}, bf16[256,1280]{1,0:T(8,128)(2,1)S(1)}, u32[]{:S(2)}, u32[]{:S(2)}) collective-permute-start(bf16[256,1280]{1,0:T(8,128)(2,1)S(1)} %add_convert_fusion.6), channel_id=1, source_target_pairs={{0,2},{2,4},{12,10},{14,12},{1,3},{3,5},{13,11},{15,13},{16,18},{1... | collective-permute-start | bytes 1966088 | tf_op jit(solution)/shard_map/ppermute | solution.py:379
  210.4 14.1 %collective-permute-start.25 = (bf16[128,1024]{1,0:T(8,128)(2,1)S(1)}, bf16[128,1024]{1,0:T(8,128)(2,1)S(1)}, u32[]{:S(2)}, u32[]{:S(2)}) collective-permute-start(bf16[128,1024]{1,0:T(8,128)(2,1)S(1)} %select_convert_fusion.2), channel_id=1, source_target_pairs={{0,8},{8,0},{1,9},{9,1},{2,10},{10,2},{3,11},{11,3},{4,12},{12,4},... | collective-permute-start | bytes 786440 | tf_op jit(solution)/shard_map/ppermute | solution.py:292
  213.0 13.9 %collective-permute-start.34 = (bf16[256,1280]{1,0:T(8,128)(2,1)S(1)}, bf16[256,1280]{1,0:T(8,128)(2,1)S(1)}, u32[]{:S(2)}, u32[]{:S(2)}) collective-permute-start(bf16[256,1280]{1,0:T(8,128)(2,1)S(1)} %add_convert_fusion.4), channel_id=1, source_target_pairs={{0,2},{2,4},{12,10},{14,12},{1,3},{3,5},{13,11},{15,13},{16,18},{1... | collective-permute-start | bytes 1966088 | tf_op jit(solution)/shard_map/ppermute | solution.py:379
  (34 other events, 326.1 us)

commit v7 on v6

--- a/solution.py
+++ b/solution.py
@@ -366,7 +366,7 @@
             (rest, -1, up_c, 0, u2), (half_depth + rest, -1, up_c, 1, u2),
         ],
     )
-    down_ax, down_b, crossed, piece = together((down_ax, down_b, crossed, pieces[3]))
+    down_ax, crossed, piece = together((down_ax, crossed, pieces[3]))
 
     def expert(first, near, far, *earlier):
         return down_call(
@@ -391,7 +391,7 @@
 
     down_bx, down_c = relay(down_b), swap(piece)
     home_a, away_a = expert(0, down_a, down_ax)
-    a1, a2, a3 = thirds(away_a, across(away_a))
+    a1, a2, a3 = thirds(away_a, across(after(away_a, down_b)))
     moving_a = step(a3, None, 3)
     home_b, away_b = expert(2 * d0, down_b, down_bx, moving_a, down_c)
     down_cx = relay(down_c)

time: 245 us -> 242 us (0.988)
    ppermute x8, waiting for transfers between devices: 49.8 us -> 47.3 us  [swap(): return lax.ppermute(x, 'local', swap_half)]
  transfers between devices with their start and end apart: 37 -> 37, of which waited for: 23 -> 23; matrix products, arithmetic and copies ran while one was open for 10% -> 10% of each run, Pallas kernels for 11% -> 13%
where the time goes in v7:
time: 242 us; the launch traced here: 241 us
  waiting for transfers between devices  95.1 us (39%)
  starting transfers between devices  76.1 us (31%)
  Pallas kernels  31.6 us (13%)
  local copies, waits for them, and re-layouts  21.3 us (9%)
  other arithmetic  16.4 us (7%)
    ppermute x9, starting transfers between devices, step(): return lax.ppermute(rows, both, back_pairs(k))  47.9 us
    ppermute x8, waiting for transfers between devices, swap(): return lax.ppermute(x, 'local', swap_half)  47.3 us
    ppermute x7, waiting for transfers between devices, relay(): return lax.ppermute(x, 'parts', swap_two)  23.2 us
    ppermute x9, waiting for transfers between devices, step(): return lax.ppermute(rows, both, back_pairs(k))  21.2 us
    pallas_call x3, Pallas kernels, hidden_call(): pl.pallas_call(functools.partial(hidden_kernel, batches, gate_pieces, up_...  18.4 us
    pallas_call x3, Pallas kernels, down_call(): pl.pallas_call(functools.partial(down_kernel, batches, first, width), gri...  13.3 us
    ppermute x8, starting transfers between devices, swap(): return lax.ppermute(x, 'local', swap_half)  10.6 us
    dynamic_slice x6, local copies, waits for them, and re-layouts, cut(): return lax.dynamic_slice_in_dim(array, begin, length, dim)  10.1 us
  transfers between devices with their start and end apart: 37, of which 23 were waited for; matrix products, arithmetic and copies ran while one was open for 10% of the time, Pallas kernels for 13%

profile of v7, /device:TPU:0, one launch (start us, length us, event | category | flops | bytes accessed | tf_op | source)
XLA Modules:
  0.0 241.2 jit_solution(11812954725702020558)
XLA Ops:
  11.9 9.8 %collective-permute-done.3.refs_2_ = bf16[512,512]{1,0:T(8,128)(2,1)S(1)} collective-permute-done((bf16[512,512]{1,0:T(8,128)(2,1)S(1)}, bf16[512,512]{1,0:T(8,128)(2,1)S(1)}, u32[]{:S(2)}, u32[]{:S(2)}) %collective-permute-start.3) | collective-permute-done | bytes 524320 | tf_op jit(solution)/shard_map/ppermute | solution.py:303
  26.2 6.0 %collective-permute-done.4.refs_5_ = bf16[512,512]{1,0:T(8,128)(2,1)S(1)} collective-permute-done((bf16[512,512]{1,0:T(8,128)(2,1)S(1)}, bf16[512,512]{1,0:T(8,128)(2,1)S(1)}, u32[]{:S(2)}, u32[]{:S(2)}) %collective-permute-start.4) | collective-permute-done | bytes 524320 | tf_op jit(solution)/shard_map/ppermute | solution.py:306
  33.1 5.4 %collective-permute-done.2.refs_3_ = bf16[768,512]{1,0:T(8,128)(2,1)S(1)} collective-permute-done((bf16[768,512]{1,0:T(8,128)(2,1)S(1)}, bf16[768,512]{1,0:T(8,128)(2,1)S(1)}, u32[]{:S(2)}, u32[]{:S(2)}) %collective-permute-start.2) | collective-permute-done | bytes 786464 | tf_op jit(solution)/shard_map/ppermute | solution.py:303
  54.4 10.0 %collective-permute-done.7.refs_6_ = bf16[768,512]{1,0:T(8,128)(2,1)S(1)} collective-permute-done((bf16[768,512]{1,0:T(8,128)(2,1)S(1)}, bf16[768,512]{1,0:T(8,128)(2,1)S(1)}, u32[]{:S(2)}, u32[]{:S(2)}) %collective-permute-start.7) | collective-permute-done | bytes 786464 | tf_op jit(solution)/shard_map/ppermute | solution.py:306
  79.8 4.7 %shard_map.64.refs_2_ = bf16[512,512]{1,0:T(8,128)(2,1)S(1)} custom-call(s32[4]{0:T(128)S(1)} %pad_add_fusion.where_ref, bf16[512,3712]{1,0:T(8,128)(2,1)S(1)} %pad_maximum_fusion.refs_0_, bf16[3584,512]{1,0:T(8,128)(2,1)S(1)} %bitcast.32, bf16[3584,512]{1,0:T(8,128)(2,1)S(1)} %bitcast.30), custom_call_target="tpu_custom_call" | custom-call | flops 3758096384 | bytes 11665408 | tf_op jit(solution)/shard_map/pallas_call | solution.py:175
  84.5 11.7 %collective-permute-done.10.refs_9_ = bf16[1024,512]{1,0:T(8,128)(2,1)S(1)} collective-permute-done((bf16[1024,512]{1,0:T(8,128)(2,1)S(1)}, bf16[1024,512]{1,0:T(8,128)(2,1)S(1)}, u32[]{:S(2)}, u32[]{:S(2)}) %collective-permute-start.10) | collective-permute-done | bytes 1048608 | tf_op jit(solution)/shard_map/ppermute | solution.py:303
  109.7 4.7 %shard_map.65.refs_3_ = bf16[512,512]{1,0:T(8,128)(2,1)S(1)} custom-call(s32[4]{0:T(128)S(1)} %pad_add_fusion.where_ref, bf16[512,3712]{1,0:T(8,128)(2,1)S(1)} %pad_maximum_fusion.1.refs_0_.refs_1_, bf16[3584,512]{1,0:T(8,128)(2,1)S(1)} %bitcast.33, bf16[3584,512]{1,0:T(8,128)(2,1)S(1)} %bitcast.31), custom_call_target="tpu_custom_call" | custom-call | flops 3758096384 | bytes 11665408 | tf_op jit(solution)/shard_map/pallas_call | solution.py:175
  115.2 10.5 %collective-permute-done.16.refs_6_ = bf16[512,512]{1,0:T(8,128)(2,1)S(1)} collective-permute-done((bf16[512,512]{1,0:T(8,128)(2,1)}, bf16[512,512]{1,0:T(8,128)(2,1)S(1)}, u32[]{:S(2)}, u32[]{:S(2)}) %collective-permute-start.16) | collective-permute-done | bytes 524320 | tf_op jit(solution)/shard_map/ppermute | solution.py:303
  127.0 9.0 %shard_map.66.refs_4_ = bf16[1024,512]{1,0:T(8,128)(2,1)S(1)} custom-call(s32[4]{0:T(128)S(1)} %pad_add_fusion.where_ref, bf16[512,3712]{1,0:T(8,128)(2,1)S(1)} %copy-done.1, bf16[512,3712]{1,0:T(8,128)(2,1)S(1)} %pad_maximum_fusion.1.refs_0_.refs_1_, bf16[512,512]{1,0:T(8,128)(2,1)S(1)} %copy-done.12, bf16[768,512]{1,0:T(8,128)(2,1)S(1)} %collective-permute-done.2.refs_3_, ...), custom_call_target="tpu_custom_call" | custom-call | flops 7516192768 | bytes 15990784 | tf_op jit(solution)/shard_map/pallas_call | solution.py:175
  138.9 3.7 %shard_map.67 = (bf16[256,1024]{1,0:T(8,128)(2,1)S(1)}, bf16[768,1024]{1,0:T(8,128)(2,1)S(1)}) custom-call(s32[4]{0:T(128)S(1)} %pad_add_fusion.where_ref, bf16[512,3712]{1,0:T(8,128)(2,1)S(1)} %copy-done.1, bf16[512,3712]{1,0:T(8,128)(2,1)S(1)} %pad_maximum_fusion.1.refs_0_.refs_1_, bf16[512,512]{1,0:T(8,128)(2,1)S(1)} %shard_map.64.refs_2_, ...), custom_call_target="tpu_custom_call" | custom-call | flops 2147483648 | bytes 6291456 | tf_op jit(solution)/shard_map/pallas_call | solution.py:232
  146.8 7.4 %collective-permute-start.22 = (bf16[256,1024]{1,0:T(8,128)(2,1)S(1)}, bf16[256,1024]{1,0:T(8,128)(2,1)S(1)}, u32[]{:S(2)}, u32[]{:S(2)}) collective-permute-start(bf16[256,1024]{1,0:T(8,128)(2,1)S(1)} %get-tuple-element.102), channel_id=1, source_target_pairs={{0,2},{14,12},{1,3},{15,13},{16,18},{30,28},{17,19},{31,29}} | collective-permute-start | bytes 1572872 | tf_op jit(solution)/shard_map/ppermute | solution.py:379
  154.2 5.6 %collective-permute-done.21.refs_6_ = bf16[512,640]{1,0:T(8,128)(2,1)S(1)} collective-permute-done((bf16[512,640]{1,0:T(8,128)(2,1)S(1)}, bf16[512,640]{1,0:T(8,128)(2,1)S(1)}, u32[]{:S(2)}, u32[]{:S(2)}) %collective-permute-start.21) | collective-permute-done | bytes 655392 | tf_op jit(solution)/shard_map/ppermute | solution.py:303
  161.0 7.3 %collective-permute-start.23 = (bf16[256,1024]{1,0:T(8,128)(2,1)S(1)}, bf16[256,1024]{1,0:T(8,128)(2,1)S(1)}, u32[]{:S(2)}, u32[]{:S(2)}) collective-permute-start(bf16[256,1024]{1,0:T(8,128)(2,1)S(1)} %add_convert_fusion.8), channel_id=1, source_target_pairs={{0,2},{2,4},{12,10},{14,12},{1,3},{3,5},{13,11},{15,13},{16,18},{1... | collective-permute-start | bytes 1572872 | tf_op jit(solution)/shard_map/ppermute | solution.py:379
  168.4 4.8 %shard_map.68 = (bf16[256,1280]{1,0:T(8,128)(2,1)S(1)}, bf16[768,1280]{1,0:T(8,128)(2,1)S(1)}) custom-call(s32[4]{0:T(128)S(1)} %pad_add_fusion.where_ref, bf16[512,3712]{1,0:T(8,128)(2,1)S(1)} %copy-done.1, bf16[512,3712]{1,0:T(8,128)(2,1)S(1)} %pad_maximum_fusion.1.refs_0_.refs_1_, bf16[512,512]{1,0:T(8,128)(2,1)S(1)} %shard_map.64.refs_2_, ...), custom_call_target="tpu_custom_call" | custom-call | flops 2684354560 | bytes 7340032 | tf_op jit(solution)/shard_map/pallas_call | solution.py:232
  176.4 7.4 %collective-permute-start.24 = (bf16[256,1024]{1,0:T(8,128)(2,1)S(1)}, bf16[256,1024]{1,0:T(8,128)(2,1)S(1)}, u32[]{:S(2)}, u32[]{:S(2)}) collective-permute-start(bf16[256,1024]{1,0:T(8,128)(2,1)S(1)} %add_convert_fusion.7), channel_id=1, source_target_pairs={{0,2},{2,4},{4,6},{10,8},{12,10},{14,12},{1,3},{3,5},{5,7},{11,9},... | collective-permute-start | bytes 1572872 | tf_op jit(solution)/shard_map/ppermute | solution.py:379
  184.3 4.8 %shard_map.69 = (bf16[256,1280]{1,0:T(8,128)(2,1)S(1)}, bf16[768,1280]{1,0:T(8,128)(2,1)S(1)}) custom-call(s32[4]{0:T(128)S(1)} %pad_add_fusion.where_ref, bf16[512,3712]{1,0:T(8,128)(2,1)S(1)} %copy-done.1, bf16[512,3712]{1,0:T(8,128)(2,1)S(1)} %pad_maximum_fusion.1.refs_0_.refs_1_, bf16[512,512]{1,0:T(8,128)(2,1)S(1)} %shard_map.64.refs_2_, ...), custom_call_target="tpu_custom_call" | custom-call | flops 2684354560 | bytes 7340032 | tf_op jit(solution)/shard_map/pallas_call | solution.py:232
  190.7 4.3 %collective-permute-start.28 = (bf16[256,1280]{1,0:T(8,128)(2,1)S(1)}, bf16[256,1280]{1,0:T(8,128)(2,1)S(1)}, u32[]{:S(2)}, u32[]{:S(2)}) collective-permute-start(bf16[256,1280]{1,0:T(8,128)(2,1)S(1)} %slice.82), channel_id=1, source_target_pairs={{0,2},{14,12},{1,3},{15,13},{16,18},{30,28},{17,19},{31,29}} | collective-permute-start | bytes 1966088 | tf_op jit(solution)/shard_map/ppermute | solution.py:379
  195.6 3.8 %collective-permute-start.33 = (bf16[256,1280]{1,0:T(8,128)(2,1)S(1)}, bf16[256,1280]{1,0:T(8,128)(2,1)S(1)}, u32[]{:S(2)}, u32[]{:S(2)}) collective-permute-start(bf16[256,1280]{1,0:T(8,128)(2,1)S(1)} %slice.87), channel_id=1, source_target_pairs={{0,2},{14,12},{1,3},{15,13},{16,18},{30,28},{17,19},{31,29}} | collective-permute-start | bytes 1966088 | tf_op jit(solution)/shard_map/ppermute | solution.py:379
  199.3 3.7 %collective-permute-done.28 = bf16[256,1280]{1,0:T(8,128)(2,1)S(1)} collective-permute-done((bf16[256,1280]{1,0:T(8,128)(2,1)S(1)}, bf16[256,1280]{1,0:T(8,128)(2,1)S(1)}, u32[]{:S(2)}, u32[]{:S(2)}) %collective-permute-start.28) | collective-permute-done | bytes 655392 | tf_op jit(solution)/shard_map/ppermute | solution.py:379
  203.2 4.4 %collective-permute-start.29 = (bf16[256,1280]{1,0:T(8,128)(2,1)S(1)}, bf16[256,1280]{1,0:T(8,128)(2,1)S(1)}, u32[]{:S(2)}, u32[]{:S(2)}) collective-permute-start(bf16[256,1280]{1,0:T(8,128)(2,1)S(1)} %add_convert_fusion.6), channel_id=1, source_target_pairs={{0,2},{2,4},{12,10},{14,12},{1,3},{3,5},{13,11},{15,13},{16,18},{1... | collective-permute-start | bytes 1966088 | tf_op jit(solution)/shard_map/ppermute | solution.py:379
  210.2 4.4 %collective-permute-start.34 = (bf16[256,1280]{1,0:T(8,128)(2,1)S(1)}, bf16[256,1280]{1,0:T(8,128)(2,1)S(1)}, u32[]{:S(2)}, u32[]{:S(2)}) collective-permute-start(bf16[256,1280]{1,0:T(8,128)(2,1)S(1)} %add_convert_fusion.4), channel_id=1, source_target_pairs={{0,2},{2,4},{12,10},{14,12},{1,3},{3,5},{13,11},{15,13},{16,18},{1... | collective-permute-start | bytes 1966088 | tf_op jit(solution)/shard_map/ppermute | solution.py:379
  217.4 4.4 %collective-permute-start.30 = (bf16[256,1280]{1,0:T(8,128)(2,1)S(1)}, bf16[256,1280]{1,0:T(8,128)(2,1)S(1)}, u32[]{:S(2)}, u32[]{:S(2)}) collective-permute-start(bf16[256,1280]{1,0:T(8,128)(2,1)S(1)} %add_convert_fusion.5), channel_id=1, source_target_pairs={{0,2},{2,4},{4,6},{10,8},{12,10},{14,12},{1,3},{3,5},{5,7},{11,9},... | collective-permute-start | bytes 1966088 | tf_op jit(solution)/shard_map/ppermute | solution.py:379
  224.3 4.4 %collective-permute-start.35 = (bf16[256,1280]{1,0:T(8,128)(2,1)S(1)}, bf16[256,1280]{1,0:T(8,128)(2,1)S(1)}, u32[]{:S(2)}, u32[]{:S(2)}) collective-permute-start(bf16[256,1280]{1,0:T(8,128)(2,1)S(1)} %add_convert_fusion.3), channel_id=1, source_target_pairs={{0,2},{2,4},{4,6},{10,8},{12,10},{14,12},{1,3},{3,5},{5,7},{11,9},... | collective-permute-start | bytes 1966088 | tf_op jit(solution)/shard_map/ppermute | solution.py:379
  231.4 6.7 %collective-permute-done.35 = bf16[256,1280]{1,0:T(8,128)(2,1)S(1)} collective-permute-done((bf16[256,1280]{1,0:T(8,128)(2,1)S(1)}, bf16[256,1280]{1,0:T(8,128)(2,1)S(1)}, u32[]{:S(2)}, u32[]{:S(2)}) %collective-permute-start.35) | collective-permute-done | bytes 655392 | tf_op jit(solution)/shard_map/ppermute | solution.py:379
  (141 shorter events, 91.6 us)
Async XLA Ops:
  6.0 32.5 %collective-permute-start.1 = (bf16[256,3712]{1,0:T(8,128)(2,1)S(1)}, bf16[256,3712]{1,0:T(8,128)(2,1)}, u32[]{:S(2)}, u32[]{:S(2)}) collective-permute-start(bf16[256,3712]{1,0:T(8,128)(2,1)S(1)} %pad_maximum_fusion.2), channel_id=1, source_target_pairs={{2,0},{4,2},{6,4},{8,10},{10,12},{12,14},{3,1},{5,3},{7,5},{9,11},... | collective-permute-start | bytes 5701640 | tf_op jit(solution)/shard_map/ppermute | solution.py:309
  11.8 26.7 %collective-permute-start.2 = (bf16[768,512]{1,0:T(8,128)(2,1)S(1)}, bf16[768,512]{1,0:T(8,128)(2,1)S(1)}, u32[]{:S(2)}, u32[]{:S(2)}) collective-permute-start(bf16[768,512]{1,0:T(8,128)(2,1)S(1)} %copy-done.18), channel_id=1, source_target_pairs={{0,1},{1,0},{2,3},{3,2},{4,5},{5,4},{6,7},{7,6},{8,9},{9,8},{10,11... | collective-permute-start | bytes 2359304 | tf_op jit(solution)/shard_map/ppermute | solution.py:303
  38.5 30.2 %collective-permute-start.5 = (bf16[256,3712]{1,0:T(8,128)(2,1)}, bf16[256,3712]{1,0:T(8,128)(2,1)}, u32[]{:S(2)}, u32[]{:S(2)}) collective-permute-start(bf16[256,3712]{1,0:T(8,128)(2,1)} %collective-permute-done.1), channel_id=1, source_target_pairs={{2,0},{4,2},{10,12},{12,14},{3,1},{5,3},{11,13},{13,15},{18,16},{2... | collective-permute-start | bytes 5701640 | tf_op jit(solution)/shard_map/ppermute | solution.py:309
  39.8 28.9 %collective-permute-start.8 = (bf16[256,3712]{1,0:T(8,128)(2,1)}, bf16[256,3712]{1,0:T(8,128)(2,1)}, u32[]{:S(2)}, u32[]{:S(2)}) collective-permute-start(bf16[256,3712]{1,0:T(8,128)(2,1)} %collective-permute-done.1), channel_id=1, source_target_pairs={{0,8},{8,0},{1,9},{9,1},{2,10},{10,2},{3,11},{11,3},{4,12},{12,4},... | collective-permute-start | bytes 5701640 | tf_op jit(solution)/shard_map/ppermute | solution.py:292
  43.2 25.6 %collective-permute-start.6 = (bf16[1024,512]{1,0:T(8,128)(2,1)}, bf16[1024,512]{1,0:T(8,128)(2,1)S(1)}, u32[]{:S(2)}, u32[]{:S(2)}) collective-permute-start(bf16[1024,512]{1,0:T(8,128)(2,1)} %pad_maximum_fusion.3), channel_id=1, source_target_pairs={{0,1},{1,0},{2,3},{3,2},{4,5},{5,4},{6,7},{7,6},{8,9},{9,8},{10,11... | collective-permute-start | bytes 3145736 | tf_op jit(solution)/shard_map/ppermute | solution.py:303
  45.2 19.2 %collective-permute-start.7 = (bf16[768,512]{1,0:T(8,128)(2,1)S(1)}, bf16[768,512]{1,0:T(8,128)(2,1)S(1)}, u32[]{:S(2)}, u32[]{:S(2)}) collective-permute-start(bf16[768,512]{1,0:T(8,128)(2,1)S(1)} %collective-permute-done.2.refs_3_), channel_id=1, source_target_pairs={{0,16},{16,0},{1,17},{17,1},{2,18},{18,2},{3,19},{19,3},{4,20},{20... | collective-permute-start | bytes 2359304 | tf_op jit(solution)/shard_map/ppermute | solution.py:306
  68.8 29.9 %collective-permute-start.12 = (bf16[256,3712]{1,0:T(8,128)(2,1)}, bf16[256,3712]{1,0:T(8,128)(2,1)}, u32[]{:S(2)}, u32[]{:S(2)}) collective-permute-start(bf16[256,3712]{1,0:T(8,128)(2,1)} %collective-permute-done.5), channel_id=1, source_target_pairs={{0,8},{8,0},{1,9},{9,1},{2,10},{10,2},{3,11},{11,3},{4,12},{12,4},... | collective-permute-start | bytes 5701640 | tf_op jit(solution)/shard_map/ppermute | solution.py:292
  68.8 29.9 %collective-permute-start.9 = (bf16[256,3712]{1,0:T(8,128)(2,1)}, bf16[256,3712]{1,0:T(8,128)(2,1)}, u32[]{:S(2)}, u32[]{:S(2)}) collective-permute-start(bf16[256,3712]{1,0:T(8,128)(2,1)} %collective-permute-done.5), channel_id=1, source_target_pairs={{2,0},{12,14},{3,1},{13,15},{18,16},{28,30},{19,17},{29,31}} | collective-permute-start | bytes 5701640 | tf_op jit(solution)/shard_map/ppermute | solution.py:309
  70.2 26.0 %collective-permute-start.10 = (bf16[1024,512]{1,0:T(8,128)(2,1)S(1)}, bf16[1024,512]{1,0:T(8,128)(2,1)S(1)}, u32[]{:S(2)}, u32[]{:S(2)}) collective-permute-start(bf16[1024,512]{1,0:T(8,128)(2,1)S(1)} %dynamic-slice_bitcast_fusion), channel_id=1, source_target_pairs={{0,1},{1,0},{2,3},{3,2},{4,5},{5,4},{6,7},{7,6},{8,9},{9,8},{10,11... | collective-permute-start | bytes 3145736 | tf_op jit(solution)/shard_map/ppermute | solution.py:303
  72.0 25.6 %collective-permute-start.11 = (bf16[1024,512]{1,0:T(8,128)(2,1)S(1)}, bf16[1024,512]{1,0:T(8,128)(2,1)S(1)}, u32[]{:S(2)}, u32[]{:S(2)}) collective-permute-start(bf16[1024,512]{1,0:T(8,128)(2,1)S(1)} %collective-permute-done.6.refs_4_.refs_8_), channel_id=1, source_target_pairs={{0,16},{16,0},{1,17},{17,1},{2,18},{18,2},{3,19},{19,3},{4,20},{20... | collective-permute-start | bytes 3145736 | tf_op jit(solution)/shard_map/ppermute | solution.py:306
  98.7 27.0 %collective-permute-start.14 = (bf16[1024,512]{1,0:T(8,128)(2,1)S(1)}, bf16[1024,512]{1,0:T(8,128)(2,1)S(1)}, u32[]{:S(2)}, u32[]{:S(2)}) collective-permute-start(bf16[1024,512]{1,0:T(8,128)(2,1)S(1)} %collective-permute-done.10.refs_9_), channel_id=1, source_target_pairs={{0,16},{16,0},{1,17},{17,1},{2,18},{18,2},{3,19},{19,3},{4,20},{20... | collective-permute-start | bytes 3145736 | tf_op jit(solution)/shard_map/ppermute | solution.py:306
  100.3 15.0 %collective-permute-start.15 = (bf16[512,512]{1,0:T(8,128)(2,1)}, bf16[512,512]{1,0:T(8,128)(2,1)S(1)}, u32[]{:S(2)}, u32[]{:S(2)}) collective-permute-start(bf16[512,512]{1,0:T(8,128)(2,1)} %pad_maximum_fusion.5), channel_id=1, source_target_pairs={{0,1},{1,0},{2,3},{3,2},{4,5},{5,4},{6,7},{7,6},{8,9},{9,8},{10,11... | collective-permute-start | bytes 1572872 | tf_op jit(solution)/shard_map/ppermute | solution.py:303
  101.0 24.7 %collective-permute-start.16 = (bf16[512,512]{1,0:T(8,128)(2,1)}, bf16[512,512]{1,0:T(8,128)(2,1)S(1)}, u32[]{:S(2)}, u32[]{:S(2)}) collective-permute-start(bf16[512,512]{1,0:T(8,128)(2,1)} %dynamic-slice_bitcast_fusion.4), channel_id=1, source_target_pairs={{0,1},{1,0},{2,3},{3,2},{4,5},{5,4},{6,7},{7,6},{8,9},{9,8},{10,11... | collective-permute-start | bytes 1572872 | tf_op jit(solution)/shard_map/ppermute | solution.py:303
  126.2 16.3 %collective-permute-start.18 = (bf16[512,640]{1,0:T(8,128)(2,1)S(1)}, bf16[512,640]{1,0:T(8,128)(2,1)S(1)}, u32[]{:S(2)}, u32[]{:S(2)}) collective-permute-start(bf16[512,640]{1,0:T(8,128)(2,1)S(1)} %copy-done.20), channel_id=1, source_target_pairs={{0,1},{1,0},{2,3},{3,2},{4,5},{5,4},{6,7},{7,6},{8,9},{9,8},{10,11... | collective-permute-start | bytes 1966088 | tf_op jit(solution)/shard_map/ppermute | solution.py:303
  142.6 17.1 %collective-permute-start.21 = (bf16[512,640]{1,0:T(8,128)(2,1)S(1)}, bf16[512,640]{1,0:T(8,128)(2,1)S(1)}, u32[]{:S(2)}, u32[]{:S(2)}) collective-permute-start(bf16[512,640]{1,0:T(8,128)(2,1)S(1)} %copy-done.19), channel_id=1, source_target_pairs={{0,1},{1,0},{2,3},{3,2},{4,5},{5,4},{6,7},{7,6},{8,9},{9,8},{10,11... | collective-permute-start | bytes 1966088 | tf_op jit(solution)/shard_map/ppermute | solution.py:303
  143.5 17.0 %collective-permute-start.20 = (bf16[512,640]{1,0:T(8,128)(2,1)S(1)}, bf16[512,640]{1,0:T(8,128)(2,1)S(1)}, u32[]{:S(2)}, u32[]{:S(2)}) collective-permute-start(bf16[512,640]{1,0:T(8,128)(2,1)S(1)} %collective-permute-done.18.refs_6_), channel_id=1, source_target_pairs={{0,16},{16,0},{1,17},{17,1},{2,18},{18,2},{3,19},{19,3},{4,20},{20... | collective-permute-start | bytes 1966088 | tf_op jit(solution)/shard_map/ppermute | solution.py:306
  146.8 14.0 %collective-permute-start.22 = (bf16[256,1024]{1,0:T(8,128)(2,1)S(1)}, bf16[256,1024]{1,0:T(8,128)(2,1)S(1)}, u32[]{:S(2)}, u32[]{:S(2)}) collective-permute-start(bf16[256,1024]{1,0:T(8,128)(2,1)S(1)} %get-tuple-element.102), channel_id=1, source_target_pairs={{0,2},{14,12},{1,3},{15,13},{16,18},{30,28},{17,19},{31,29}} | collective-permute-start | bytes 1572872 | tf_op jit(solution)/shard_map/ppermute | solution.py:379
  159.8 16.3 %collective-permute-start.26 = (bf16[512,640]{1,0:T(8,128)(2,1)S(1)}, bf16[512,640]{1,0:T(8,128)(2,1)S(1)}, u32[]{:S(2)}, u32[]{:S(2)}) collective-permute-start(bf16[512,640]{1,0:T(8,128)(2,1)S(1)} %collective-permute-done.21.refs_6_), channel_id=1, source_target_pairs={{0,16},{16,0},{1,17},{17,1},{2,18},{18,2},{3,19},{19,3},{4,20},{20... | collective-permute-start | bytes 1966088 | tf_op jit(solution)/shard_map/ppermute | solution.py:306
  161.0 15.0 %collective-permute-start.23 = (bf16[256,1024]{1,0:T(8,128)(2,1)S(1)}, bf16[256,1024]{1,0:T(8,128)(2,1)S(1)}, u32[]{:S(2)}, u32[]{:S(2)}) collective-permute-start(bf16[256,1024]{1,0:T(8,128)(2,1)S(1)} %add_convert_fusion.8), channel_id=1, source_target_pairs={{0,2},{2,4},{12,10},{14,12},{1,3},{3,5},{13,11},{15,13},{16,18},{1... | collective-permute-start | bytes 1572872 | tf_op jit(solution)/shard_map/ppermute | solution.py:379
  176.4 14.0 %collective-permute-start.24 = (bf16[256,1024]{1,0:T(8,128)(2,1)S(1)}, bf16[256,1024]{1,0:T(8,128)(2,1)S(1)}, u32[]{:S(2)}, u32[]{:S(2)}) collective-permute-start(bf16[256,1024]{1,0:T(8,128)(2,1)S(1)} %add_convert_fusion.7), channel_id=1, source_target_pairs={{0,2},{2,4},{4,6},{10,8},{12,10},{14,12},{1,3},{3,5},{5,7},{11,9},... | collective-permute-start | bytes 1572872 | tf_op jit(solution)/shard_map/ppermute | solution.py:379
  195.6 14.5 %collective-permute-start.33 = (bf16[256,1280]{1,0:T(8,128)(2,1)S(1)}, bf16[256,1280]{1,0:T(8,128)(2,1)S(1)}, u32[]{:S(2)}, u32[]{:S(2)}) collective-permute-start(bf16[256,1280]{1,0:T(8,128)(2,1)S(1)} %slice.87), channel_id=1, source_target_pairs={{0,2},{14,12},{1,3},{15,13},{16,18},{30,28},{17,19},{31,29}} | collective-permute-start | bytes 1966088 | tf_op jit(solution)/shard_map/ppermute | solution.py:379
  203.2 13.9 %collective-permute-start.29 = (bf16[256,1280]{1,0:T(8,128)(2,1)S(1)}, bf16[256,1280]{1,0:T(8,128)(2,1)S(1)}, u32[]{:S(2)}, u32[]{:S(2)}) collective-permute-start(bf16[256,1280]{1,0:T(8,128)(2,1)S(1)} %add_convert_fusion.6), channel_id=1, source_target_pairs={{0,2},{2,4},{12,10},{14,12},{1,3},{3,5},{13,11},{15,13},{16,18},{1... | collective-permute-start | bytes 1966088 | tf_op jit(solution)/shard_map/ppermute | solution.py:379
  207.7 14.1 %collective-permute-start.25 = (bf16[128,1024]{1,0:T(8,128)(2,1)S(1)}, bf16[128,1024]{1,0:T(8,128)(2,1)S(1)}, u32[]{:S(2)}, u32[]{:S(2)}) collective-permute-start(bf16[128,1024]{1,0:T(8,128)(2,1)S(1)} %select_convert_fusion.2), channel_id=1, source_target_pairs={{0,8},{8,0},{1,9},{9,1},{2,10},{10,2},{3,11},{11,3},{4,12},{12,4},... | collective-permute-start | bytes 786440 | tf_op jit(solution)/shard_map/ppermute | solution.py:292
  210.2 13.9 %collective-permute-start.34 = (bf16[256,1280]{1,0:T(8,128)(2,1)S(1)}, bf16[256,1280]{1,0:T(8,128)(2,1)S(1)}, u32[]{:S(2)}, u32[]{:S(2)}) collective-permute-start(bf16[256,1280]{1,0:T(8,128)(2,1)S(1)} %add_convert_fusion.4), channel_id=1, source_target_pairs={{0,2},{2,4},{12,10},{14,12},{1,3},{3,5},{13,11},{15,13},{16,18},{1... | collective-permute-start | bytes 1966088 | tf_op jit(solution)/shard_map/ppermute | solution.py:379
  (34 other events, 323.5 us)
